TPU v7x, 32 devices: a whole 2x2x4 slice. The times are simulated.
32 devices in a mesh: batch: 4 (over z), proto: 8 (over y, x, core).
Axes of the slice: x: 2, y: 2, z: 4, core: 2. Of those that a mesh axis runs over, the one named last changes fastest.
Arguments:
- teacher_feats: bfloat16 [1024, 256], P('batch'), may hold values from -2 to 2
- student_feats: bfloat16 [1024, 256], P('batch'), may hold values from -2 to 2
- teacher_weight: bfloat16 [256, 32768], P(None, 'proto'), may hold values from -2 to 2
- student_weight: bfloat16 [256, 32768], P(None, 'proto'), may hold values from -2 to 2
Outputs:
- weight_grad: bfloat16 [256, 32768], P('batch', 'proto')
- feature_grad: bfloat16 [1024, 256], P('batch')
All inputs are finite; a program needn't handle non-finite values.
Results may differ from a plain program's by a relative error of at most 0.025.
Values may be sent and summed in bfloat16 or wider, within the bound.
No kernel may reach another device: no remote copies, remote signals or barrier semaphores. Data moves between devices by JAX's collectives and lax.ppermute only.
A program may use at most 64 MiB of HBM per device.

v0:
```python
import math

import jax
import jax.numpy as jnp
from jax import lax
from jax.sharding import PartitionSpec as P

ITERS = 3


teacher_temp = 0.07
student_temp = 0.1
epsilon = 1e-06


def unit_rows(raw):
    values = raw.astype(jnp.float32)
    length = jnp.sqrt(jnp.sum(values * values, axis=1, keepdims=True) + epsilon)
    return (values / length, length)


def unit_columns(raw):
    values = raw.astype(jnp.float32)
    length = jnp.sqrt(jnp.sum(values * values, axis=0, keepdims=True) + epsilon)
    return (values / length).astype(jnp.bfloat16)


def proto_update(teacher_exp, crop_scale):
    sums = lax.psum(jnp.sum(teacher_exp * crop_scale[:, None], axis=0), "batch")
    return 1.0 / sums


def through_norm(unit_grad, unit, length):
    along = jnp.sum(unit * unit_grad, axis=1, keepdims=True)
    return ((unit_grad - unit * along) / length).astype(jnp.bfloat16)


def shards(teacher_feats, student_feats, teacher_weight, student_weight):
    teacher_unit, _ = unit_rows(teacher_feats)
    teacher_half = teacher_unit.astype(jnp.bfloat16)
    student_unit, student_len = unit_rows(student_feats)
    student_half = student_unit.astype(jnp.bfloat16)
    teacher_cols = unit_columns(teacher_weight)
    student_cols = unit_columns(student_weight)
    crops_here = teacher_half.shape[0]
    width = teacher_half.shape[1]
    batch_count = lax.axis_size("batch")
    proto_count = lax.axis_size("proto")
    crops_all = crops_here * batch_count
    protos_all = teacher_cols.shape[1] * proto_count
    teacher_exp = jnp.exp(
        jnp.dot(teacher_half, teacher_cols, preferred_element_type=jnp.float32) / teacher_temp
    )
    logits = jnp.dot(student_half, student_cols, preferred_element_type=jnp.float32) / student_temp
    local_totals = jnp.sum(jnp.exp(logits), axis=1)
    crop_scale = jnp.ones((crops_here,), jnp.float32)
    for sweep_index in range(ITERS):
        proto_scale = proto_update(teacher_exp, crop_scale)
        crop_sums = lax.psum(jnp.sum(teacher_exp * proto_scale[None, :], axis=1), "proto")
        crop_scale = 1.0 / crop_sums
    student_totals = lax.psum(local_totals, "proto")
    targets = teacher_exp * proto_scale[None, :] * crop_scale[:, None]
    log_total = jnp.log(student_totals)[:, None]
    student_prob = jnp.exp(logits - log_total)
    grad_logits = (protos_all * (student_prob - targets)).astype(jnp.bfloat16)
    weight_factor = math.sqrt(width / crops_all)
    weight_term_all = (
        lax.dot_general(
            student_half, grad_logits, (((0,), (0,)), ((), ())), preferred_element_type=jnp.float32
        )
        * weight_factor
    )
    weight_part = lax.psum_scatter(
        weight_term_all.astype(jnp.bfloat16), "batch", scatter_dimension=0, tiled=True
    )
    feature_factor = math.sqrt(width / protos_all)
    local_grad = (
        lax.dot_general(
            grad_logits, student_cols, (((1,), (1,)), ((), ())), preferred_element_type=jnp.float32
        )
        * feature_factor
    )
    unit_grad = lax.psum(local_grad.astype(jnp.bfloat16), "proto").astype(jnp.float32)
    feature_grad = through_norm(unit_grad, student_unit, student_len)
    return (weight_part, feature_grad)


def solution(mesh):
    return jax.shard_map(
        shards,
        mesh=mesh,
        in_specs=(P("batch", None), P("batch", None), P(None, "proto"), P(None, "proto")),
        out_specs=(P("batch", "proto"), P("batch", None)),
        check_vma=False,
    )
```

profile of v0, /device:TPU:0, one launch (start us, length us, event | category | flops | bytes accessed | tf_op | source)
XLA Modules:
  0.0 188.6 jit_solution(15052787830097034176)
XLA Ops:
  8.0 0.0 copy-start.4
  8.0 0.0 copy-start.1
  8.0 0.0 all-reduce.3.cloned.1.call-start
  8.1 1.2 fusion.10
  9.2 1.0 fusion.9
  10.3 2.0 %fusion.4 = f32[4096]{0:T(1024)S(1)} fusion(bf16[256,4096]{1,0:T(8,128)(2,1)} %param.6), kind=kLoop, calls=%fused_computation.11 | loop fusion | flops 3141632 | bytes 2113536 | tf_op jit(solution)/shard_map/reduce_sum | solution.py:24
  12.3 2.0 %fusion.2 = f32[4096]{0:T(1024)S(1)} fusion(bf16[256,4096]{1,0:T(8,128)(2,1)} %param.7), kind=kLoop, calls=%fused_computation.9 | loop fusion | flops 3141632 | bytes 2113536 | tf_op jit(solution)/shard_map/reduce_sum | solution.py:24
  14.4 0.0 copy-done.4
  14.4 0.0 copy-done.1
  14.4 3.1 %fusion.21 = (f32[4096]{0:T(1024)S(1)}, f32[256,4096]{1,0:T(8,128)}) fusion(bf16[256,4096]{1,0:T(8,128)(2,1)S(1)} %copy-done.1, f32[4096]{0:T(1024)S(1)} %add_sqrt_fusion, bf16[256,256]{1,0:T(8,128)(2,1)S(1)} %copy-done.4, f32[256]{0:T(256)S(1)} %add_sqrt_fusion.2), kind=kOutput, calls=%fused_computation.48 | convolution fusion | flops 542306304 | bytes 6456320 | tf_op jit(solution)/shard_map/dot_general | solution.py:52
  17.5 20.5 %psum.57 = f32[4096]{0:T(1024)S(1)} all-reduce(f32[4096]{0:T(1024)S(1)} %get-tuple-element.4), channel_id=1, replica_groups=mesh['batch'=4,'proto'=8] {'batch'}, use_global_device_ids=true, to_apply=%region_7.0 | all-reduce | flops 4096 | bytes 32768 | tf_op jit(solution)/shard_map/psum | solution.py:29
  38.0 2.6 %multiply_reduce_fusion.3 = f32[256]{0:T(256)S(1)} fusion(f32[256,4096]{1,0:T(8,128)} %get-tuple-element.5, f32[4096]{0:T(1024)S(1)} %broadcast_divide_fusion.2), kind=kLoop, calls=%fused_computation.17 | loop fusion | flops 2096896 | bytes 4211712 | tf_op jit(solution)/shard_map/reduce_sum | solution.py:59
  40.6 11.8 %psum.58 = f32[256]{0:T(256)S(1)} all-reduce(f32[256]{0:T(256)S(1)} %multiply_reduce_fusion.3), channel_id=1, replica_groups=mesh['batch'=4,'proto'=8] {'proto'}, use_global_device_ids=true, to_apply=%region_9.0 | all-reduce | flops 256 | bytes 2048 | tf_op jit(solution)/shard_map/psum | solution.py:59
  52.4 2.7 %multiply_reduce_fusion.2 = f32[4096]{0:T(1024)S(1)} fusion(f32[256,4096]{1,0:T(8,128)} %get-tuple-element.5, f32[256]{0:T(256)S(1)} %broadcast_divide_fusion.5), kind=kLoop, calls=%fused_computation.16 | loop fusion | flops 2093056 | bytes 4211712 | tf_op jit(solution)/shard_map/reduce_sum | solution.py:29
  55.1 15.5 %psum.59 = f32[4096]{0:T(1024)S(1)} all-reduce(f32[4096]{0:T(1024)S(1)} %multiply_reduce_fusion.2), channel_id=1, replica_groups=mesh['batch'=4,'proto'=8] {'batch'}, use_global_device_ids=true, to_apply=%region_11.0 | all-reduce | flops 4096 | bytes 32768 | tf_op jit(solution)/shard_map/psum | solution.py:29
  70.7 2.6 %multiply_reduce_fusion.1 = f32[256]{0:T(256)S(1)} fusion(f32[256,4096]{1,0:T(8,128)} %get-tuple-element.5, f32[4096]{0:T(1024)S(1)} %broadcast_divide_fusion.1), kind=kLoop, calls=%fused_computation.15 | loop fusion | flops 2096896 | bytes 4211712 | tf_op jit(solution)/shard_map/reduce_sum | solution.py:59
  73.2 11.8 %psum.60 = f32[256]{0:T(256)S(1)} all-reduce(f32[256]{0:T(256)S(1)} %multiply_reduce_fusion.1), channel_id=1, replica_groups=mesh['batch'=4,'proto'=8] {'proto'}, use_global_device_ids=true, to_apply=%region_13.0 | all-reduce | flops 256 | bytes 2048 | tf_op jit(solution)/shard_map/psum | solution.py:59
  85.0 0.0 copy-start
  85.0 0.0 copy-start.2
  85.0 2.8 %multiply_reduce_fusion = f32[4096]{0:T(1024)S(1)} fusion(f32[256,4096]{1,0:T(8,128)} %get-tuple-element.5, f32[256]{0:T(256)S(1)} %broadcast_divide_fusion.4), kind=kLoop, calls=%fused_computation.14 | loop fusion | flops 2093056 | bytes 4211712 | tf_op jit(solution)/shard_map/reduce_sum | solution.py:29
  87.9 16.3 %psum.61 = f32[4096]{0:T(1024)S(1)} all-reduce(f32[4096]{0:T(1024)S(1)} %multiply_reduce_fusion), channel_id=1, replica_groups=mesh['batch'=4,'proto'=8] {'batch'}, use_global_device_ids=true, to_apply=%region_15.0 | all-reduce | flops 4096 | bytes 32768 | tf_op jit(solution)/shard_map/psum | solution.py:29
  104.2 2.6 %multiply_reduce_fusion.4 = f32[256]{0:T(256)S(1)} fusion(f32[256,4096]{1,0:T(8,128)} %get-tuple-element.5, f32[4096]{0:T(1024)S(1)} %broadcast_divide_fusion), kind=kLoop, calls=%fused_computation.19 | loop fusion | flops 2096896 | bytes 4211712 | tf_op jit(solution)/shard_map/reduce_sum | solution.py:59
  106.7 0.0 copy-done
  106.7 0.0 copy-done.2
  106.8 3.0 %exponential_reduce_fusion = (f32[256]{0:T(256)S(1)}, f32[256,4096]{1,0:T(8,128)}) fusion(bf16[256,4096]{1,0:T(8,128)(2,1)S(1)} %copy-done.2, f32[4096]{0:T(1024)S(1)} %add_sqrt_fusion.1, f32[256]{0:T(256)S(1)} %add_sqrt_fusion.3, bf16[256,256]{1,0:T(8,128)(2,1)S(1)} %copy-done), kind=kOutput, calls=%fused_computation.18 | convolution fusion | flops 542310144 | bytes 6440960 | tf_op jit(solution)/shard_map/dot_general | solution.py:54
  109.8 11.8 %all-reduce = (f32[256]{0:T(256)S(1)}, f32[256]{0:T(256)S(1)}) all-reduce(f32[256]{0:T(256)S(1)} %multiply_reduce_fusion.4, f32[256]{0:T(256)S(1)} %get-tuple-element.6), channel_id=1, replica_groups=mesh['batch'=4,'proto'=8] {'proto'}, use_global_device_ids=true, to_apply=%region_17.0 | all-reduce | flops 512 | bytes 4096 | tf_op jit(solution)/shard_map/psum | solution.py:59
  121.6 0.0 copy-start.3
  121.6 4.9 %multiply_convert_fusion = bf16[256,4096]{1,0:T(8,128)(2,1)S(1)} fusion(f32[256,4096]{1,0:T(8,128)} %get-tuple-element.7, f32[256,4096]{1,0:T(8,128)} %get-tuple-element.5, f32[256]{0:T(256)S(1)} %broadcast_divide_fusion.3, f32[4096]{0:T(1024)S(1)} %broadcast_divide_fusion, f32[256]{0:T(256)S(1)} %log.3), kind=kLoop, calls=%fused_computation.13 | loop fusion | flops 6291456 | bytes 10504192 | tf_op jit(solution)/shard_map/convert_element_type | solution.py:65
  126.5 0.0 copy-done.3
  126.5 1.4 fusion.8
  127.9 0.0 all-reduce.3.cloned.1.call-update
  127.9 0.0 reduce-scatter.2.cloned.1.call-start
  128.0 2.2 %fusion.1 = bf16[256,4096]{1,0:T(8,128)(2,1)} fusion(bf16[256,4096]{1,0:T(8,128)(2,1)S(1)} %multiply_convert_fusion, bf16[256,256]{1,0:T(8,128)(2,1)S(1)} %copy-done, f32[256]{0:T(256)S(1)} %add_sqrt_fusion.3), kind=kOutput, calls=%fused_computation.8 | convolution fusion | flops 539164672 | bytes 4326400 | tf_op jit(solution)/shard_map/dot_general | solution.py:68
  130.2 0.0 reduce-scatter.2.cloned.1.call-update
  130.2 48.2 %all-reduce.3.cloned.1.call-done = bf16[256,256]{1,0:T(8,128)(2,1)} async-done(((bf16[256,256]{1,0:T(8,128)(2,1)}), bf16[256,256]{1,0:T(8,128)(2,1)}) %all-reduce.3.cloned.1.call-update) | async-done | bytes 131088 | tf_op jit(solution)/shard_map/psum | solution.py:83
  178.4 1.1 fusion.12
  179.5 1.7 fusion.14
  181.2 0.0 reduce-scatter.2.cloned.1.call-done
  (11 shorter events, 0.1 us)
Async XLA Ops:
  8.0 6.4 %copy-start.4 = (bf16[256,256]{1,0:T(8,128)(2,1)S(1)}, bf16[256,256]{1,0:T(8,128)(2,1)}, u32[]{:S(2)}) copy-start(bf16[256,256]{1,0:T(8,128)(2,1)} %param.4) | copy-start | bytes 393220
  8.0 6.4 %copy-start.1 = (bf16[256,4096]{1,0:T(8,128)(2,1)S(1)}, bf16[256,4096]{1,0:T(8,128)(2,1)}, u32[]{:S(2)}) copy-start(bf16[256,4096]{1,0:T(8,128)(2,1)} %param.6) | copy-start | bytes 6291460
  8.0 170.3 %all-reduce.3.cloned.1.call-start = ((), (), s32[]{:S(2)}) async-start(), calls=%async_computation.2 | async-start | bytes 262144 | tf_op jit(solution)/shard_map/psum | solution.py:83
  85.0 21.7 %copy-start = (bf16[256,256]{1,0:T(8,128)(2,1)S(1)}, bf16[256,256]{1,0:T(8,128)(2,1)}, u32[]{:S(2)}) copy-start(bf16[256,256]{1,0:T(8,128)(2,1)} %param.5) | copy-start | bytes 393220
  85.0 21.7 %copy-start.2 = (bf16[256,4096]{1,0:T(8,128)(2,1)S(1)}, bf16[256,4096]{1,0:T(8,128)(2,1)}, u32[]{:S(2)}) copy-start(bf16[256,4096]{1,0:T(8,128)(2,1)} %param.7) | copy-start | bytes 6291460
  121.6 4.9 %copy-start.3 = (bf16[256,4096]{1,0:T(8,128)(2,1)S(1)}, bf16[256,4096]{1,0:T(8,128)(2,1)}, u32[]{:S(2)}) copy-start(bf16[256,4096]{1,0:T(8,128)(2,1)} %param.7) | copy-start | bytes 6291460
  127.9 53.2 %reduce-scatter.2.cloned.1.call-start = ((), (), s32[]{:S(2)}) async-start(), calls=%async_computation.1 | async-start | bytes 2621440 | tf_op jit(solution)/shard_map/reduce_scatter | solution.py:73
Sparse Core Ops, SparseCore 0:
  128.0 50.2 all-reduce.2
Sparse Core Ops, SparseCore 1:
  131.3 40.8 reduce-scatter.1
where the time goes:
time: 189 us
  blocking collectives  87.7 us (46%)
  waiting for transfers between devices  48.2 us (26%)
  other arithmetic  27.2 us (14%)
  between operations  15.6 us (8%)
  matrix products  9.77 us (5%)
    psum x3, blocking collectives, proto_update(): sums = lax.psum(jnp.sum(teacher_exp * crop_scale[:, None], axis=0), 'batch')  52.3 us
    psum x1, waiting for transfers between devices, shards(): lax.psum(local_grad.astype(jnp.bfloat16), 'proto').astype(jnp.float32)  48.2 us
    psum x3, blocking collectives, shards(): lax.psum(jnp.sum(teacher_exp * proto_scale[None, :], axis=1), 'proto')  35.4 us
    reduce_sum x3, other arithmetic, shards(): jnp.sum(teacher_exp * proto_scale[None, :], axis=1)  7.68 us
    reduce_sum x2, other arithmetic, proto_update(): sums = lax.psum(jnp.sum(teacher_exp * crop_scale[:, None], axis=0), 'batch')  5.53 us
    convert_element_type x1, other arithmetic, shards(): grad_logits = (protos_all * (student_prob - targets)).astype(jnp.bfloat16)  4.87 us
    reduce_sum x2, other arithmetic, unit_columns(): length = jnp.sqrt(jnp.sum(values * values, axis=0, keepdims=True) + epsilon)  4.06 us
  transfers between devices with their start and end apart: 2, of which 1 were waited for; matrix products, arithmetic and copies ran while one was open for 3% of the time, Pallas kernels for 0%

commit v1 on v0

v1 whole, which is shorter than its diff:
```python
import functools
import math

import jax
import jax.numpy as jnp
from jax import lax
from jax.experimental import pallas as pl
from jax.experimental.pallas import tpu as pltpu
from jax.sharding import PartitionSpec as P

ITERS = 3

teacher_temp = 0.07
student_temp = 0.1
epsilon = 1e-06
LOG2E = 1.4426950408889634
BF = jnp.bfloat16
F32 = jnp.float32
MIB = 1024 * 1024
BLK = 512
LANES = 128


def dot(a, b):
    return jnp.dot(a, b, preferred_element_type=F32)


def split(values):
    high = values.astype(BF).astype(F32)
    return high, (values - high).astype(BF).astype(F32)


def split_rows(row):
    high, low = split(row)
    at = lax.broadcasted_iota(jnp.int32, (16, row.shape[1]), 0)
    return jnp.where(at == 0, high, jnp.where(at == 1, low, 0.0)).astype(BF)


def unit_rows(raw):
    values = raw.astype(F32)
    length = jnp.sqrt(jnp.sum(values * values, axis=1, keepdims=True) + epsilon)
    return values / length, length


def over(count, size, body, carry):
    if count <= 4:
        for i in range(count):
            carry = body(pl.ds(i * size, size), carry)
        return carry

    def step(i, carry):
        return body(pl.ds(pl.multiple_of(i * size, size), size), carry)

    return lax.fori_loop(0, count, step, carry)


def chunks(span):
    for at in range(0, span.size, 64):
        start = span.start + at
        yield pl.ds(start if isinstance(start, int) else pl.multiple_of(start, 64), 64)


def block(i):
    return pl.ds(pl.multiple_of(i * BLK, BLK), BLK)


def each_step(low, high, body):
    for i in range(low, high):
        body(i)


def two_steps(steps, first, second):
    carry = first(0)
    for i in range(1, steps):
        second(i - 1, carry)
        carry = first(i)
    second(steps - 1, carry)


def lane_groups(values):
    out = values[:, :LANES]
    for at in range(LANES, values.shape[1], LANES):
        out = out + values[:, at : at + LANES]
    return out


def sublane_groups(values):
    return jnp.sum(values.reshape(-1, 8, values.shape[1]), axis=0)


def joined(total, nb, at=0):
    return total[at : at + nb] + total[at + nb : at + 2 * nb]


def blocks_of(crops):
    height = next(h for h in (768, 512, 256, crops) if crops % h == 0)
    return crops // height, height


def row_sums(nb, rows, acc, at=0):
    spans = [slice(at + i * rows, at + (i + 1) * rows) for i in range(nb)]
    return [jnp.sum(acc[span, :].T, axis=0, keepdims=True) for span in spans]


def put_sums(sums, out, at=0):
    for i, row in enumerate(sums):
        high, low = split(row)
        out[at + i : at + i + 1, :] = high
        out[at + len(sums) + i : at + len(sums) + i + 1, :] = low


def deal(hops, head, read, count, outs, kept, chips=0):
    many = 1 + len(hops)
    me = lax.axis_index("proto")
    digit = (me // hops[0]) % many
    for hop, out in zip((0, *hops), (kept, *outs)):
        out[0 : head.shape[0], :] = head[...].astype(out.dtype)
        for m in range(count // many):
            turn = (me // 2 % chips == m % chips).astype(jnp.int32) if chips else 0
            rows = read(m * many + (digit ^ (hop // hops[0]) ^ turn)).astype(out.dtype)
            at = head.shape[0] + m * rows.shape[0]
            out[at : at + rows.shape[0], :] = rows


def added(refs):
    acc = refs[0][...].astype(F32)
    for ref in refs[1:]:
        acc = acc + ref[...].astype(F32)
    return acc


def halves_kernel(teacher_ref, student_ref, out, sems):
    half = out.shape[0] * 2 // 3
    me = lax.axis_index("proto")
    start = pl.multiple_of(me % 2 * half, half)
    quarter = pl.multiple_of(start + me // 2 % 2 * (half // 2), half // 2)
    first = pltpu.make_async_copy(
        teacher_ref.at[pl.ds(start, half), :], out.at[0:half, :], sems.at[0]
    )
    second = pltpu.make_async_copy(
        student_ref.at[pl.ds(quarter, half // 2), :], out.at[half:, :], sems.at[1]
    )
    first.start()
    second.start()
    first.wait()
    second.wait()


def units_kernel(after, also, *refs):
    blocks, outs = refs[-3::-1], refs[-2:]
    start = 0
    for out in outs:
        size = out.shape[0] // len(blocks)
        for i, ref in enumerate(blocks):
            rows = unit_rows(ref[start : start + size, :])[0]
            out[i * size : (i + 1) * size, :] = rows.astype(BF)
        start += size


def quarters_kernel(size, after, mine, moved, out):
    side = lax.axis_index("proto") // 2 % 2
    for i in range(mine.shape[0] // size):
        for ref, place in ((mine, side), (moved, 1 - side)):
            at = pl.multiple_of((2 * i + place) * size, size)
            out[pl.ds(at, size), :] = ref[i * size : (i + 1) * size, :]


def place_kernel(mine, other, out):
    far = mine.shape[0]
    core = lax.axis_index("proto") % 2
    for ref, place in ((mine, core), (other, 1 - core)):
        out[pl.ds(pl.multiple_of(place * far, 128), far), :] = ref[...]


def weights_kernel(wt_ref, ws_ref, wt_out, ws_out, turned_out, raw, sems):
    steps = wt_out.shape[0]

    def copy(i, which):
        src = (wt_ref, ws_ref)[which]
        return pltpu.make_async_copy(src.at[:, block(i)], raw.at[which, i], sems.at[which, i])

    for which in range(2):
        for i in range(steps):
            copy(i, which).start()

    def unit(i, which):
        copy(i, which).wait()
        values = raw[which, i].astype(F32)
        length = jnp.sqrt(jnp.sum(values * values, axis=0, keepdims=True) + epsilon)
        return (values * ((LOG2E / (teacher_temp, student_temp)[which]) / length)).astype(BF)

    def teacher(i):
        wt_out[i] = unit(i, 0)

    def student(i):
        ws = unit(i, 1)
        ws_out[i] = ws
        turned_out[i] = ws.T

    each_step(0, steps, teacher)
    each_step(0, steps, student)


def add_across(rows, refs, i, ps, acc):
    own, rest = refs
    ps = ps.astype(BF)

    def across(ref, start):
        def step(span, carry):
            for at in chunks(span):
                to = pl.ds(at.start + start, at.size)
                scaled = ref[i, at, :] * ps
                half = scaled[:, : BLK // 2] + scaled[:, BLK // 2 :]
                acc[to, :] += lane_groups(half.astype(F32))
            return carry

        return step

    over(1, rows, across(own, 0), 0)
    over(*blocks_of(rest.shape[1]), across(rest, rows), 0)


def own_first_kernel(own, wt_ref, e_ref, cols_ref, zt):
    zt[...] = unit_rows(own[...])[0].astype(BF)

    def body(i):
        e = jnp.exp2(dot(zt[...], wt_ref[i]))
        e_ref[i] = e.astype(BF)
        cols_ref[i] = sublane_groups(e)

    each_step(0, wt_ref.shape[0], body)


def exps_of(side, units, i, wt_ref, e_ref, cols):
    far = units.shape[0]
    height = 384 if far % 384 == 0 else 128

    def down(span, total):
        logits = dot(units[span, :], wt_ref[i])
        for k, at in enumerate(chunks(span)):
            e = jnp.exp2(logits[k * 64 : (k + 1) * 64, :])
            to = pl.ds(pl.multiple_of(side * far + at.start, 64), 64)
            e_ref[i, to, :] = e.astype(BF)
            total = total + sublane_groups(e)
        return total

    return over(far // height, height, down, cols)


def mine_first_kernel(mine, wt_ref, own_cols, e_ref, cols_ref):
    side = lax.axis_index("proto") % 2

    def body(i):
        cols_ref[i] = exps_of(side, mine, i, wt_ref, e_ref, own_cols[i])

    each_step(0, wt_ref.shape[0], body)


def first_kernel(nb, begun, *refs):
    mine, other, wt_ref, own_ref, cols_ref, e_ref, out_ref, acc = refs[begun:]
    rows = own_ref.shape[1]
    side = lax.axis_index("proto") % 2
    acc[...] = jnp.zeros_like(acc)

    def exps(i):
        total = exps_of(1 - side, other, i, wt_ref, e_ref, cols_ref[i])
        if not begun:
            total = exps_of(side, mine, i, wt_ref, e_ref, total)
        return 1.0 / jnp.sum(total, axis=0, keepdims=True)

    refs = (own_ref, e_ref)
    two_steps(wt_ref.shape[0], exps, lambda i, ps: add_across(rows, refs, i, ps, acc))
    for i, row in enumerate(row_sums(nb, rows, acc)):
        out_ref[i : i + 1, :] = row


def start_sweep(nb, sums, cs, turned, acc):
    width = sums.shape[1]
    for i in range(nb):
        scale = 1.0 / sums[i : i + 1]
        span = slice(i * width, (i + 1) * width)
        if i < 2:
            turned[span, :] = jnp.broadcast_to(scale, (LANES, width)).T.astype(BF)
        else:
            cs[:, span] = split_rows(scale)
    acc[...] = jnp.zeros_like(acc)


def proto_scale(refs, i, cs, turned):
    own, rest = refs
    rows = own.shape[1]
    total = jnp.zeros((8, BLK), F32)
    for ref, start in ((own, 0), (rest, rows)):
        for at in chunks(pl.ds(0, rows)):
            scale = turned[start + at.start : start + at.start + 64, :]
            scaled = ref[i, at, :] * jnp.concatenate([scale] * (BLK // LANES), axis=1)
            total = total + sublane_groups((scaled[:32] + scaled[32:]).astype(F32))
    down = dot(cs[:, 2 * rows :], rest[i, rows:, :])
    total = jnp.sum(total, axis=0, keepdims=True) + jnp.sum(down, axis=0, keepdims=True)
    return 1.0 / total


def sweep_kernel(nb, after, x_ref, own_ref, e_ref, out_ref, cs, turned, acc):
    rows = own_ref.shape[1]
    both = (own_ref, e_ref)
    start_sweep(nb, x_ref[...], cs, turned, acc)
    two_steps(
        e_ref.shape[0],
        lambda i: proto_scale(both, i, cs, turned),
        lambda i, ps: add_across(rows, both, i, ps, acc),
    )
    for i, row in enumerate(row_sums(nb, rows, acc)):
        out_ref[i : i + 1, :] = row


def last_sweep_kernel(nb, k, n, hops, chips, x_ref, own_ref, e_ref, ws_rows, student, own_tot, *refs):
    tots, ps_ref, kept, outs = refs[:k], refs[k], refs[k + 1], refs[k + 2 : -5]
    cs, turned, acc, head, grad = refs[-5:]
    rows = own_ref.shape[1]
    both = (own_ref, e_ref)
    start_sweep(nb, x_ref[...], cs, turned, acc)
    grad[...] = jnp.zeros_like(grad)

    def across(i, ps):
        ps_ref[i] = ps
        add_across(rows, both, i, ps, acc)
        grad[...] += dot(own_ref[i] * ps.astype(BF), ws_rows[i])

    two_steps(e_ref.shape[0], lambda i: proto_scale(both, i, cs, turned), across)
    head[...] = jnp.zeros_like(head)
    put_sums(row_sums(nb, rows, acc), head)
    tot = tots[0][...]
    for more in tots[1:]:
        tot = tot + more[...]
    put_sums([own_tot[...]] + [tot[i : i + 1] for i in range(nb - 1)], head, 2 * nb)
    part = rows // n

    def read(r):
        at = pl.ds(pl.multiple_of(r * part, part), part)
        fill = [jnp.zeros((16 - part, grad.shape[1]), F32)] if part < 16 else []
        return jnp.concatenate([grad[at, :], *fill, student[at, :], *fill], axis=0)

    deal(hops, head, read, n, outs, kept, chips)


def deal_kernel(nb, count, hops, *refs):
    k = len(refs) - 3 - len(hops)
    arrived, kept, outs, (head, sums) = refs[:k], refs[k], refs[k + 1 : -2], refs[-2:]
    total = added(arrived)
    head[...] = jnp.zeros_like(head)
    for at in (0, 2 * nb):
        both = joined(total, nb, at)
        put_sums([both[i : i + 1] for i in range(nb)], head, at)
    sums[...] = total[head.shape[0] :]
    size = sums.shape[0] // count

    def read(r):
        return sums[pl.ds(pl.multiple_of(r * size, size), size), :]

    deal(hops, head, read, count, outs, kept)


def own_student_kernel(own, ws_ref, turned_ref, zs_ref, tot_ref, grad, s_ref, acc):
    zs_ref[...] = unit_rows(own[...])[0].astype(BF)
    acc[...] = jnp.zeros_like(acc)
    grad[...] = jnp.zeros_like(grad)
    kept = s_ref.shape[0] > 1

    def body(i):
        s = jnp.exp2(dot(zs_ref[...], ws_ref[i]))
        acc[...] += lane_groups(s)
        s_ref[i if kept else 0] = s.astype(BF)
        grad[...] += dot(s.astype(BF), turned_ref[i])

    each_step(0, ws_ref.shape[0], body)
    tot_ref[...] = row_sums(1, own.shape[0], acc)[0]


def student_kernel(first, count, after, zs_ref, ws_ref, tot_ref, s_ref, acc):
    acc[...] = jnp.zeros_like(acc)
    kept = s_ref.shape[0] > 1
    rows = tot_ref.shape[1]

    def body(i):
        j = i if kept else 0

        def exps(span, carry):
            logits = dot(zs_ref[span, :], ws_ref[i + first])
            for k, at in enumerate(chunks(span)):
                s = jnp.exp2(logits[k * 64 : (k + 1) * 64, :])
                acc[at, :] += lane_groups(s)
                s_ref[j, at, :] = s.astype(BF)
            return carry

        over(zs_ref.shape[0] // rows, rows, exps, 0)

    each_step(0, count, body)
    for i, row in enumerate(row_sums(tot_ref.shape[0], rows, acc)):
        tot_ref[i : i + 1, :] = row


def scaled_features(zs_refs, sums, out):
    here, width = out.shape[0], zs_refs[0].shape[1]
    at = lax.broadcasted_iota(jnp.int32, (here, width), 1)
    row = lax.broadcasted_iota(jnp.int32, (here, width), 0)
    pick = jnp.where(at == row + lax.axis_index("batch") * here, 1.0, 0.0).astype(BF)
    rows = zs_refs[0].shape[0]
    i = 0
    for ref in zs_refs:
        for start in range(0, ref.shape[0], rows):
            turned = lax.dot_general(
                pick,
                ref[start : start + rows, :],
                (((1,), (1,)), ((), ())),
                preferred_element_type=F32,
            )
            out[:, i * rows : (i + 1) * rows] = (turned * (1.0 / sums[i : i + 1])).astype(BF)
            i += 1


def feature_kernel(nb, k, factor, *refs):
    arrived, (feats_ref, own_zs, zs_ref, share_ref, lhs, ratio) = refs[:k], refs[k:]
    part, width = share_ref.shape
    rows = feats_ref.shape[0]
    padded = max(part, 16)
    total = added(arrived)
    sums, tots = joined(total, nb), joined(total, nb, 2 * nb)
    teacher, student = total[-2 * padded :][:part], total[-padded:][:part]
    at = lax.broadcasted_iota(jnp.int32, (part, rows), 1)
    row = lax.broadcasted_iota(jnp.int32, (part, rows), 0)
    pick = at == row + (lax.axis_index("proto") ^ 1) * part
    crop_scale = 1.0 / jnp.sum(jnp.where(pick, sums[0:1], 0.0), axis=1, keepdims=True)
    prob_scale = 1.0 / jnp.sum(jnp.where(pick, tots[0:1], 0.0), axis=1, keepdims=True)
    raw = dot(jnp.where(pick, 1.0, 0.0).astype(BF), feats_ref[...])
    unit, length = unit_rows(raw)
    grad = factor * (student * prob_scale - teacher * crop_scale)
    along = jnp.sum(unit * grad, axis=1, keepdims=True)
    share_ref[...] = ((grad - unit * along) / length).astype(share_ref.dtype)

    scaled_features((own_zs, zs_ref), sums, lhs)
    for i in range(nb):
        span = slice(i * rows, (i + 1) * rows)
        scale = jnp.broadcast_to(sums[i : i + 1] / tots[i : i + 1], (LANES, rows)).T
        ratio[span, :] = scale.astype(BF)


def weight_kernel(first, count, factor, aliased, starts, *refs):
    own_e, e_ref, ps_ref, own_zs, zs_ref, lhs, ratio = refs[1 + aliased : 8 + aliased]
    sources, (out_ref, token, diff, put, sems) = refs[8 + aliased : -5], refs[-5:]
    token[...] = jnp.zeros_like(token)
    rows = own_e.shape[1]

    def copy(i):
        return pltpu.make_async_copy(put.at[i], out_ref.at[:, block(i + first)], sems.at[i])

    def body(i, own_s, s_ref):
        ps = ps_ref[i].astype(BF)

        def down(zs, s, e, start):
            def step(span, acc):
                to = pl.ds(span.start + start, span.size)
                if not starts:
                    diff[to, :] = jnp.exp2(dot(zs[span, :], s[...])).astype(BF)
                for at in chunks(span):
                    to = pl.ds(at.start + start, at.size)
                    scale = jnp.concatenate([ratio[to, :]] * (BLK // LANES), axis=1)
                    left = (s[at, :] if starts else diff[to, :]) * scale
                    diff[to, :] = left - e[i, at, :] * ps
                to = pl.ds(span.start + start, span.size)
                return acc + dot(lhs[:, to], diff[to, :])

            return step

        acc = over(1, rows, down(own_zs, own_s, own_e, 0), jnp.zeros((lhs.shape[0], BLK), F32))
        acc = over(zs_ref.shape[0] // rows, rows, down(zs_ref, s_ref, e_ref, rows), acc)
        put[i - first] = (factor * acc).astype(BF)
        copy(i - first).start()

    def run(low, high, pick):
        if low < high:
            each_step(low, high, lambda i: body(i, *pick(i)))

    if starts:
        own_s, *kept = sources
        for low, high, ref in zip(starts, starts[1:], kept):
            run(
                max(low, first),
                min(high, first + count),
                lambda i, low=low, ref=ref: (own_s.at[i], ref.at[i - low]),
            )
    else:
        run(first, first + count, lambda i: (sources[0].at[i], sources[0].at[i]))
    for i in range(count):
        copy(i).wait()


def join_kernel(hops, after, share, *refs):
    moved, out_ref = refs[:-1], refs[-1]
    rows = share.shape[0]
    me = lax.axis_index("proto") ^ 1
    for hop, ref in zip((0, *hops[::-1]), (share, *moved)):
        place = ((me ^ hop) // hops[0]) % (1 + len(hops))
        out_ref[pl.ds(pl.multiple_of(place * rows, rows), rows), :] = ref[...].astype(out_ref.dtype)


def permute(value, axis, s):
    n = lax.axis_size(axis)
    return lax.ppermute(value, axis, [(i, i ^ s) for i in range(n)])


def stages(n):
    bits = n.bit_length() - 1
    pairs = [[1 << b, 2 << b, 3 << b] if b + 1 < bits else [1 << b] for b in range(1, bits, 2)]
    return [[1]] + pairs


def permutes(value, axis, hops):
    return [permute(value, axis, hop) for hop in reversed(hops)][::-1]


def crossed(hop):
    return hop | 1


def shards(teacher_feats, student_feats, teacher_weight, student_weight):
    rows, width = teacher_feats.shape
    protos = teacher_weight.shape[1]
    nb, n = lax.axis_size("batch"), lax.axis_size("proto")
    crops, protos_all = rows * nb, protos * n
    here, part = width // nb, rows // n
    padded = max(part, 16)
    large = -(-4 * nb // 16) * 16
    keep = crops * protos <= 8 * MIB
    big = crops * protos
    wide = width * protos
    steps = protos // BLK

    limit = (16 if keep else 56) * MIB

    vmem = pl.BlockSpec(memory_space=pltpu.VMEM)
    hbm = pl.BlockSpec(memory_space=pltpu.HBM)
    anywhere = pl.BlockSpec(memory_space=pl.ANY)

    def shape(*dims, dtype=F32):
        return jax.ShapeDtypeStruct(dims, dtype)

    def call(kernel, out_shape, scratch, flops, moved, exps, *args, far=(), after=(), aliases={}):
        far = [pltpu.with_memory_space_constraint(a, pltpu.HBM) for a in far]
        return pl.pallas_call(
            kernel,
            out_shape=out_shape,
            in_specs=[hbm] * len(far)
            + [anywhere] * len(after)
            + [vmem] * len(args),
            out_specs=[vmem] * len(out_shape),
            scratch_shapes=scratch,
            input_output_aliases=aliases,
            compiler_params=pltpu.CompilerParams(vmem_limit_bytes=limit),
            cost_estimate=pl.CostEstimate(
                flops=int(flops), bytes_accessed=int(moved), transcendentals=int(exps)
            ),
        )(*far, *after, *args)

    def weight_call(kernel, out_shape, scratch, flops, moved, done, after, *args):
        return pl.pallas_call(
            kernel,
            out_shape=[out_shape, shape(8, LANES)],
            in_specs=[hbm] * len(done) + [anywhere] + [vmem] * len(args),
            out_specs=[hbm, vmem],
            scratch_shapes=scratch,
            input_output_aliases={0: 0} if done else {},
            compiler_params=pltpu.CompilerParams(vmem_limit_bytes=limit),
            cost_estimate=pl.CostEstimate(
                flops=int(flops), bytes_accessed=int(moved), transcendentals=0
            ),
        )(*done, after, *args)

    rest, half = crops - rows, rows // 2
    turned_crops = pltpu.VMEM((16, crops), BF)
    lane_sums = pltpu.VMEM((crops, LANES), F32)
    rounds = stages(n)
    sizes = [steps // 4, steps - steps // 4]
    weight_sizes = [steps // 4, steps - steps // 4]

    (mine,) = call(
        halves_kernel,
        [shape(half * 3 // 2, width, dtype=BF)],
        [pltpu.SemaphoreType.DMA((2,))],
        0,
        4 * rows * width,
        0,
        far=(teacher_feats, student_feats),
    )
    blocks = permutes(mine, "batch", range(1, nb))

    unit_wt, unit_ws, turned_ws = call(
        weights_kernel,
        [shape(steps, width, BLK, dtype=BF)] * 2 + [shape(steps, BLK, width, dtype=BF)],
        [pltpu.VMEM((2, steps, width, BLK), BF), pltpu.SemaphoreType.DMA((2, steps))],
        16 * wide,
        10 * wide,
        0,
        far=(teacher_weight, student_weight),
    )
    own_e, own_cols = call(
        own_first_kernel,
        [shape(steps, rows, BLK, dtype=BF), shape(steps, 8, BLK)],
        [pltpu.VMEM((rows, width), BF)],
        2 * rows * protos * width,
        2 * rows * protos,
        rows * protos,
        teacher_feats,
        unit_wt,
    )
    own_zs, own_tot, grad, own_s = call(
        own_student_kernel,
        [
            shape(rows, width, dtype=BF),
            shape(1, rows),
            shape(rows, width),
            shape(steps if keep else 1, rows, BLK, dtype=BF),
        ],
        [pltpu.VMEM((rows, LANES), F32)],
        4 * rows * protos * width,
        2 * rows * protos,
        rows * protos,
        student_feats,
        unit_ws,
        turned_ws,
    )

    mine, quarters = call(
        units_kernel,
        [shape(rest // 2, width, dtype=BF), shape(rest // 4, width, dtype=BF)],
        [],
        8 * crops * width,
        2 * crops * width,
        0,
        *reversed(blocks),
        after=(own_cols, own_tot),
    )
    other = permute(mine, "proto", 1)
    moved = permute(quarters, "proto", 2)

    begun, cols = (), own_cols
    if keep:
        *begun, cols = call(
            mine_first_kernel,
            [shape(steps, rest, BLK, dtype=BF), shape(steps, 8, BLK)],
            [],
            rest * protos * width,
            rest * protos,
            rest * protos // 2,
            mine,
            unit_wt,
            own_cols,
        )
    e, x = call(
        functools.partial(first_kernel, nb, len(begun)),
        [shape(steps, rest, BLK, dtype=BF), shape(nb, width)],
        [lane_sums],
        2 * big * width,
        2 * big,
        big,
        *begun,
        mine,
        other,
        unit_wt,
        own_e,
        cols,
        aliases={0: 0} if begun else {},
    )
    (student_mine,) = call(
        functools.partial(quarters_kernel, half // 2),
        [shape(rest // 2, width, dtype=BF)],
        [],
        0,
        2 * rest * width,
        0,
        quarters,
        moved,
        after=(x,),
    )
    (zs,) = call(
        place_kernel,
        [shape(rest, width, dtype=BF)],
        [],
        0,
        4 * rest * width,
        0,
        student_mine,
        permute(student_mine, "proto", 1),
    )

    tots, kept = [], []

    def student_piece(after):
        k = len(kept)
        tot, piece = call(
            functools.partial(student_kernel, sum(sizes[:k]), sizes[k]),
            [shape(nb - 1, rows), shape(sizes[k] if keep else 1, rest, BLK, dtype=BF)],
            [pltpu.VMEM((rest, LANES), F32)],
            2 * rest * width * BLK * sizes[k],
            2 * rest * BLK * sizes[k],
            rest * BLK * sizes[k],
            zs,
            unit_ws,
            after=(after,),
        )
        tots.append(tot)
        kept.append(piece)

    def summed(x, pieces):
        for k, hops in enumerate(rounds):
            moved = permutes(x, "proto", [crossed(hop) for hop in hops])
            if k in pieces:
                student_piece(x)
            for value in reversed(moved):
                x = x + value
        return x

    x = summed(x, ())
    (x,) = call(
        functools.partial(sweep_kernel, nb),
        [shape(nb, width)],
        [turned_crops, pltpu.VMEM((2 * rows, LANES), BF), lane_sums],
        4 * big,
        2 * big,
        0,
        x,
        own_e,
        e,
        after=(zs,),
    )
    x = summed(x, (0, 1))

    def dealt(count, many):
        height = large + count // many * 2 * padded
        return [shape(height, width)] + [shape(height, width, dtype=BF)] * (many - 1)

    scale, *x = call(
        functools.partial(last_sweep_kernel, nb, len(tots), n, rounds[0], 1 + len(rounds[1])),
        [shape(steps, 1, BLK)] + dealt(n, 1 + len(rounds[0])),
        [
            turned_crops,
            pltpu.VMEM((2 * rows, LANES), BF),
            lane_sums,
            pltpu.VMEM((large, width), F32),
            pltpu.VMEM((rows, width), F32),
        ],
        4 * big,
        2 * big,
        0,
        x,
        own_e,
        e,
        turned_ws,
        grad,
        own_tot,
        *tots,
    )
    count = n
    for k, hops in enumerate(rounds):
        pairs = [crossed(hop) if k == 1 else hop for hop in hops]
        moved = [permute(x[1 + i], "proto", pairs[i]) for i in reversed(range(len(pairs)))]
        x = [x[0]] + moved
        count //= 1 + len(hops)
        if k + 1 < len(rounds):
            x = call(
                functools.partial(deal_kernel, nb, count, rounds[k + 1]),
                dealt(count, 1 + len(rounds[k + 1])),
                [pltpu.VMEM((large, width), F32), pltpu.VMEM((count * 2 * padded, width), F32)],
                4 * count * padded * width,
                8 * count * padded * width,
                0,
                *x,
            )

    factor = protos_all * math.sqrt(width / protos_all) * (student_temp / LOG2E)
    share, lhs, ratio = call(
        functools.partial(feature_kernel, nb, len(x), factor),
        [
            shape(part, width, dtype=BF if part % 16 == 0 else F32),
            shape(here, crops, dtype=BF),
            shape(crops, LANES, dtype=BF),
        ],
        [],
        0,
        8 * rows * width,
        0,
        *x,
        student_feats,
        own_zs,
        zs,
    )

    done = ()
    for k, hops in enumerate(rounds):
        moved = permutes(share, "proto", [crossed(hop) for hop in hops])
        if k < len(weight_sizes):
            first, size = sum(weight_sizes[:k]), weight_sizes[k]
            *done, token = weight_call(
                functools.partial(
                    weight_kernel,
                    first,
                    size,
                    protos_all * math.sqrt(width / crops),
                    len(done),
                    [sum(sizes[:i]) for i in range(len(sizes) + 1)] if keep else [],
                ),
                shape(here, protos, dtype=BF),
                [
                    pltpu.VMEM((crops, BLK), BF),
                    pltpu.VMEM((size, here, BLK), BF),
                    pltpu.SemaphoreType.DMA((size,)),
                ],
                2 * big * here * size // steps,
                4 * big * size // steps,
                done,
                share,
                own_e,
                e,
                scale,
                own_zs,
                zs,
                lhs,
                ratio,
                *((own_s, *kept) if keep else (unit_ws,)),
            )
        (share,) = call(
            functools.partial(join_kernel, hops),
            [shape((1 + len(hops)) * share.shape[0], width, dtype=BF if k + 1 == len(rounds) else share.dtype)],
            [],
            0,
            8 * share.shape[0] * width,
            0,
            share,
            *reversed(moved),
            after=(token,),
        )
    return (done[0], share)


def solution(mesh):
    return jax.shard_map(
        shards,
        mesh=mesh,
        in_specs=(P("batch", None), P("batch", None), P(None, "proto"), P(None, "proto")),
        out_specs=(P("batch", "proto"), P("batch", None)),
        check_vma=False,
    )
```

time: 189 us -> 53.9 us (0.29)
  blocking collectives: 87.7 us -> 0 us
  waiting for transfers between devices: 48.2 us -> 9.76 us
  other arithmetic: 27.2 us -> 0.02 us
  Pallas kernels: 0 us -> 22 us
  starting transfers between devices: 0.08 us -> 21 us
  between operations: 15.6 us -> 0.82 us
  matrix products: 9.77 us -> 0 us
    psum x6 -> x0, blocking collectives: 87.7 us -> none  [the longest x3 52.3 us: proto_update(): sums = lax.psum(jnp.sum(teacher_exp * crop_scale[:, None], axis=0), 'batch')]
    psum x1 -> x0, waiting for transfers between devices: 48.2 us -> none  [shards(): lax.psum(local_grad.astype(jnp.bfloat16), 'proto').astype(jnp.float32)]
    pallas_call x0 -> x19, Pallas kernels: none -> 22 us  [the longest x17 18.7 us: call(): pl.pallas_call(kernel, out_shape=out_shape, in_specs=[hbm] * len(far) + [...]
    ppermute x0 -> x22, starting transfers between devices: none -> 21 us  [permute(): return lax.ppermute(value, axis, [(i, i ^ s) for i in range(n)])]
    reduce_sum x10 -> x0, other arithmetic: 20.5 us -> none  [the longest x3 7.68 us: shards(): jnp.sum(teacher_exp * proto_scale[None, :], axis=1)]
    dot_general x4 -> x0, matrix products: 9.77 us -> none  [the longest x1 3.13 us: shards(): jnp.dot(teacher_half, teacher_cols, preferred_element_type=jnp.float32)]
    ppermute x0 -> x22, waiting for transfers between devices: none -> 9.76 us  [permute(): return lax.ppermute(value, axis, [(i, i ^ s) for i in range(n)])]
    convert_element_type x2 -> x0, other arithmetic: 6.59 us -> none  [the longest x1 4.87 us: shards(): grad_logits = (protos_all * (student_prob - targets)).astype(jnp.bfloat16)]
  transfers between devices with their start and end apart: 2 -> 22, of which waited for: 1 -> 13; matrix products, arithmetic and copies ran while one was open for 3% -> 0% of each run, Pallas kernels for 0% -> 28%
where the time goes in v1:
time: 53.9 us; the launch traced here: 53.7 us
  Pallas kernels  22 us (41%)
  starting transfers between devices  21 us (39%)
  waiting for transfers between devices  9.76 us (18%)
  between operations  0.82 us (2%)
    ppermute x22, starting transfers between devices, permute(): return lax.ppermute(value, axis, [(i, i ^ s) for i in range(n)])  21 us
    pallas_call x17, Pallas kernels, call(): pl.pallas_call(kernel, out_shape=out_shape, in_specs=[hbm] * len(far) + [...  18.7 us
    ppermute x22, waiting for transfers between devices, permute(): return lax.ppermute(value, axis, [(i, i ^ s) for i in range(n)])  9.76 us
    pallas_call x2, Pallas kernels, weight_call(): pl.pallas_call(kernel, out_shape=[out_shape, shape(8, LANES)], in_specs=[...  3.31 us
  transfers between devices with their start and end apart: 22, of which 13 were waited for; matrix products, arithmetic and copies ran while one was open for 0% of the time, Pallas kernels for 28%

profile of v1, /device:TPU:0, one launch (start us, length us, event | category | flops | bytes accessed | tf_op | source)
XLA Modules:
  0.0 53.7 jit_solution(1567190018385655310)
XLA Ops:
  0.6 0.9 %shard_map.62 = bf16[192,256]{1,0:T(8,128)(2,1)S(1)} custom-call(bf16[256,256]{1,0:T(8,128)(2,1)} %teacher_ref.1, bf16[256,256]{1,0:T(8,128)(2,1)} %refs_4_.1), custom_call_target="tpu_custom_call" | custom-call | bytes 262144 | tf_op jit(solution)/shard_map/pallas_call | solution.py:549
  1.5 5.1 %collective-permute-start = (bf16[192,256]{1,0:T(8,128)(2,1)S(1)}, bf16[192,256]{1,0:T(8,128)(2,1)S(1)}, u32[]{:S(2)}, u32[]{:S(2)}) collective-permute-start(bf16[192,256]{1,0:T(8,128)(2,1)S(1)} %shard_map.62), channel_id=1, source_target_pairs={{0,24},{8,16},{16,8},{24,0},{1,25},{9,17},{17,9},{25,1},{2,26},{10... | collective-permute-start | bytes 294920 | tf_op jit(solution)/shard_map/ppermute | solution.py:508
  6.6 0.6 %collective-permute-start.2 = (bf16[192,256]{1,0:T(8,128)(2,1)S(1)}, bf16[192,256]{1,0:T(8,128)(2,1)S(1)}, u32[]{:S(2)}, u32[]{:S(2)}) collective-permute-start(bf16[192,256]{1,0:T(8,128)(2,1)S(1)} %shard_map.62), channel_id=1, source_target_pairs={{0,8},{8,0},{16,24},{24,16},{1,9},{9,1},{17,25},{25,17},{2,10},{10... | collective-permute-start | bytes 294920 | tf_op jit(solution)/shard_map/ppermute | solution.py:508
  7.3 3.3 %shard_map.59 = (bf16[8,256,512]{2,1,0:T(8,128)(2,1)S(1)}, bf16[8,256,512]{2,1,0:T(8,128)(2,1)S(1)}, bf16[8,512,256]{2,1,0:T(8,128)(2,1)S(1)}) custom-call(bf16[256,4096]{1,0:T(8,128)(2,1)} %wt_ref.1, bf16[256,4096]{1,0:T(8,128)(2,1)} %ws_ref.1), custom_call_target="tpu_custom_call" | custom-call | flops 16777216 | bytes 10485760 | tf_op jit(solution)/shard_map/pallas_call | solution.py:549
  10.7 0.8 %shard_map.60 = (bf16[8,256,512]{2,1,0:T(8,128)(2,1)S(1)}, f32[8,8,512]{2,1,0:T(8,128)S(1)}) custom-call(bf16[256,256]{1,0:T(8,128)(2,1)S(1)} %copy-done.1, bf16[8,256,512]{2,1,0:T(8,128)(2,1)S(1)} %get-tuple-element.35.wt_ref.refs_3_), custom_call_target="tpu_custom_call" | custom-call | flops 536870912 | bytes 2097152 | tf_op jit(solution)/shard_map/pallas_call | solution.py:549
  11.5 1.5 %shard_map.61 = (bf16[256,256]{1,0:T(8,128)(2,1)S(1)}, f32[1,256]{1,0:T(1,128)S(1)}, f32[256,256]{1,0:T(8,128)S(1)}, bf16[8,256,512]{2,1,0:T(8,128)(2,1)S(1)}) custom-call(bf16[256,256]{1,0:T(8,128)(2,1)S(1)} %copy-done, bf16[8,256,512]{2,1,0:T(8,128)(2,1)S(1)} %get-tuple-element.37.ws_ref, bf16[8,512,256]{2,1,0:T(8,128)(2,1)S(1)} %get-tuple-element.38.turned_ref.ws_rows), custom_call_target="tpu_custom_call" | custom-call | flops 1073741824 | bytes 2097152 | tf_op jit(solution)/shard_map/pallas_call | solution.py:549
  13.0 1.9 %collective-permute-done.1.refs_1_ = bf16[192,256]{1,0:T(8,128)(2,1)S(1)} collective-permute-done((bf16[192,256]{1,0:T(8,128)(2,1)S(1)}, bf16[192,256]{1,0:T(8,128)(2,1)S(1)}, u32[]{:S(2)}, u32[]{:S(2)}) %collective-permute-start.1) | collective-permute-done | bytes 98336 | tf_op jit(solution)/shard_map/ppermute | solution.py:508
  14.9 0.2 shard_map.63
  15.2 1.6 %collective-permute-start.4 = (bf16[192,256]{1,0:T(8,128)(2,1)S(1)}, bf16[192,256]{1,0:T(8,128)(2,1)S(1)}, u32[]{:S(2)}, u32[]{:S(2)}) collective-permute-start(bf16[192,256]{1,0:T(8,128)(2,1)S(1)} %get-tuple-element.45.mine), channel_id=1, source_target_pairs={{0,2},{1,3},{2,0},{3,1},{4,6},{5,7},{6,4},{7,5},{8,10},{9,11},{10,... | collective-permute-start | bytes 294920 | tf_op jit(solution)/shard_map/ppermute | solution.py:508
  16.8 1.0 %shard_map.64 = (bf16[8,768,512]{2,1,0:T(8,128)(2,1)S(1)}, f32[8,8,512]{2,1,0:T(8,128)S(1)}) custom-call(bf16[384,256]{1,0:T(8,128)(2,1)S(1)} %get-tuple-element.40.mine.refs_1_, bf16[8,256,512]{2,1,0:T(8,128)(2,1)S(1)} %get-tuple-element.35.wt_ref.refs_3_, f32[8,8,512]{2,1,0:T(8,128)S(1)} %get-tuple-element.36.after.own_cols), custom_call_target="tpu_custom_call" | custom-call | flops 805306368 | bytes 3145728 | tf_op jit(solution)/shard_map/pallas_call | solution.py:549
  17.7 2.9 %shard_map.65 = (bf16[8,768,512]{2,1,0:T(8,128)(2,1)S(1)}, f32[4,256]{1,0:T(4,128)S(1)}) custom-call(bf16[8,768,512]{2,1,0:T(8,128)(2,1)S(1)} %get-tuple-element.41.refs_0_, bf16[384,256]{1,0:T(8,128)(2,1)S(1)} %get-tuple-element.40.mine.refs_1_, bf16[384,256]{1,0:T(8,128)(2,1)S(1)} %collective-permute-done.3.refs_2_, ...), custom_call_target="tpu_custom_call", output_to_operand_aliasing={{0}: (0, {})} | custom-call | flops 2147483648 | bytes 8388608 | tf_op jit(solution)/shard_map/pallas_call | solution.py:549
  20.7 0.2 collective-permute-start.6
  20.9 1.0 %collective-permute-done.6 = f32[4,256]{1,0:T(4,128)S(1)} collective-permute-done((f32[4,256]{1,0:T(4,128)S(1)}, f32[4,256]{1,0:T(4,128)S(1)}, u32[]{:S(2)}, u32[]{:S(2)}) %collective-permute-start.6) | collective-permute-done | bytes 4128 | tf_op jit(solution)/shard_map/ppermute | solution.py:508
  21.9 1.3 %collective-permute-start.7 = (f32[4,256]{1,0:T(4,128)S(1)}, f32[4,256]{1,0:T(4,128)S(1)}, u32[]{:S(2)}, u32[]{:S(2)}) collective-permute-start(f32[4,256]{1,0:T(4,128)S(1)} %add.24), channel_id=1, source_target_pairs={{0,7},{1,6},{2,5},{3,4},{4,3},{5,2},{6,1},{7,0},{8,15},{9,14},{10,... | collective-permute-start | bytes 12296 | tf_op jit(solution)/shard_map/ppermute | solution.py:508
  23.2 0.5 collective-permute-start.8
  23.7 1.3 %collective-permute-start.9 = (f32[4,256]{1,0:T(4,128)S(1)}, f32[4,256]{1,0:T(4,128)S(1)}, u32[]{:S(2)}, u32[]{:S(2)}) collective-permute-start(f32[4,256]{1,0:T(4,128)S(1)} %add.24), channel_id=1, source_target_pairs={{0,3},{1,2},{2,1},{3,0},{4,7},{5,6},{6,5},{7,4},{8,11},{9,10},{10,... | collective-permute-start | bytes 12296 | tf_op jit(solution)/shard_map/ppermute | solution.py:508
  24.9 0.4 collective-permute-start.5
  25.4 0.5 collective-permute-done.7
  25.9 0.4 collective-permute-done.8
  26.2 0.4 collective-permute-done.9
  26.7 2.0 %shard_map.68.after = f32[4,256]{1,0:T(4,128)S(1)} custom-call(bf16[768,256]{1,0:T(8,128)(2,1)S(1)} %shard_map.67.after.zs_ref.refs_6_.refs_5_, f32[4,256]{1,0:T(4,128)S(1)} %add_add_fusion.1.x_ref, bf16[8,256,512]{2,1,0:T(8,128)(2,1)S(1)} %get-tuple-element.42.refs_4_.own_ref.refs_1_.refs_2_, bf16[8,768,512]{2,1,0:T(8,128)(2,1)S(1)} %get-tuple-element.46.e_ref.refs_2_.refs_3_), custom_call_target="tpu_custom_call" | custom-call | flops 16777216 | bytes 8388608 | tf_op jit(solution)/shard_map/pallas_call | solution.py:549
  28.7 0.2 collective-permute-start.10
  29.0 0.7 %shard_map.69 = (f32[3,256]{1,0:T(4,128)S(1)}, bf16[2,768,512]{2,1,0:T(8,128)(2,1)S(1)}) custom-call(f32[4,256]{1,0:T(4,128)S(1)} %shard_map.68.after, bf16[768,256]{1,0:T(8,128)(2,1)S(1)} %shard_map.67.after.zs_ref.refs_6_.refs_5_, bf16[8,256,512]{2,1,0:T(8,128)(2,1)S(1)} %get-tuple-element.37.ws_ref), custom_call_target="tpu_custom_call" | custom-call | flops 402653184 | bytes 1572864 | tf_op jit(solution)/shard_map/pallas_call | solution.py:549
  29.7 0.3 collective-permute-done.10
  30.0 2.2 %collective-permute-start.11 = (f32[4,256]{1,0:T(4,128)S(1)}, f32[4,256]{1,0:T(4,128)S(1)}, u32[]{:S(2)}, u32[]{:S(2)}) collective-permute-start(f32[4,256]{1,0:T(4,128)S(1)} %add.28.after), channel_id=1, source_target_pairs={{0,7},{1,6},{2,5},{3,4},{4,3},{5,2},{6,1},{7,0},{8,15},{9,14},{10,... | collective-permute-start | bytes 12296 | tf_op jit(solution)/shard_map/ppermute | solution.py:508
  32.2 0.5 collective-permute-start.12
  32.6 0.3 collective-permute-start.13
  33.0 1.7 %shard_map.70 = (f32[3,256]{1,0:T(4,128)S(1)}, bf16[6,768,512]{2,1,0:T(8,128)(2,1)S(1)}) custom-call(f32[4,256]{1,0:T(4,128)S(1)} %add.28.after, bf16[768,256]{1,0:T(8,128)(2,1)S(1)} %shard_map.67.after.zs_ref.refs_6_.refs_5_, bf16[8,256,512]{2,1,0:T(8,128)(2,1)S(1)} %get-tuple-element.37.ws_ref), custom_call_target="tpu_custom_call" | custom-call | flops 1207959552 | bytes 4718592 | tf_op jit(solution)/shard_map/pallas_call | solution.py:549
  34.7 0.5 %collective-permute-done.12 = f32[4,256]{1,0:T(4,128)S(1)} collective-permute-done((f32[4,256]{1,0:T(4,128)S(1)}, f32[4,256]{1,0:T(4,128)S(1)}, u32[]{:S(2)}, u32[]{:S(2)}) %collective-permute-start.12) | collective-permute-done | bytes 4128 | tf_op jit(solution)/shard_map/ppermute | solution.py:508
  35.2 0.5 collective-permute-done.13
  35.7 2.5 %shard_map.71 = (f32[8,1,512]{2,1,0:T(1,128)S(1)}, f32[272,256]{1,0:T(8,128)S(1)}, bf16[272,256]{1,0:T(8,128)(2,1)S(1)}) custom-call(f32[4,256]{1,0:T(4,128)S(1)} %add_add_fusion.x_ref, bf16[8,256,512]{2,1,0:T(8,128)(2,1)S(1)} %get-tuple-element.42.refs_4_.own_ref.refs_1_.refs_2_, bf16[8,768,512]{2,1,0:T(8,128)(2,1)S(1)} %get-tuple-element.46.e_ref.refs_2_.refs_3_, ...), custom_call_target="tpu_custom_call" | custom-call | flops 16777216 | bytes 8388608 | tf_op jit(solution)/shard_map/pallas_call | solution.py:549
  38.2 0.2 collective-permute-start.14
  38.4 1.2 %collective-permute-done.14.refs_1_ = bf16[272,256]{1,0:T(8,128)(2,1)S(1)} collective-permute-done((bf16[272,256]{1,0:T(8,128)(2,1)S(1)}, bf16[272,256]{1,0:T(8,128)(2,1)S(1)}, u32[]{:S(2)}, u32[]{:S(2)}) %collective-permute-start.14) | collective-permute-done | bytes 139296 | tf_op jit(solution)/shard_map/ppermute | solution.py:508
  39.7 1.5 %collective-permute-start.15 = (bf16[80,256]{1,0:T(8,128)(2,1)S(1)}, bf16[80,256]{1,0:T(8,128)(2,1)S(1)}, u32[]{:S(2)}, u32[]{:S(2)}) collective-permute-start(bf16[80,256]{1,0:T(8,128)(2,1)S(1)} %get-tuple-element.53), channel_id=1, source_target_pairs={{0,7},{1,6},{2,5},{3,4},{4,3},{5,2},{6,1},{7,0},{8,15},{9,14},{10,... | collective-permute-start | bytes 122888 | tf_op jit(solution)/shard_map/ppermute | solution.py:508
  41.1 0.3 collective-permute-start.16
  41.5 1.3 %collective-permute-start.17 = (bf16[80,256]{1,0:T(8,128)(2,1)S(1)}, bf16[80,256]{1,0:T(8,128)(2,1)S(1)}, u32[]{:S(2)}, u32[]{:S(2)}) collective-permute-start(bf16[80,256]{1,0:T(8,128)(2,1)S(1)} %get-tuple-element.55), channel_id=1, source_target_pairs={{0,3},{1,2},{2,1},{3,0},{4,7},{5,6},{6,5},{7,4},{8,11},{9,10},{10,... | collective-permute-start | bytes 122888 | tf_op jit(solution)/shard_map/ppermute | solution.py:508
  42.7 1.5 %collective-permute-done.15.refs_1_ = bf16[80,256]{1,0:T(8,128)(2,1)S(1)} collective-permute-done((bf16[80,256]{1,0:T(8,128)(2,1)S(1)}, bf16[80,256]{1,0:T(8,128)(2,1)S(1)}, u32[]{:S(2)}, u32[]{:S(2)}) %collective-permute-start.15) | collective-permute-done | bytes 40992 | tf_op jit(solution)/shard_map/ppermute | solution.py:508
  44.2 1.1 %collective-permute-done.16.refs_2_ = bf16[80,256]{1,0:T(8,128)(2,1)S(1)} collective-permute-done((bf16[80,256]{1,0:T(8,128)(2,1)S(1)}, bf16[80,256]{1,0:T(8,128)(2,1)S(1)}, u32[]{:S(2)}, u32[]{:S(2)}) %collective-permute-start.16) | collective-permute-done | bytes 40992 | tf_op jit(solution)/shard_map/ppermute | solution.py:508
  45.3 0.4 shard_map.73
  45.7 0.2 collective-permute-start.18
  45.9 1.2 %shard_map.74 = (bf16[64,4096]{1,0:T(8,128)(2,1)}, f32[8,128]{1,0:T(8,128)S(1)}) custom-call(bf16[32,256]{1,0:T(8,128)(2,1)S(1)} %get-tuple-element.57.refs_0_.share, bf16[8,256,512]{2,1,0:T(8,128)(2,1)S(1)} %get-tuple-element.42.refs_4_.own_ref.refs_1_.refs_2_, bf16[8,768,512]{2,1,0:T(8,128)(2,1)S(1)} %get-tuple-element.46.e_ref.refs_2_.refs_3_, ...), custom_call_target="tpu_custom_call" | custom-call | flops 134217728 | bytes 4194304 | tf_op jit(solution)/shard_map/pallas_call | solution.py:565
  47.2 2.2 %collective-permute-start.19 = (bf16[64,256]{1,0:T(8,128)(2,1)S(1)}, bf16[64,256]{1,0:T(8,128)(2,1)S(1)}, u32[]{:S(2)}, u32[]{:S(2)}) collective-permute-start(bf16[64,256]{1,0:T(8,128)(2,1)S(1)} %shard_map.75.refs_1_.share), channel_id=1, source_target_pairs={{0,7},{1,6},{2,5},{3,4},{4,3},{5,2},{6,1},{7,0},{8,15},{9,14},{10,... | collective-permute-start | bytes 98312 | tf_op jit(solution)/shard_map/ppermute | solution.py:508
  49.4 0.3 collective-permute-start.20
  49.7 0.8 %collective-permute-start.21 = (bf16[64,256]{1,0:T(8,128)(2,1)S(1)}, bf16[64,256]{1,0:T(8,128)(2,1)S(1)}, u32[]{:S(2)}, u32[]{:S(2)}) collective-permute-start(bf16[64,256]{1,0:T(8,128)(2,1)S(1)} %shard_map.75.refs_1_.share), channel_id=1, source_target_pairs={{0,3},{1,2},{2,1},{3,0},{4,7},{5,6},{6,5},{7,4},{8,11},{9,10},{10,... | collective-permute-start | bytes 98312 | tf_op jit(solution)/shard_map/ppermute | solution.py:508
  50.5 2.1 %shard_map.76 = (bf16[64,4096]{1,0:T(8,128)(2,1)}, f32[8,128]{1,0:T(8,128)S(1)}) custom-call(bf16[64,4096]{1,0:T(8,128)(2,1)} %get-tuple-element.64.refs_0_, bf16[64,256]{1,0:T(8,128)(2,1)S(1)} %shard_map.75.refs_1_.share, bf16[8,256,512]{2,1,0:T(8,128)(2,1)S(1)} %get-tuple-element.42.refs_4_.own_ref.refs_1_.refs_2_, ...), custom_call_target="tpu_custom_call", output_to_operand_aliasing={{0}: (0, {})} | custom-call | flops 402653184 | bytes 12582912 | tf_op jit(solution)/shard_map/pallas_call | solution.py:565
  52.6 0.2 collective-permute-done.20.refs_1_
  52.8 0.3 collective-permute-done.21.refs_2_
  53.0 0.7 %shard_map.77 = bf16[256,256]{1,0:T(8,128)(2,1)} custom-call(f32[8,128]{1,0:T(8,128)S(1)} %get-tuple-element.67.after, bf16[64,256]{1,0:T(8,128)(2,1)S(1)} %shard_map.75.refs_1_.share, bf16[64,256]{1,0:T(8,128)(2,1)S(1)} %collective-permute-done.19.refs_0_, bf16[64,256]{1,0:T(8,128)(2,1)S(1)} %collective-permute-done.20.refs_1_, ...), custom_call_target="tpu_custom_call" | custom-call | bytes 131072 | tf_op jit(solution)/shard_map/pallas_call | solution.py:549
  (23 shorter events, 0.4 us)
Async XLA Ops:
  1.5 9.1 %copy-start.1 = (bf16[256,256]{1,0:T(8,128)(2,1)S(1)}, bf16[256,256]{1,0:T(8,128)(2,1)}, u32[]{:S(2)}) copy-start(bf16[256,256]{1,0:T(8,128)(2,1)} %teacher_ref.1) | copy-start | bytes 393220
  1.5 11.5 %collective-permute-start = (bf16[192,256]{1,0:T(8,128)(2,1)S(1)}, bf16[192,256]{1,0:T(8,128)(2,1)S(1)}, u32[]{:S(2)}, u32[]{:S(2)}) collective-permute-start(bf16[192,256]{1,0:T(8,128)(2,1)S(1)} %shard_map.62), channel_id=1, source_target_pairs={{0,24},{8,16},{16,8},{24,0},{1,25},{9,17},{17,9},{25,1},{2,26},{10... | collective-permute-start | bytes 294920 | tf_op jit(solution)/shard_map/ppermute | solution.py:508
  6.6 8.3 %collective-permute-start.1 = (bf16[192,256]{1,0:T(8,128)(2,1)S(1)}, bf16[192,256]{1,0:T(8,128)(2,1)S(1)}, u32[]{:S(2)}, u32[]{:S(2)}) collective-permute-start(bf16[192,256]{1,0:T(8,128)(2,1)S(1)} %shard_map.62), channel_id=1, source_target_pairs={{0,16},{8,24},{16,0},{24,8},{1,17},{9,25},{17,1},{25,9},{2,18},{10... | collective-permute-start | bytes 294920 | tf_op jit(solution)/shard_map/ppermute | solution.py:508
  6.6 8.3 %collective-permute-start.2 = (bf16[192,256]{1,0:T(8,128)(2,1)S(1)}, bf16[192,256]{1,0:T(8,128)(2,1)S(1)}, u32[]{:S(2)}, u32[]{:S(2)}) collective-permute-start(bf16[192,256]{1,0:T(8,128)(2,1)S(1)} %shard_map.62), channel_id=1, source_target_pairs={{0,8},{8,0},{16,24},{24,16},{1,9},{9,1},{17,25},{25,17},{2,10},{10... | collective-permute-start | bytes 294920 | tf_op jit(solution)/shard_map/ppermute | solution.py:508
  10.6 0.9 %copy-start = (bf16[256,256]{1,0:T(8,128)(2,1)S(1)}, bf16[256,256]{1,0:T(8,128)(2,1)}, u32[]{:S(2)}) copy-start(bf16[256,256]{1,0:T(8,128)(2,1)} %refs_4_.1) | copy-start | bytes 393220
  15.1 2.6 %collective-permute-start.3 = (bf16[384,256]{1,0:T(8,128)(2,1)S(1)}, bf16[384,256]{1,0:T(8,128)(2,1)S(1)}, u32[]{:S(2)}, u32[]{:S(2)}) collective-permute-start(bf16[384,256]{1,0:T(8,128)(2,1)S(1)} %get-tuple-element.40.mine.refs_1_), channel_id=1, source_target_pairs={{0,1},{1,0},{2,3},{3,2},{4,5},{5,4},{6,7},{7,6},{8,9},{9,8},{10,11... | collective-permute-start | bytes 589832 | tf_op jit(solution)/shard_map/ppermute | solution.py:508
  15.2 9.7 %collective-permute-start.4 = (bf16[192,256]{1,0:T(8,128)(2,1)S(1)}, bf16[192,256]{1,0:T(8,128)(2,1)S(1)}, u32[]{:S(2)}, u32[]{:S(2)}) collective-permute-start(bf16[192,256]{1,0:T(8,128)(2,1)S(1)} %get-tuple-element.45.mine), channel_id=1, source_target_pairs={{0,2},{1,3},{2,0},{3,1},{4,6},{5,7},{6,4},{7,5},{8,10},{9,11},{10,... | collective-permute-start | bytes 294920 | tf_op jit(solution)/shard_map/ppermute | solution.py:508
  20.7 1.2 %collective-permute-start.6 = (f32[4,256]{1,0:T(4,128)S(1)}, f32[4,256]{1,0:T(4,128)S(1)}, u32[]{:S(2)}, u32[]{:S(2)}) collective-permute-start(f32[4,256]{1,0:T(4,128)S(1)} %get-tuple-element.44.after), channel_id=1, source_target_pairs={{0,1},{1,0},{2,3},{3,2},{4,5},{5,4},{6,7},{7,6},{8,9},{9,8},{10,11... | collective-permute-start | bytes 12296 | tf_op jit(solution)/shard_map/ppermute | solution.py:508
  21.9 3.9 %collective-permute-start.7 = (f32[4,256]{1,0:T(4,128)S(1)}, f32[4,256]{1,0:T(4,128)S(1)}, u32[]{:S(2)}, u32[]{:S(2)}) collective-permute-start(f32[4,256]{1,0:T(4,128)S(1)} %add.24), channel_id=1, source_target_pairs={{0,7},{1,6},{2,5},{3,4},{4,3},{5,2},{6,1},{7,0},{8,15},{9,14},{10,... | collective-permute-start | bytes 12296 | tf_op jit(solution)/shard_map/ppermute | solution.py:508
  23.2 3.1 %collective-permute-start.8 = (f32[4,256]{1,0:T(4,128)S(1)}, f32[4,256]{1,0:T(4,128)S(1)}, u32[]{:S(2)}, u32[]{:S(2)}) collective-permute-start(f32[4,256]{1,0:T(4,128)S(1)} %add.24), channel_id=1, source_target_pairs={{0,5},{1,4},{2,7},{3,6},{4,1},{5,0},{6,3},{7,2},{8,13},{9,12},{10,... | collective-permute-start | bytes 12296 | tf_op jit(solution)/shard_map/ppermute | solution.py:508
  23.7 3.0 %collective-permute-start.9 = (f32[4,256]{1,0:T(4,128)S(1)}, f32[4,256]{1,0:T(4,128)S(1)}, u32[]{:S(2)}, u32[]{:S(2)}) collective-permute-start(f32[4,256]{1,0:T(4,128)S(1)} %add.24), channel_id=1, source_target_pairs={{0,3},{1,2},{2,1},{3,0},{4,7},{5,6},{6,5},{7,4},{8,11},{9,10},{10,... | collective-permute-start | bytes 12296 | tf_op jit(solution)/shard_map/ppermute | solution.py:508
  24.9 1.7 %collective-permute-start.5 = (bf16[384,256]{1,0:T(8,128)(2,1)S(1)}, bf16[384,256]{1,0:T(8,128)(2,1)S(1)}, u32[]{:S(2)}, u32[]{:S(2)}) collective-permute-start(bf16[384,256]{1,0:T(8,128)(2,1)S(1)} %shard_map.66.mine), channel_id=1, source_target_pairs={{0,1},{1,0},{2,3},{3,2},{4,5},{5,4},{6,7},{7,6},{8,9},{9,8},{10,11... | collective-permute-start | bytes 589832 | tf_op jit(solution)/shard_map/ppermute | solution.py:508
  28.7 1.2 %collective-permute-start.10 = (f32[4,256]{1,0:T(4,128)S(1)}, f32[4,256]{1,0:T(4,128)S(1)}, u32[]{:S(2)}, u32[]{:S(2)}) collective-permute-start(f32[4,256]{1,0:T(4,128)S(1)} %shard_map.68.after), channel_id=1, source_target_pairs={{0,1},{1,0},{2,3},{3,2},{4,5},{5,4},{6,7},{7,6},{8,9},{9,8},{10,11... | collective-permute-start | bytes 12296 | tf_op jit(solution)/shard_map/ppermute | solution.py:508
  30.0 4.7 %collective-permute-start.11 = (f32[4,256]{1,0:T(4,128)S(1)}, f32[4,256]{1,0:T(4,128)S(1)}, u32[]{:S(2)}, u32[]{:S(2)}) collective-permute-start(f32[4,256]{1,0:T(4,128)S(1)} %add.28.after), channel_id=1, source_target_pairs={{0,7},{1,6},{2,5},{3,4},{4,3},{5,2},{6,1},{7,0},{8,15},{9,14},{10,... | collective-permute-start | bytes 12296 | tf_op jit(solution)/shard_map/ppermute | solution.py:508
  32.2 3.0 %collective-permute-start.12 = (f32[4,256]{1,0:T(4,128)S(1)}, f32[4,256]{1,0:T(4,128)S(1)}, u32[]{:S(2)}, u32[]{:S(2)}) collective-permute-start(f32[4,256]{1,0:T(4,128)S(1)} %add.28.after), channel_id=1, source_target_pairs={{0,5},{1,4},{2,7},{3,6},{4,1},{5,0},{6,3},{7,2},{8,13},{9,12},{10,... | collective-permute-start | bytes 12296 | tf_op jit(solution)/shard_map/ppermute | solution.py:508
  32.6 3.0 %collective-permute-start.13 = (f32[4,256]{1,0:T(4,128)S(1)}, f32[4,256]{1,0:T(4,128)S(1)}, u32[]{:S(2)}, u32[]{:S(2)}) collective-permute-start(f32[4,256]{1,0:T(4,128)S(1)} %add.28.after), channel_id=1, source_target_pairs={{0,3},{1,2},{2,1},{3,0},{4,7},{5,6},{6,5},{7,4},{8,11},{9,10},{10,... | collective-permute-start | bytes 12296 | tf_op jit(solution)/shard_map/ppermute | solution.py:508
  38.2 1.4 %collective-permute-start.14 = (bf16[272,256]{1,0:T(8,128)(2,1)S(1)}, bf16[272,256]{1,0:T(8,128)(2,1)S(1)}, u32[]{:S(2)}, u32[]{:S(2)}) collective-permute-start(bf16[272,256]{1,0:T(8,128)(2,1)S(1)} %get-tuple-element.51), channel_id=1, source_target_pairs={{0,1},{1,0},{2,3},{3,2},{4,5},{5,4},{6,7},{7,6},{8,9},{9,8},{10,11... | collective-permute-start | bytes 417800 | tf_op jit(solution)/shard_map/ppermute | solution.py:508
  39.7 4.6 %collective-permute-start.15 = (bf16[80,256]{1,0:T(8,128)(2,1)S(1)}, bf16[80,256]{1,0:T(8,128)(2,1)S(1)}, u32[]{:S(2)}, u32[]{:S(2)}) collective-permute-start(bf16[80,256]{1,0:T(8,128)(2,1)S(1)} %get-tuple-element.53), channel_id=1, source_target_pairs={{0,7},{1,6},{2,5},{3,4},{4,3},{5,2},{6,1},{7,0},{8,15},{9,14},{10,... | collective-permute-start | bytes 122888 | tf_op jit(solution)/shard_map/ppermute | solution.py:508
  41.1 4.2 %collective-permute-start.16 = (bf16[80,256]{1,0:T(8,128)(2,1)S(1)}, bf16[80,256]{1,0:T(8,128)(2,1)S(1)}, u32[]{:S(2)}, u32[]{:S(2)}) collective-permute-start(bf16[80,256]{1,0:T(8,128)(2,1)S(1)} %get-tuple-element.54), channel_id=1, source_target_pairs={{0,5},{1,4},{2,7},{3,6},{4,1},{5,0},{6,3},{7,2},{8,13},{9,12},{10,... | collective-permute-start | bytes 122888 | tf_op jit(solution)/shard_map/ppermute | solution.py:508
  41.5 3.9 %collective-permute-start.17 = (bf16[80,256]{1,0:T(8,128)(2,1)S(1)}, bf16[80,256]{1,0:T(8,128)(2,1)S(1)}, u32[]{:S(2)}, u32[]{:S(2)}) collective-permute-start(bf16[80,256]{1,0:T(8,128)(2,1)S(1)} %get-tuple-element.55), channel_id=1, source_target_pairs={{0,3},{1,2},{2,1},{3,0},{4,7},{5,6},{6,5},{7,4},{8,11},{9,10},{10,... | collective-permute-start | bytes 122888 | tf_op jit(solution)/shard_map/ppermute | solution.py:508
  45.7 1.4 %collective-permute-start.18 = (bf16[32,256]{1,0:T(8,128)(2,1)S(1)}, bf16[32,256]{1,0:T(8,128)(2,1)S(1)}, u32[]{:S(2)}, u32[]{:S(2)}) collective-permute-start(bf16[32,256]{1,0:T(8,128)(2,1)S(1)} %get-tuple-element.57.refs_0_.share), channel_id=1, source_target_pairs={{0,1},{1,0},{2,3},{3,2},{4,5},{5,4},{6,7},{7,6},{8,9},{9,8},{10,11... | collective-permute-start | bytes 49160 | tf_op jit(solution)/shard_map/ppermute | solution.py:508
  47.2 5.4 %collective-permute-start.19 = (bf16[64,256]{1,0:T(8,128)(2,1)S(1)}, bf16[64,256]{1,0:T(8,128)(2,1)S(1)}, u32[]{:S(2)}, u32[]{:S(2)}) collective-permute-start(bf16[64,256]{1,0:T(8,128)(2,1)S(1)} %shard_map.75.refs_1_.share), channel_id=1, source_target_pairs={{0,7},{1,6},{2,5},{3,4},{4,3},{5,2},{6,1},{7,0},{8,15},{9,14},{10,... | collective-permute-start | bytes 98312 | tf_op jit(solution)/shard_map/ppermute | solution.py:508
  49.4 3.4 %collective-permute-start.20 = (bf16[64,256]{1,0:T(8,128)(2,1)S(1)}, bf16[64,256]{1,0:T(8,128)(2,1)S(1)}, u32[]{:S(2)}, u32[]{:S(2)}) collective-permute-start(bf16[64,256]{1,0:T(8,128)(2,1)S(1)} %shard_map.75.refs_1_.share), channel_id=1, source_target_pairs={{0,5},{1,4},{2,7},{3,6},{4,1},{5,0},{6,3},{7,2},{8,13},{9,12},{10,... | collective-permute-start | bytes 98312 | tf_op jit(solution)/shard_map/ppermute | solution.py:508
  49.7 3.4 %collective-permute-start.21 = (bf16[64,256]{1,0:T(8,128)(2,1)S(1)}, bf16[64,256]{1,0:T(8,128)(2,1)S(1)}, u32[]{:S(2)}, u32[]{:S(2)}) collective-permute-start(bf16[64,256]{1,0:T(8,128)(2,1)S(1)} %shard_map.75.refs_1_.share), channel_id=1, source_target_pairs={{0,3},{1,2},{2,1},{3,0},{4,7},{5,6},{6,5},{7,4},{8,11},{9,10},{10,... | collective-permute-start | bytes 98312 | tf_op jit(solution)/shard_map/ppermute | solution.py:508

commit v2 on v1

--- a/solution.py
+++ b/solution.py
@@ -69,12 +69,23 @@
         body(i)
 
 
+def in_turn(left, right):
+    done = 0
+    for k, run in enumerate(left):
+        run()
+        while done * len(left) < (k + 1) * len(right):
+            right[done]()
+            done += 1
+
+
 def two_steps(steps, first, second):
-    carry = first(0)
+    runs, result = first(0)
+    in_turn(runs, [])
     for i in range(1, steps):
-        second(i - 1, carry)
-        carry = first(i)
-    second(steps - 1, carry)
+        carry = result()
+        runs, result = first(i)
+        in_turn(second(i - 1, carry), runs)
+    in_turn(second(steps - 1, result()), [])
 
 
 def lane_groups(values):
@@ -147,7 +158,7 @@
 
 
 def units_kernel(after, also, *refs):
-    blocks, outs = refs[-3::-1], refs[-2:]
+    blocks, outs = refs[:-2], refs[-2:]
     start = 0
     for out in outs:
         size = out.shape[0] // len(blocks)
@@ -205,19 +216,25 @@
     own, rest = refs
     ps = ps.astype(BF)
 
-    def across(ref, start):
+    def add(ref, at, to):
+        scaled = ref[i, at, :] * ps
+        half = scaled[:, : BLK // 2] + scaled[:, BLK // 2 :]
+        acc[to, :] += lane_groups(half.astype(F32))
+
+    def many():
         def step(span, carry):
             for at in chunks(span):
-                to = pl.ds(at.start + start, at.size)
-                scaled = ref[i, at, :] * ps
-                half = scaled[:, : BLK // 2] + scaled[:, BLK // 2 :]
-                acc[to, :] += lane_groups(half.astype(F32))
+                add(rest, at, pl.ds(at.start + rows, at.size))
             return carry
 
-        return step
-
-    over(1, rows, across(own, 0), 0)
-    over(*blocks_of(rest.shape[1]), across(rest, rows), 0)
+        over(*blocks_of(rest.shape[1]), step, 0)
+
+    runs = [functools.partial(add, own, at, at) for at in chunks(pl.ds(0, rows))]
+    if rest.shape[1] > 1024:
+        return runs + [many]
+    for at in chunks(pl.ds(0, rest.shape[1])):
+        runs.append(functools.partial(add, rest, at, pl.ds(at.start + rows, at.size)))
+    return runs
 
 
 def own_first_kernel(own, wt_ref, e_ref, cols_ref, zt):
@@ -231,42 +248,59 @@
     each_step(0, wt_ref.shape[0], body)
 
 
-def exps_of(side, units, i, wt_ref, e_ref, cols):
+def exps_of(side, units, i, wt_ref, e_ref, cell):
     far = units.shape[0]
     height = 384 if far % 384 == 0 else 128
-
-    def down(span, total):
-        logits = dot(units[span, :], wt_ref[i])
+    logits = [None]
+
+    def multiply(span):
+        logits[0] = dot(units[span, :], wt_ref[i])
+
+    def put(k, start):
+        e = jnp.exp2(logits[0][k * 64 : (k + 1) * 64, :])
+        e_ref[i, pl.ds(pl.multiple_of(side * far + start, 64), 64), :] = e.astype(BF)
+        cell[0] = cell[0] + sublane_groups(e)
+
+    def step(span, total):
+        cell[0] = total
+        multiply(span)
         for k, at in enumerate(chunks(span)):
-            e = jnp.exp2(logits[k * 64 : (k + 1) * 64, :])
-            to = pl.ds(pl.multiple_of(side * far + at.start, 64), 64)
-            e_ref[i, to, :] = e.astype(BF)
-            total = total + sublane_groups(e)
-        return total
-
-    return over(far // height, height, down, cols)
+            put(k, at.start)
+        return cell[0]
+
+    def many():
+        cell[0] = over(far // height, height, step, cell[0])
+
+    if far > height:
+        return [many]
+    runs = [functools.partial(multiply, pl.ds(0, far))]
+    return runs + [functools.partial(put, k, k * 64) for k in range(far // 64)]
 
 
 def mine_first_kernel(mine, wt_ref, own_cols, e_ref, cols_ref):
     side = lax.axis_index("proto") % 2
 
     def body(i):
-        cols_ref[i] = exps_of(side, mine, i, wt_ref, e_ref, own_cols[i])
+        cell = [own_cols[i]]
+        in_turn(exps_of(side, mine, i, wt_ref, e_ref, cell), [])
+        cols_ref[i] = cell[0]
 
     each_step(0, wt_ref.shape[0], body)
 
 
 def first_kernel(nb, begun, *refs):
-    mine, other, wt_ref, own_ref, cols_ref, e_ref, out_ref, acc = refs[begun:]
+    mine, other, wt_ref, own_ref, cols_ref, quarters, e_ref, out_ref, passed, acc = refs[begun:]
+    passed[...] = quarters[...]
     rows = own_ref.shape[1]
     side = lax.axis_index("proto") % 2
     acc[...] = jnp.zeros_like(acc)
 
     def exps(i):
-        total = exps_of(1 - side, other, i, wt_ref, e_ref, cols_ref[i])
+        cell = [cols_ref[i]]
+        runs = exps_of(1 - side, other, i, wt_ref, e_ref, cell)
         if not begun:
-            total = exps_of(side, mine, i, wt_ref, e_ref, total)
-        return 1.0 / jnp.sum(total, axis=0, keepdims=True)
+            runs = runs + exps_of(side, mine, i, wt_ref, e_ref, cell)
+        return runs, lambda: 1.0 / jnp.sum(cell[0], axis=0, keepdims=True)
 
     refs = (own_ref, e_ref)
     two_steps(wt_ref.shape[0], exps, lambda i, ps: add_across(rows, refs, i, ps, acc))
@@ -289,15 +323,25 @@
 def proto_scale(refs, i, cs, turned):
     own, rest = refs
     rows = own.shape[1]
-    total = jnp.zeros((8, BLK), F32)
+    cell, down = [jnp.zeros((8, BLK), F32)], [None]
+
+    def multiply():
+        down[0] = dot(cs[:, 2 * rows :], rest[i, rows:, :])
+
+    def add(ref, start, at):
+        scale = turned[start + at.start : start + at.start + 64, :]
+        scaled = ref[i, at, :] * jnp.concatenate([scale] * (BLK // LANES), axis=1)
+        cell[0] = cell[0] + sublane_groups((scaled[:32] + scaled[32:]).astype(F32))
+
+    runs = [multiply]
     for ref, start in ((own, 0), (rest, rows)):
-        for at in chunks(pl.ds(0, rows)):
-            scale = turned[start + at.start : start + at.start + 64, :]
-            scaled = ref[i, at, :] * jnp.concatenate([scale] * (BLK // LANES), axis=1)
-            total = total + sublane_groups((scaled[:32] + scaled[32:]).astype(F32))
-    down = dot(cs[:, 2 * rows :], rest[i, rows:, :])
-    total = jnp.sum(total, axis=0, keepdims=True) + jnp.sum(down, axis=0, keepdims=True)
-    return 1.0 / total
+        runs += [functools.partial(add, ref, start, at) for at in chunks(pl.ds(0, rows))]
+
+    def result():
+        total = jnp.sum(cell[0], axis=0, keepdims=True) + jnp.sum(down[0], axis=0, keepdims=True)
+        return 1.0 / total
+
+    return runs, result
 
 
 def sweep_kernel(nb, after, x_ref, own_ref, e_ref, out_ref, cs, turned, acc):
@@ -322,9 +366,11 @@
     grad[...] = jnp.zeros_like(grad)
 
     def across(i, ps):
-        ps_ref[i] = ps
-        add_across(rows, both, i, ps, acc)
-        grad[...] += dot(own_ref[i] * ps.astype(BF), ws_rows[i])
+        def add_grad():
+            ps_ref[i] = ps
+            grad[...] += dot(own_ref[i] * ps.astype(BF), ws_rows[i])
+
+        return [add_grad] + add_across(rows, both, i, ps, acc)
 
     two_steps(e_ref.shape[0], lambda i: proto_scale(both, i, cs, turned), across)
     head[...] = jnp.zeros_like(head)
@@ -498,7 +544,7 @@
     moved, out_ref = refs[:-1], refs[-1]
     rows = share.shape[0]
     me = lax.axis_index("proto") ^ 1
-    for hop, ref in zip((0, *hops[::-1]), (share, *moved)):
+    for hop, ref in zip((0, *hops), (share, *moved)):
         place = ((me ^ hop) // hops[0]) % (1 + len(hops))
         out_ref[pl.ds(pl.multiple_of(place * rows, rows), rows), :] = ref[...].astype(out_ref.dtype)
 
@@ -636,11 +682,10 @@
         8 * crops * width,
         2 * crops * width,
         0,
-        *reversed(blocks),
+        *blocks,
         after=(own_cols, own_tot),
     )
     other = permute(mine, "proto", 1)
-    moved = permute(quarters, "proto", 2)
 
     begun, cols = (), own_cols
     if keep:
@@ -655,9 +700,13 @@
             unit_wt,
             own_cols,
         )
-    e, x = call(
+    e, x, quarters = call(
         functools.partial(first_kernel, nb, len(begun)),
-        [shape(steps, rest, BLK, dtype=BF), shape(nb, width)],
+        [
+            shape(steps, rest, BLK, dtype=BF),
+            shape(nb, width),
+            shape(rest // 4, width, dtype=BF),
+        ],
         [lane_sums],
         2 * big * width,
         2 * big,
@@ -668,6 +717,7 @@
         unit_wt,
         own_e,
         cols,
+        quarters,
         aliases={0: 0} if begun else {},
     )
     (student_mine,) = call(
@@ -678,7 +728,7 @@
         2 * rest * width,
         0,
         quarters,
-        moved,
+        permute(quarters, "proto", 2),
         after=(x,),
     )
     (zs,) = call(
@@ -715,7 +765,7 @@
             moved = permutes(x, "proto", [crossed(hop) for hop in hops])
             if k in pieces:
                 student_piece(x)
-            for value in reversed(moved):
+            for value in moved:
                 x = x + value
         return x
 
@@ -835,7 +885,7 @@
             8 * share.shape[0] * width,
             0,
             share,
-            *reversed(moved),
+            *moved,
             after=(token,),
         )
     return (done[0], share)

time: 53.9 us -> 53.9 us (level)
  waiting for transfers between devices: 9.76 us -> 10.4 us
    ppermute x22, waiting for transfers between devices: 9.76 us -> 10.4 us  [permute(): return lax.ppermute(value, axis, [(i, i ^ s) for i in range(n)])]
  transfers between devices with their start and end apart: 22 -> 22, of which waited for: 13 -> 14; matrix products, arithmetic and copies ran while one was open for 0% -> 0% of each run, Pallas kernels for 28% -> 23%
where the time goes in v2:
time: 53.9 us; the launch traced here: 53.7 us
  Pallas kernels  21.7 us (40%)
  starting transfers between devices  20.7 us (38%)
  waiting for transfers between devices  10.4 us (19%)
  between operations  0.81 us (2%)
    ppermute x22, starting transfers between devices, permute(): return lax.ppermute(value, axis, [(i, i ^ s) for i in range(n)])  20.7 us
    pallas_call x17, Pallas kernels, call(): pl.pallas_call(kernel, out_shape=out_shape, in_specs=[hbm] * len(far) + [...  18.4 us
    ppermute x22, waiting for transfers between devices, permute(): return lax.ppermute(value, axis, [(i, i ^ s) for i in range(n)])  10.4 us
    pallas_call x2, Pallas kernels, weight_call(): pl.pallas_call(kernel, out_shape=[out_shape, shape(8, LANES)], in_specs=[...  3.31 us
  transfers between devices with their start and end apart: 22, of which 14 were waited for; matrix products, arithmetic and copies ran while one was open for 0% of the time, Pallas kernels for 23%

profile of v2, /device:TPU:0, one launch (start us, length us, event | category | flops | bytes accessed | tf_op | source)
XLA Modules:
  0.0 53.7 jit_solution(18429148503458378361)
XLA Ops:
  0.6 0.9 %shard_map.62 = bf16[192,256]{1,0:T(8,128)(2,1)S(1)} custom-call(bf16[256,256]{1,0:T(8,128)(2,1)} %teacher_ref.1, bf16[256,256]{1,0:T(8,128)(2,1)} %refs_4_.1), custom_call_target="tpu_custom_call" | custom-call | bytes 262144 | tf_op jit(solution)/shard_map/pallas_call | solution.py:595
  1.5 5.1 %collective-permute-start.2 = (bf16[192,256]{1,0:T(8,128)(2,1)S(1)}, bf16[192,256]{1,0:T(8,128)(2,1)S(1)}, u32[]{:S(2)}, u32[]{:S(2)}) collective-permute-start(bf16[192,256]{1,0:T(8,128)(2,1)S(1)} %shard_map.62), channel_id=1, source_target_pairs={{0,24},{8,16},{16,8},{24,0},{1,25},{9,17},{17,9},{25,1},{2,26},{10... | collective-permute-start | bytes 294920 | tf_op jit(solution)/shard_map/ppermute | solution.py:554
  6.6 0.6 %collective-permute-start = (bf16[192,256]{1,0:T(8,128)(2,1)S(1)}, bf16[192,256]{1,0:T(8,128)(2,1)S(1)}, u32[]{:S(2)}, u32[]{:S(2)}) collective-permute-start(bf16[192,256]{1,0:T(8,128)(2,1)S(1)} %shard_map.62), channel_id=1, source_target_pairs={{0,8},{8,0},{16,24},{24,16},{1,9},{9,1},{17,25},{25,17},{2,10},{10... | collective-permute-start | bytes 294920 | tf_op jit(solution)/shard_map/ppermute | solution.py:554
  7.3 3.3 %shard_map.59 = (bf16[8,256,512]{2,1,0:T(8,128)(2,1)S(1)}, bf16[8,256,512]{2,1,0:T(8,128)(2,1)S(1)}, bf16[8,512,256]{2,1,0:T(8,128)(2,1)S(1)}) custom-call(bf16[256,4096]{1,0:T(8,128)(2,1)} %wt_ref.1, bf16[256,4096]{1,0:T(8,128)(2,1)} %ws_ref.1), custom_call_target="tpu_custom_call" | custom-call | flops 16777216 | bytes 10485760 | tf_op jit(solution)/shard_map/pallas_call | solution.py:595
  10.7 0.8 %shard_map.60 = (bf16[8,256,512]{2,1,0:T(8,128)(2,1)S(1)}, f32[8,8,512]{2,1,0:T(8,128)S(1)}) custom-call(bf16[256,256]{1,0:T(8,128)(2,1)S(1)} %copy-done.1, bf16[8,256,512]{2,1,0:T(8,128)(2,1)S(1)} %get-tuple-element.36.wt_ref.refs_3_), custom_call_target="tpu_custom_call" | custom-call | flops 536870912 | bytes 2097152 | tf_op jit(solution)/shard_map/pallas_call | solution.py:595
  11.5 1.5 %shard_map.61 = (bf16[256,256]{1,0:T(8,128)(2,1)S(1)}, f32[1,256]{1,0:T(1,128)S(1)}, f32[256,256]{1,0:T(8,128)S(1)}, bf16[8,256,512]{2,1,0:T(8,128)(2,1)S(1)}) custom-call(bf16[256,256]{1,0:T(8,128)(2,1)S(1)} %copy-done, bf16[8,256,512]{2,1,0:T(8,128)(2,1)S(1)} %get-tuple-element.38.ws_ref, bf16[8,512,256]{2,1,0:T(8,128)(2,1)S(1)} %get-tuple-element.39.turned_ref.ws_rows), custom_call_target="tpu_custom_call" | custom-call | flops 1073741824 | bytes 2097152 | tf_op jit(solution)/shard_map/pallas_call | solution.py:595
  13.0 1.9 %collective-permute-done.1.refs_1_ = bf16[192,256]{1,0:T(8,128)(2,1)S(1)} collective-permute-done((bf16[192,256]{1,0:T(8,128)(2,1)S(1)}, bf16[192,256]{1,0:T(8,128)(2,1)S(1)}, u32[]{:S(2)}, u32[]{:S(2)}) %collective-permute-start.1) | collective-permute-done | bytes 98336 | tf_op jit(solution)/shard_map/ppermute | solution.py:554
  14.9 0.2 shard_map.63
  15.2 1.0 %shard_map.64 = (bf16[8,768,512]{2,1,0:T(8,128)(2,1)S(1)}, f32[8,8,512]{2,1,0:T(8,128)S(1)}) custom-call(bf16[384,256]{1,0:T(8,128)(2,1)S(1)} %get-tuple-element.41.mine.refs_1_, bf16[8,256,512]{2,1,0:T(8,128)(2,1)S(1)} %get-tuple-element.36.wt_ref.refs_3_, f32[8,8,512]{2,1,0:T(8,128)S(1)} %get-tuple-element.37.after.own_cols), custom_call_target="tpu_custom_call" | custom-call | flops 805306368 | bytes 3145728 | tf_op jit(solution)/shard_map/pallas_call | solution.py:595
  16.2 0.4 collective-permute-done.3.refs_2_
  16.6 2.6 %shard_map.65 = (bf16[8,768,512]{2,1,0:T(8,128)(2,1)S(1)}, f32[4,256]{1,0:T(4,128)S(1)}, bf16[192,256]{1,0:T(8,128)(2,1)S(1)}) custom-call(bf16[8,768,512]{2,1,0:T(8,128)(2,1)S(1)} %get-tuple-element.42.refs_0_, bf16[384,256]{1,0:T(8,128)(2,1)S(1)} %get-tuple-element.41.mine.refs_1_, ...), custom_call_target="tpu_custom_call", output_to_operand_aliasing={{0}: (0, {})} | custom-call | flops 2147483648 | bytes 8388608 | tf_op jit(solution)/shard_map/pallas_call | solution.py:595
  19.2 1.6 %collective-permute-start.4 = (bf16[192,256]{1,0:T(8,128)(2,1)S(1)}, bf16[192,256]{1,0:T(8,128)(2,1)S(1)}, u32[]{:S(2)}, u32[]{:S(2)}) collective-permute-start(bf16[192,256]{1,0:T(8,128)(2,1)S(1)} %get-tuple-element.47.mine), channel_id=1, source_target_pairs={{0,2},{1,3},{2,0},{3,1},{4,6},{5,7},{6,4},{7,5},{8,10},{9,11},{10,... | collective-permute-start | bytes 294920 | tf_op jit(solution)/shard_map/ppermute | solution.py:554
  20.8 1.2 %collective-permute-done.6 = f32[4,256]{1,0:T(4,128)S(1)} collective-permute-done((f32[4,256]{1,0:T(4,128)S(1)}, f32[4,256]{1,0:T(4,128)S(1)}, u32[]{:S(2)}, u32[]{:S(2)}) %collective-permute-start.6) | collective-permute-done | bytes 4128 | tf_op jit(solution)/shard_map/ppermute | solution.py:554
  21.9 1.3 %collective-permute-start.9 = (f32[4,256]{1,0:T(4,128)S(1)}, f32[4,256]{1,0:T(4,128)S(1)}, u32[]{:S(2)}, u32[]{:S(2)}) collective-permute-start(f32[4,256]{1,0:T(4,128)S(1)} %add.24), channel_id=1, source_target_pairs={{0,7},{1,6},{2,5},{3,4},{4,3},{5,2},{6,1},{7,0},{8,15},{9,14},{10,... | collective-permute-start | bytes 12296 | tf_op jit(solution)/shard_map/ppermute | solution.py:554
  23.2 0.5 collective-permute-start.8
  23.7 1.3 %collective-permute-start.7 = (f32[4,256]{1,0:T(4,128)S(1)}, f32[4,256]{1,0:T(4,128)S(1)}, u32[]{:S(2)}, u32[]{:S(2)}) collective-permute-start(f32[4,256]{1,0:T(4,128)S(1)} %add.24), channel_id=1, source_target_pairs={{0,3},{1,2},{2,1},{3,0},{4,7},{5,6},{6,5},{7,4},{8,11},{9,10},{10,... | collective-permute-start | bytes 12296 | tf_op jit(solution)/shard_map/ppermute | solution.py:554
  25.0 0.4 collective-permute-start.5
  25.4 0.5 collective-permute-done.9
  25.9 0.4 collective-permute-done.8
  26.3 0.4 collective-permute-done.7
  26.8 2.0 %shard_map.68.after = f32[4,256]{1,0:T(4,128)S(1)} custom-call(bf16[768,256]{1,0:T(8,128)(2,1)S(1)} %shard_map.67.after.zs_ref.refs_6_.refs_5_, f32[4,256]{1,0:T(4,128)S(1)} %add_add_fusion.1.x_ref, bf16[8,256,512]{2,1,0:T(8,128)(2,1)S(1)} %get-tuple-element.43.refs_4_.own_ref.refs_1_.refs_2_, bf16[8,768,512]{2,1,0:T(8,128)(2,1)S(1)} %get-tuple-element.48.e_ref.refs_2_.refs_3_), custom_call_target="tpu_custom_call" | custom-call | flops 16777216 | bytes 8388608 | tf_op jit(solution)/shard_map/pallas_call | solution.py:595
  28.7 0.2 collective-permute-start.10
  29.0 0.7 %shard_map.69 = (f32[3,256]{1,0:T(4,128)S(1)}, bf16[2,768,512]{2,1,0:T(8,128)(2,1)S(1)}) custom-call(f32[4,256]{1,0:T(4,128)S(1)} %shard_map.68.after, bf16[768,256]{1,0:T(8,128)(2,1)S(1)} %shard_map.67.after.zs_ref.refs_6_.refs_5_, bf16[8,256,512]{2,1,0:T(8,128)(2,1)S(1)} %get-tuple-element.38.ws_ref), custom_call_target="tpu_custom_call" | custom-call | flops 402653184 | bytes 1572864 | tf_op jit(solution)/shard_map/pallas_call | solution.py:595
  29.7 0.3 collective-permute-done.10
  30.0 2.2 %collective-permute-start.13 = (f32[4,256]{1,0:T(4,128)S(1)}, f32[4,256]{1,0:T(4,128)S(1)}, u32[]{:S(2)}, u32[]{:S(2)}) collective-permute-start(f32[4,256]{1,0:T(4,128)S(1)} %add.28.after), channel_id=1, source_target_pairs={{0,7},{1,6},{2,5},{3,4},{4,3},{5,2},{6,1},{7,0},{8,15},{9,14},{10,... | collective-permute-start | bytes 12296 | tf_op jit(solution)/shard_map/ppermute | solution.py:554
  32.2 0.5 collective-permute-start.12
  32.7 0.3 collective-permute-start.11
  33.0 1.7 %shard_map.70 = (f32[3,256]{1,0:T(4,128)S(1)}, bf16[6,768,512]{2,1,0:T(8,128)(2,1)S(1)}) custom-call(f32[4,256]{1,0:T(4,128)S(1)} %add.28.after, bf16[768,256]{1,0:T(8,128)(2,1)S(1)} %shard_map.67.after.zs_ref.refs_6_.refs_5_, bf16[8,256,512]{2,1,0:T(8,128)(2,1)S(1)} %get-tuple-element.38.ws_ref), custom_call_target="tpu_custom_call" | custom-call | flops 1207959552 | bytes 4718592 | tf_op jit(solution)/shard_map/pallas_call | solution.py:595
  34.7 0.5 collective-permute-done.12
  35.2 0.5 collective-permute-done.11
  35.7 2.5 %shard_map.71 = (f32[8,1,512]{2,1,0:T(1,128)S(1)}, f32[272,256]{1,0:T(8,128)S(1)}, bf16[272,256]{1,0:T(8,128)(2,1)S(1)}) custom-call(f32[4,256]{1,0:T(4,128)S(1)} %add_add_fusion.x_ref, bf16[8,256,512]{2,1,0:T(8,128)(2,1)S(1)} %get-tuple-element.43.refs_4_.own_ref.refs_1_.refs_2_, bf16[8,768,512]{2,1,0:T(8,128)(2,1)S(1)} %get-tuple-element.48.e_ref.refs_2_.refs_3_, ...), custom_call_target="tpu_custom_call" | custom-call | flops 16777216 | bytes 8388608 | tf_op jit(solution)/shard_map/pallas_call | solution.py:595
  38.2 0.2 collective-permute-start.14
  38.4 1.2 %collective-permute-done.14.refs_1_ = bf16[272,256]{1,0:T(8,128)(2,1)S(1)} collective-permute-done((bf16[272,256]{1,0:T(8,128)(2,1)S(1)}, bf16[272,256]{1,0:T(8,128)(2,1)S(1)}, u32[]{:S(2)}, u32[]{:S(2)}) %collective-permute-start.14) | collective-permute-done | bytes 139296 | tf_op jit(solution)/shard_map/ppermute | solution.py:554
  39.7 1.5 %collective-permute-start.15 = (bf16[80,256]{1,0:T(8,128)(2,1)S(1)}, bf16[80,256]{1,0:T(8,128)(2,1)S(1)}, u32[]{:S(2)}, u32[]{:S(2)}) collective-permute-start(bf16[80,256]{1,0:T(8,128)(2,1)S(1)} %get-tuple-element.55), channel_id=1, source_target_pairs={{0,7},{1,6},{2,5},{3,4},{4,3},{5,2},{6,1},{7,0},{8,15},{9,14},{10,... | collective-permute-start | bytes 122888 | tf_op jit(solution)/shard_map/ppermute | solution.py:554
  41.2 0.3 collective-permute-start.16
  41.5 1.3 %collective-permute-start.17 = (bf16[80,256]{1,0:T(8,128)(2,1)S(1)}, bf16[80,256]{1,0:T(8,128)(2,1)S(1)}, u32[]{:S(2)}, u32[]{:S(2)}) collective-permute-start(bf16[80,256]{1,0:T(8,128)(2,1)S(1)} %get-tuple-element.57), channel_id=1, source_target_pairs={{0,3},{1,2},{2,1},{3,0},{4,7},{5,6},{6,5},{7,4},{8,11},{9,10},{10,... | collective-permute-start | bytes 122888 | tf_op jit(solution)/shard_map/ppermute | solution.py:554
  42.7 1.5 %collective-permute-done.15.refs_1_ = bf16[80,256]{1,0:T(8,128)(2,1)S(1)} collective-permute-done((bf16[80,256]{1,0:T(8,128)(2,1)S(1)}, bf16[80,256]{1,0:T(8,128)(2,1)S(1)}, u32[]{:S(2)}, u32[]{:S(2)}) %collective-permute-start.15) | collective-permute-done | bytes 40992 | tf_op jit(solution)/shard_map/ppermute | solution.py:554
  44.3 1.1 %collective-permute-done.16.refs_2_ = bf16[80,256]{1,0:T(8,128)(2,1)S(1)} collective-permute-done((bf16[80,256]{1,0:T(8,128)(2,1)S(1)}, bf16[80,256]{1,0:T(8,128)(2,1)S(1)}, u32[]{:S(2)}, u32[]{:S(2)}) %collective-permute-start.16) | collective-permute-done | bytes 40992 | tf_op jit(solution)/shard_map/ppermute | solution.py:554
  45.4 0.4 shard_map.73
  45.8 0.2 collective-permute-start.18
  45.9 1.2 %shard_map.74 = (bf16[64,4096]{1,0:T(8,128)(2,1)}, f32[8,128]{1,0:T(8,128)S(1)}) custom-call(bf16[32,256]{1,0:T(8,128)(2,1)S(1)} %get-tuple-element.59.refs_0_.share, bf16[8,256,512]{2,1,0:T(8,128)(2,1)S(1)} %get-tuple-element.43.refs_4_.own_ref.refs_1_.refs_2_, bf16[8,768,512]{2,1,0:T(8,128)(2,1)S(1)} %get-tuple-element.48.e_ref.refs_2_.refs_3_, ...), custom_call_target="tpu_custom_call" | custom-call | flops 134217728 | bytes 4194304 | tf_op jit(solution)/shard_map/pallas_call | solution.py:611
  47.2 2.2 %collective-permute-start.21 = (bf16[64,256]{1,0:T(8,128)(2,1)S(1)}, bf16[64,256]{1,0:T(8,128)(2,1)S(1)}, u32[]{:S(2)}, u32[]{:S(2)}) collective-permute-start(bf16[64,256]{1,0:T(8,128)(2,1)S(1)} %shard_map.75.refs_1_.share), channel_id=1, source_target_pairs={{0,7},{1,6},{2,5},{3,4},{4,3},{5,2},{6,1},{7,0},{8,15},{9,14},{10,... | collective-permute-start | bytes 98312 | tf_op jit(solution)/shard_map/ppermute | solution.py:554
  49.4 0.3 collective-permute-start.20
  49.7 0.8 %collective-permute-start.19 = (bf16[64,256]{1,0:T(8,128)(2,1)S(1)}, bf16[64,256]{1,0:T(8,128)(2,1)S(1)}, u32[]{:S(2)}, u32[]{:S(2)}) collective-permute-start(bf16[64,256]{1,0:T(8,128)(2,1)S(1)} %shard_map.75.refs_1_.share), channel_id=1, source_target_pairs={{0,3},{1,2},{2,1},{3,0},{4,7},{5,6},{6,5},{7,4},{8,11},{9,10},{10,... | collective-permute-start | bytes 98312 | tf_op jit(solution)/shard_map/ppermute | solution.py:554
  50.5 2.1 %shard_map.76 = (bf16[64,4096]{1,0:T(8,128)(2,1)}, f32[8,128]{1,0:T(8,128)S(1)}) custom-call(bf16[64,4096]{1,0:T(8,128)(2,1)} %get-tuple-element.66.refs_0_, bf16[64,256]{1,0:T(8,128)(2,1)S(1)} %shard_map.75.refs_1_.share, bf16[8,256,512]{2,1,0:T(8,128)(2,1)S(1)} %get-tuple-element.43.refs_4_.own_ref.refs_1_.refs_2_, ...), custom_call_target="tpu_custom_call", output_to_operand_aliasing={{0}: (0, {})} | custom-call | flops 402653184 | bytes 12582912 | tf_op jit(solution)/shard_map/pallas_call | solution.py:611
  52.6 0.2 collective-permute-done.20.refs_1_
  52.8 0.3 collective-permute-done.19.refs_0_
  53.0 0.7 %shard_map.77 = bf16[256,256]{1,0:T(8,128)(2,1)} custom-call(f32[8,128]{1,0:T(8,128)S(1)} %get-tuple-element.69.after, bf16[64,256]{1,0:T(8,128)(2,1)S(1)} %shard_map.75.refs_1_.share, bf16[64,256]{1,0:T(8,128)(2,1)S(1)} %collective-permute-done.19.refs_0_, bf16[64,256]{1,0:T(8,128)(2,1)S(1)} %collective-permute-done.20.refs_1_, ...), custom_call_target="tpu_custom_call" | custom-call | bytes 131072 | tf_op jit(solution)/shard_map/pallas_call | solution.py:595
  (23 shorter events, 0.4 us)
Async XLA Ops:
  1.5 9.1 %copy-start.1 = (bf16[256,256]{1,0:T(8,128)(2,1)S(1)}, bf16[256,256]{1,0:T(8,128)(2,1)}, u32[]{:S(2)}) copy-start(bf16[256,256]{1,0:T(8,128)(2,1)} %teacher_ref.1) | copy-start | bytes 393220
  1.5 11.5 %collective-permute-start.2 = (bf16[192,256]{1,0:T(8,128)(2,1)S(1)}, bf16[192,256]{1,0:T(8,128)(2,1)S(1)}, u32[]{:S(2)}, u32[]{:S(2)}) collective-permute-start(bf16[192,256]{1,0:T(8,128)(2,1)S(1)} %shard_map.62), channel_id=1, source_target_pairs={{0,24},{8,16},{16,8},{24,0},{1,25},{9,17},{17,9},{25,1},{2,26},{10... | collective-permute-start | bytes 294920 | tf_op jit(solution)/shard_map/ppermute | solution.py:554
  6.6 8.3 %collective-permute-start.1 = (bf16[192,256]{1,0:T(8,128)(2,1)S(1)}, bf16[192,256]{1,0:T(8,128)(2,1)S(1)}, u32[]{:S(2)}, u32[]{:S(2)}) collective-permute-start(bf16[192,256]{1,0:T(8,128)(2,1)S(1)} %shard_map.62), channel_id=1, source_target_pairs={{0,16},{8,24},{16,0},{24,8},{1,17},{9,25},{17,1},{25,9},{2,18},{10... | collective-permute-start | bytes 294920 | tf_op jit(solution)/shard_map/ppermute | solution.py:554
  6.6 8.3 %collective-permute-start = (bf16[192,256]{1,0:T(8,128)(2,1)S(1)}, bf16[192,256]{1,0:T(8,128)(2,1)S(1)}, u32[]{:S(2)}, u32[]{:S(2)}) collective-permute-start(bf16[192,256]{1,0:T(8,128)(2,1)S(1)} %shard_map.62), channel_id=1, source_target_pairs={{0,8},{8,0},{16,24},{24,16},{1,9},{9,1},{17,25},{25,17},{2,10},{10... | collective-permute-start | bytes 294920 | tf_op jit(solution)/shard_map/ppermute | solution.py:554
  10.6 0.9 %copy-start = (bf16[256,256]{1,0:T(8,128)(2,1)S(1)}, bf16[256,256]{1,0:T(8,128)(2,1)}, u32[]{:S(2)}) copy-start(bf16[256,256]{1,0:T(8,128)(2,1)} %refs_4_.1) | copy-start | bytes 393220
  15.1 1.5 %collective-permute-start.3 = (bf16[384,256]{1,0:T(8,128)(2,1)S(1)}, bf16[384,256]{1,0:T(8,128)(2,1)S(1)}, u32[]{:S(2)}, u32[]{:S(2)}) collective-permute-start(bf16[384,256]{1,0:T(8,128)(2,1)S(1)} %get-tuple-element.41.mine.refs_1_), channel_id=1, source_target_pairs={{0,1},{1,0},{2,3},{3,2},{4,5},{5,4},{6,7},{7,6},{8,9},{9,8},{10,11... | collective-permute-start | bytes 589832 | tf_op jit(solution)/shard_map/ppermute | solution.py:554
  19.2 5.7 %collective-permute-start.4 = (bf16[192,256]{1,0:T(8,128)(2,1)S(1)}, bf16[192,256]{1,0:T(8,128)(2,1)S(1)}, u32[]{:S(2)}, u32[]{:S(2)}) collective-permute-start(bf16[192,256]{1,0:T(8,128)(2,1)S(1)} %get-tuple-element.47.mine), channel_id=1, source_target_pairs={{0,2},{1,3},{2,0},{3,1},{4,6},{5,7},{6,4},{7,5},{8,10},{9,11},{10,... | collective-permute-start | bytes 294920 | tf_op jit(solution)/shard_map/ppermute | solution.py:554
  20.8 1.2 %collective-permute-start.6 = (f32[4,256]{1,0:T(4,128)S(1)}, f32[4,256]{1,0:T(4,128)S(1)}, u32[]{:S(2)}, u32[]{:S(2)}) collective-permute-start(f32[4,256]{1,0:T(4,128)S(1)} %get-tuple-element.46.after), channel_id=1, source_target_pairs={{0,1},{1,0},{2,3},{3,2},{4,5},{5,4},{6,7},{7,6},{8,9},{9,8},{10,11... | collective-permute-start | bytes 12296 | tf_op jit(solution)/shard_map/ppermute | solution.py:554
  21.9 3.9 %collective-permute-start.9 = (f32[4,256]{1,0:T(4,128)S(1)}, f32[4,256]{1,0:T(4,128)S(1)}, u32[]{:S(2)}, u32[]{:S(2)}) collective-permute-start(f32[4,256]{1,0:T(4,128)S(1)} %add.24), channel_id=1, source_target_pairs={{0,7},{1,6},{2,5},{3,4},{4,3},{5,2},{6,1},{7,0},{8,15},{9,14},{10,... | collective-permute-start | bytes 12296 | tf_op jit(solution)/shard_map/ppermute | solution.py:554
  23.2 3.1 %collective-permute-start.8 = (f32[4,256]{1,0:T(4,128)S(1)}, f32[4,256]{1,0:T(4,128)S(1)}, u32[]{:S(2)}, u32[]{:S(2)}) collective-permute-start(f32[4,256]{1,0:T(4,128)S(1)} %add.24), channel_id=1, source_target_pairs={{0,5},{1,4},{2,7},{3,6},{4,1},{5,0},{6,3},{7,2},{8,13},{9,12},{10,... | collective-permute-start | bytes 12296 | tf_op jit(solution)/shard_map/ppermute | solution.py:554
  23.7 3.0 %collective-permute-start.7 = (f32[4,256]{1,0:T(4,128)S(1)}, f32[4,256]{1,0:T(4,128)S(1)}, u32[]{:S(2)}, u32[]{:S(2)}) collective-permute-start(f32[4,256]{1,0:T(4,128)S(1)} %add.24), channel_id=1, source_target_pairs={{0,3},{1,2},{2,1},{3,0},{4,7},{5,6},{6,5},{7,4},{8,11},{9,10},{10,... | collective-permute-start | bytes 12296 | tf_op jit(solution)/shard_map/ppermute | solution.py:554
  25.0 1.7 %collective-permute-start.5 = (bf16[384,256]{1,0:T(8,128)(2,1)S(1)}, bf16[384,256]{1,0:T(8,128)(2,1)S(1)}, u32[]{:S(2)}, u32[]{:S(2)}) collective-permute-start(bf16[384,256]{1,0:T(8,128)(2,1)S(1)} %shard_map.66.mine), channel_id=1, source_target_pairs={{0,1},{1,0},{2,3},{3,2},{4,5},{5,4},{6,7},{7,6},{8,9},{9,8},{10,11... | collective-permute-start | bytes 589832 | tf_op jit(solution)/shard_map/ppermute | solution.py:554
  28.7 1.2 %collective-permute-start.10 = (f32[4,256]{1,0:T(4,128)S(1)}, f32[4,256]{1,0:T(4,128)S(1)}, u32[]{:S(2)}, u32[]{:S(2)}) collective-permute-start(f32[4,256]{1,0:T(4,128)S(1)} %shard_map.68.after), channel_id=1, source_target_pairs={{0,1},{1,0},{2,3},{3,2},{4,5},{5,4},{6,7},{7,6},{8,9},{9,8},{10,11... | collective-permute-start | bytes 12296 | tf_op jit(solution)/shard_map/ppermute | solution.py:554
  30.0 4.7 %collective-permute-start.13 = (f32[4,256]{1,0:T(4,128)S(1)}, f32[4,256]{1,0:T(4,128)S(1)}, u32[]{:S(2)}, u32[]{:S(2)}) collective-permute-start(f32[4,256]{1,0:T(4,128)S(1)} %add.28.after), channel_id=1, source_target_pairs={{0,7},{1,6},{2,5},{3,4},{4,3},{5,2},{6,1},{7,0},{8,15},{9,14},{10,... | collective-permute-start | bytes 12296 | tf_op jit(solution)/shard_map/ppermute | solution.py:554
  32.2 3.0 %collective-permute-start.12 = (f32[4,256]{1,0:T(4,128)S(1)}, f32[4,256]{1,0:T(4,128)S(1)}, u32[]{:S(2)}, u32[]{:S(2)}) collective-permute-start(f32[4,256]{1,0:T(4,128)S(1)} %add.28.after), channel_id=1, source_target_pairs={{0,5},{1,4},{2,7},{3,6},{4,1},{5,0},{6,3},{7,2},{8,13},{9,12},{10,... | collective-permute-start | bytes 12296 | tf_op jit(solution)/shard_map/ppermute | solution.py:554
  32.7 3.0 %collective-permute-start.11 = (f32[4,256]{1,0:T(4,128)S(1)}, f32[4,256]{1,0:T(4,128)S(1)}, u32[]{:S(2)}, u32[]{:S(2)}) collective-permute-start(f32[4,256]{1,0:T(4,128)S(1)} %add.28.after), channel_id=1, source_target_pairs={{0,3},{1,2},{2,1},{3,0},{4,7},{5,6},{6,5},{7,4},{8,11},{9,10},{10,... | collective-permute-start | bytes 12296 | tf_op jit(solution)/shard_map/ppermute | solution.py:554
  38.2 1.4 %collective-permute-start.14 = (bf16[272,256]{1,0:T(8,128)(2,1)S(1)}, bf16[272,256]{1,0:T(8,128)(2,1)S(1)}, u32[]{:S(2)}, u32[]{:S(2)}) collective-permute-start(bf16[272,256]{1,0:T(8,128)(2,1)S(1)} %get-tuple-element.53), channel_id=1, source_target_pairs={{0,1},{1,0},{2,3},{3,2},{4,5},{5,4},{6,7},{7,6},{8,9},{9,8},{10,11... | collective-permute-start | bytes 417800 | tf_op jit(solution)/shard_map/ppermute | solution.py:554
  39.7 4.6 %collective-permute-start.15 = (bf16[80,256]{1,0:T(8,128)(2,1)S(1)}, bf16[80,256]{1,0:T(8,128)(2,1)S(1)}, u32[]{:S(2)}, u32[]{:S(2)}) collective-permute-start(bf16[80,256]{1,0:T(8,128)(2,1)S(1)} %get-tuple-element.55), channel_id=1, source_target_pairs={{0,7},{1,6},{2,5},{3,4},{4,3},{5,2},{6,1},{7,0},{8,15},{9,14},{10,... | collective-permute-start | bytes 122888 | tf_op jit(solution)/shard_map/ppermute | solution.py:554
  41.2 4.2 %collective-permute-start.16 = (bf16[80,256]{1,0:T(8,128)(2,1)S(1)}, bf16[80,256]{1,0:T(8,128)(2,1)S(1)}, u32[]{:S(2)}, u32[]{:S(2)}) collective-permute-start(bf16[80,256]{1,0:T(8,128)(2,1)S(1)} %get-tuple-element.56), channel_id=1, source_target_pairs={{0,5},{1,4},{2,7},{3,6},{4,1},{5,0},{6,3},{7,2},{8,13},{9,12},{10,... | collective-permute-start | bytes 122888 | tf_op jit(solution)/shard_map/ppermute | solution.py:554
  41.5 3.9 %collective-permute-start.17 = (bf16[80,256]{1,0:T(8,128)(2,1)S(1)}, bf16[80,256]{1,0:T(8,128)(2,1)S(1)}, u32[]{:S(2)}, u32[]{:S(2)}) collective-permute-start(bf16[80,256]{1,0:T(8,128)(2,1)S(1)} %get-tuple-element.57), channel_id=1, source_target_pairs={{0,3},{1,2},{2,1},{3,0},{4,7},{5,6},{6,5},{7,4},{8,11},{9,10},{10,... | collective-permute-start | bytes 122888 | tf_op jit(solution)/shard_map/ppermute | solution.py:554
  45.8 1.4 %collective-permute-start.18 = (bf16[32,256]{1,0:T(8,128)(2,1)S(1)}, bf16[32,256]{1,0:T(8,128)(2,1)S(1)}, u32[]{:S(2)}, u32[]{:S(2)}) collective-permute-start(bf16[32,256]{1,0:T(8,128)(2,1)S(1)} %get-tuple-element.59.refs_0_.share), channel_id=1, source_target_pairs={{0,1},{1,0},{2,3},{3,2},{4,5},{5,4},{6,7},{7,6},{8,9},{9,8},{10,11... | collective-permute-start | bytes 49160 | tf_op jit(solution)/shard_map/ppermute | solution.py:554
  47.2 5.4 %collective-permute-start.21 = (bf16[64,256]{1,0:T(8,128)(2,1)S(1)}, bf16[64,256]{1,0:T(8,128)(2,1)S(1)}, u32[]{:S(2)}, u32[]{:S(2)}) collective-permute-start(bf16[64,256]{1,0:T(8,128)(2,1)S(1)} %shard_map.75.refs_1_.share), channel_id=1, source_target_pairs={{0,7},{1,6},{2,5},{3,4},{4,3},{5,2},{6,1},{7,0},{8,15},{9,14},{10,... | collective-permute-start | bytes 98312 | tf_op jit(solution)/shard_map/ppermute | solution.py:554
  49.4 3.4 %collective-permute-start.20 = (bf16[64,256]{1,0:T(8,128)(2,1)S(1)}, bf16[64,256]{1,0:T(8,128)(2,1)S(1)}, u32[]{:S(2)}, u32[]{:S(2)}) collective-permute-start(bf16[64,256]{1,0:T(8,128)(2,1)S(1)} %shard_map.75.refs_1_.share), channel_id=1, source_target_pairs={{0,5},{1,4},{2,7},{3,6},{4,1},{5,0},{6,3},{7,2},{8,13},{9,12},{10,... | collective-permute-start | bytes 98312 | tf_op jit(solution)/shard_map/ppermute | solution.py:554
  49.7 3.4 %collective-permute-start.19 = (bf16[64,256]{1,0:T(8,128)(2,1)S(1)}, bf16[64,256]{1,0:T(8,128)(2,1)S(1)}, u32[]{:S(2)}, u32[]{:S(2)}) collective-permute-start(bf16[64,256]{1,0:T(8,128)(2,1)S(1)} %shard_map.75.refs_1_.share), channel_id=1, source_target_pairs={{0,3},{1,2},{2,1},{3,0},{4,7},{5,6},{6,5},{7,4},{8,11},{9,10},{10,... | collective-permute-start | bytes 98312 | tf_op jit(solution)/shard_map/ppermute | solution.py:554

commit v3 on v2

--- a/solution.py
+++ b/solution.py
@@ -84,7 +84,7 @@
     for i in range(1, steps):
         carry = result()
         runs, result = first(i)
-        in_turn(second(i - 1, carry), runs)
+        in_turn(runs, second(i - 1, carry))
     in_turn(second(steps - 1, result()), [])
 
 
@@ -158,7 +158,7 @@
 
 
 def units_kernel(after, also, *refs):
-    blocks, outs = refs[:-2], refs[-2:]
+    blocks, outs = refs[-3::-1], refs[-2:]
     start = 0
     for out in outs:
         size = out.shape[0] // len(blocks)
@@ -289,8 +289,7 @@
 
 
 def first_kernel(nb, begun, *refs):
-    mine, other, wt_ref, own_ref, cols_ref, quarters, e_ref, out_ref, passed, acc = refs[begun:]
-    passed[...] = quarters[...]
+    mine, other, wt_ref, own_ref, cols_ref, e_ref, out_ref, acc = refs[begun:]
     rows = own_ref.shape[1]
     side = lax.axis_index("proto") % 2
     acc[...] = jnp.zeros_like(acc)
@@ -544,9 +543,24 @@
     moved, out_ref = refs[:-1], refs[-1]
     rows = share.shape[0]
     me = lax.axis_index("proto") ^ 1
-    for hop, ref in zip((0, *hops), (share, *moved)):
+    for hop, ref in zip((0, *hops[::-1]), (share, *moved)):
         place = ((me ^ hop) // hops[0]) % (1 + len(hops))
         out_ref[pl.ds(pl.multiple_of(place * rows, rows), rows), :] = ref[...].astype(out_ref.dtype)
+
+
+def last_join_kernel(hops, after, share, *refs):
+    moved, out_ref, sems = refs[:-2], refs[-2], refs[-1]
+    rows = share.shape[0]
+    me = lax.axis_index("proto") ^ 1
+    copies = []
+    for k, (hop, ref) in enumerate(zip((0, *hops[::-1]), (share, *moved))):
+        place = ((me ^ hop) // hops[0]) % (1 + len(hops))
+        to = out_ref.at[pl.ds(pl.multiple_of(place * rows, rows), rows), :]
+        copies.append(pltpu.make_async_copy(ref, to, sems.at[k]))
+    for copy in copies:
+        copy.start()
+    for copy in copies:
+        copy.wait()
 
 
 def permute(value, axis, s):
@@ -682,10 +696,11 @@
         8 * crops * width,
         2 * crops * width,
         0,
-        *blocks,
+        *reversed(blocks),
         after=(own_cols, own_tot),
     )
     other = permute(mine, "proto", 1)
+    moved = permute(quarters, "proto", 2)
 
     begun, cols = (), own_cols
     if keep:
@@ -700,13 +715,9 @@
             unit_wt,
             own_cols,
         )
-    e, x, quarters = call(
+    e, x = call(
         functools.partial(first_kernel, nb, len(begun)),
-        [
-            shape(steps, rest, BLK, dtype=BF),
-            shape(nb, width),
-            shape(rest // 4, width, dtype=BF),
-        ],
+        [shape(steps, rest, BLK, dtype=BF), shape(nb, width)],
         [lane_sums],
         2 * big * width,
         2 * big,
@@ -717,7 +728,6 @@
         unit_wt,
         own_e,
         cols,
-        quarters,
         aliases={0: 0} if begun else {},
     )
     (student_mine,) = call(
@@ -728,7 +738,7 @@
         2 * rest * width,
         0,
         quarters,
-        permute(quarters, "proto", 2),
+        moved,
         after=(x,),
     )
     (zs,) = call(
@@ -765,7 +775,7 @@
             moved = permutes(x, "proto", [crossed(hop) for hop in hops])
             if k in pieces:
                 student_piece(x)
-            for value in moved:
+            for value in reversed(moved):
                 x = x + value
         return x
 
@@ -877,6 +887,16 @@
                 ratio,
                 *((own_s, *kept) if keep else (unit_ws,)),
             )
+        if k + 1 == len(rounds) and share.dtype == BF:
+            (share,) = pl.pallas_call(
+                functools.partial(last_join_kernel, hops),
+                out_shape=[shape(rows, width, dtype=BF)],
+                in_specs=[anywhere] + [vmem] * (1 + len(moved)),
+                out_specs=[hbm],
+                scratch_shapes=[pltpu.SemaphoreType.DMA((1 + len(moved),))],
+                compiler_params=pltpu.CompilerParams(vmem_limit_bytes=limit),
+            )(token, share, *reversed(moved))
+            break
         (share,) = call(
             functools.partial(join_kernel, hops),
             [shape((1 + len(hops)) * share.shape[0], width, dtype=BF if k + 1 == len(rounds) else share.dtype)],
@@ -885,7 +905,7 @@
             8 * share.shape[0] * width,
             0,
             share,
-            *moved,
+            *reversed(moved),
             after=(token,),
         )
     return (done[0], share)

time: 53.9 us -> 53.6 us (level)
  waiting for transfers between devices: 10.4 us -> 9.09 us
  starting transfers between devices: 20.7 us -> 21.6 us
    ppermute x22, waiting for transfers between devices: 10.4 us -> 9.09 us  [permute(): return lax.ppermute(value, axis, [(i, i ^ s) for i in range(n)])]
    ppermute x22, starting transfers between devices: 20.7 us -> 21.6 us  [permute(): return lax.ppermute(value, axis, [(i, i ^ s) for i in range(n)])]
    pallas_call x17 -> x16, Pallas kernels: 18.4 us -> 17.6 us  [call(): pl.pallas_call(kernel, out_shape=out_shape, in_specs=[hbm] * len(far) + [...]
    pallas_call x0 -> x1, Pallas kernels: none -> 0.68 us  [shards(): pl.pallas_call(functools.partial(last_join_kernel, hops), out_shape=[shap...]
  transfers between devices with their start and end apart: 22 -> 22, of which waited for: 14 -> 12; matrix products, arithmetic and copies ran while one was open for 0% -> 0% of each run, Pallas kernels for 23% -> 28%
where the time goes in v3:
time: 53.6 us; the launch traced here: 53.4 us
  Pallas kernels  21.6 us (40%)
  starting transfers between devices  21.6 us (40%)
  waiting for transfers between devices  9.09 us (17%)
  between operations  0.98 us (2%)
    ppermute x22, starting transfers between devices, permute(): return lax.ppermute(value, axis, [(i, i ^ s) for i in range(n)])  21.6 us
    pallas_call x16, Pallas kernels, call(): pl.pallas_call(kernel, out_shape=out_shape, in_specs=[hbm] * len(far) + [...  17.6 us
    ppermute x22, waiting for transfers between devices, permute(): return lax.ppermute(value, axis, [(i, i ^ s) for i in range(n)])  9.09 us
    pallas_call x2, Pallas kernels, weight_call(): pl.pallas_call(kernel, out_shape=[out_shape, shape(8, LANES)], in_specs=[...  3.31 us
  transfers between devices with their start and end apart: 22, of which 12 were waited for; matrix products, arithmetic and copies ran while one was open for 0% of the time, Pallas kernels for 28%

profile of v3, /device:TPU:0, one launch (start us, length us, event | category | flops | bytes accessed | tf_op | source)
XLA Modules:
  0.0 53.4 jit_solution(2804082288189639356)
XLA Ops:
  0.6 0.9 %shard_map.62 = bf16[192,256]{1,0:T(8,128)(2,1)S(1)} custom-call(bf16[256,256]{1,0:T(8,128)(2,1)} %teacher_ref.1, bf16[256,256]{1,0:T(8,128)(2,1)} %refs_4_.1), custom_call_target="tpu_custom_call" | custom-call | bytes 262144 | tf_op jit(solution)/shard_map/pallas_call | solution.py:609
  1.5 5.1 %collective-permute-start = (bf16[192,256]{1,0:T(8,128)(2,1)S(1)}, bf16[192,256]{1,0:T(8,128)(2,1)S(1)}, u32[]{:S(2)}, u32[]{:S(2)}) collective-permute-start(bf16[192,256]{1,0:T(8,128)(2,1)S(1)} %shard_map.62), channel_id=1, source_target_pairs={{0,24},{8,16},{16,8},{24,0},{1,25},{9,17},{17,9},{25,1},{2,26},{10... | collective-permute-start | bytes 294920 | tf_op jit(solution)/shard_map/ppermute | solution.py:568
  6.6 0.6 %collective-permute-start.2 = (bf16[192,256]{1,0:T(8,128)(2,1)S(1)}, bf16[192,256]{1,0:T(8,128)(2,1)S(1)}, u32[]{:S(2)}, u32[]{:S(2)}) collective-permute-start(bf16[192,256]{1,0:T(8,128)(2,1)S(1)} %shard_map.62), channel_id=1, source_target_pairs={{0,8},{8,0},{16,24},{24,16},{1,9},{9,1},{17,25},{25,17},{2,10},{10... | collective-permute-start | bytes 294920 | tf_op jit(solution)/shard_map/ppermute | solution.py:568
  7.3 3.3 %shard_map.59 = (bf16[8,256,512]{2,1,0:T(8,128)(2,1)S(1)}, bf16[8,256,512]{2,1,0:T(8,128)(2,1)S(1)}, bf16[8,512,256]{2,1,0:T(8,128)(2,1)S(1)}) custom-call(bf16[256,4096]{1,0:T(8,128)(2,1)} %wt_ref.1, bf16[256,4096]{1,0:T(8,128)(2,1)} %ws_ref.1), custom_call_target="tpu_custom_call" | custom-call | flops 16777216 | bytes 10485760 | tf_op jit(solution)/shard_map/pallas_call | solution.py:609
  10.7 0.8 %shard_map.60 = (bf16[8,256,512]{2,1,0:T(8,128)(2,1)S(1)}, f32[8,8,512]{2,1,0:T(8,128)S(1)}) custom-call(bf16[256,256]{1,0:T(8,128)(2,1)S(1)} %copy-done.1, bf16[8,256,512]{2,1,0:T(8,128)(2,1)S(1)} %get-tuple-element.35.wt_ref.refs_3_), custom_call_target="tpu_custom_call" | custom-call | flops 536870912 | bytes 2097152 | tf_op jit(solution)/shard_map/pallas_call | solution.py:609
  11.4 0.1 copy-done
  11.5 1.5 %shard_map.61 = (bf16[256,256]{1,0:T(8,128)(2,1)S(1)}, f32[1,256]{1,0:T(1,128)S(1)}, f32[256,256]{1,0:T(8,128)S(1)}, bf16[8,256,512]{2,1,0:T(8,128)(2,1)S(1)}) custom-call(bf16[256,256]{1,0:T(8,128)(2,1)S(1)} %copy-done, bf16[8,256,512]{2,1,0:T(8,128)(2,1)S(1)} %get-tuple-element.37.ws_ref, bf16[8,512,256]{2,1,0:T(8,128)(2,1)S(1)} %get-tuple-element.38.turned_ref.ws_rows), custom_call_target="tpu_custom_call" | custom-call | flops 1073741824 | bytes 2097152 | tf_op jit(solution)/shard_map/pallas_call | solution.py:609
  13.0 1.9 %collective-permute-done.1.refs_1_ = bf16[192,256]{1,0:T(8,128)(2,1)S(1)} collective-permute-done((bf16[192,256]{1,0:T(8,128)(2,1)S(1)}, bf16[192,256]{1,0:T(8,128)(2,1)S(1)}, u32[]{:S(2)}, u32[]{:S(2)}) %collective-permute-start.1) | collective-permute-done | bytes 98336 | tf_op jit(solution)/shard_map/ppermute | solution.py:568
  14.9 0.2 shard_map.63
  15.2 1.6 %collective-permute-start.4 = (bf16[192,256]{1,0:T(8,128)(2,1)S(1)}, bf16[192,256]{1,0:T(8,128)(2,1)S(1)}, u32[]{:S(2)}, u32[]{:S(2)}) collective-permute-start(bf16[192,256]{1,0:T(8,128)(2,1)S(1)} %get-tuple-element.45.mine), channel_id=1, source_target_pairs={{0,2},{1,3},{2,0},{3,1},{4,6},{5,7},{6,4},{7,5},{8,10},{9,11},{10,... | collective-permute-start | bytes 294920 | tf_op jit(solution)/shard_map/ppermute | solution.py:568
  16.8 1.0 %shard_map.64 = (bf16[8,768,512]{2,1,0:T(8,128)(2,1)S(1)}, f32[8,8,512]{2,1,0:T(8,128)S(1)}) custom-call(bf16[384,256]{1,0:T(8,128)(2,1)S(1)} %get-tuple-element.40.mine.refs_1_, bf16[8,256,512]{2,1,0:T(8,128)(2,1)S(1)} %get-tuple-element.35.wt_ref.refs_3_, f32[8,8,512]{2,1,0:T(8,128)S(1)} %get-tuple-element.36.after.own_cols), custom_call_target="tpu_custom_call" | custom-call | flops 805306368 | bytes 3145728 | tf_op jit(solution)/shard_map/pallas_call | solution.py:609
  17.7 2.6 %shard_map.65 = (bf16[8,768,512]{2,1,0:T(8,128)(2,1)S(1)}, f32[4,256]{1,0:T(4,128)S(1)}) custom-call(bf16[8,768,512]{2,1,0:T(8,128)(2,1)S(1)} %get-tuple-element.41.refs_0_, bf16[384,256]{1,0:T(8,128)(2,1)S(1)} %get-tuple-element.40.mine.refs_1_, bf16[384,256]{1,0:T(8,128)(2,1)S(1)} %collective-permute-done.3.refs_2_, ...), custom_call_target="tpu_custom_call", output_to_operand_aliasing={{0}: (0, {})} | custom-call | flops 2147483648 | bytes 8388608 | tf_op jit(solution)/shard_map/pallas_call | solution.py:609
  20.3 0.4 collective-permute-start.6
  20.7 0.9 %collective-permute-done.6 = f32[4,256]{1,0:T(4,128)S(1)} collective-permute-done((f32[4,256]{1,0:T(4,128)S(1)}, f32[4,256]{1,0:T(4,128)S(1)}, u32[]{:S(2)}, u32[]{:S(2)}) %collective-permute-start.6) | collective-permute-done | bytes 4128 | tf_op jit(solution)/shard_map/ppermute | solution.py:568
  21.6 1.4 %collective-permute-start.7 = (f32[4,256]{1,0:T(4,128)S(1)}, f32[4,256]{1,0:T(4,128)S(1)}, u32[]{:S(2)}, u32[]{:S(2)}) collective-permute-start(f32[4,256]{1,0:T(4,128)S(1)} %add.24), channel_id=1, source_target_pairs={{0,7},{1,6},{2,5},{3,4},{4,3},{5,2},{6,1},{7,0},{8,15},{9,14},{10,... | collective-permute-start | bytes 12296 | tf_op jit(solution)/shard_map/ppermute | solution.py:568
  23.0 0.3 collective-permute-start.8
  23.3 1.4 %collective-permute-start.9 = (f32[4,256]{1,0:T(4,128)S(1)}, f32[4,256]{1,0:T(4,128)S(1)}, u32[]{:S(2)}, u32[]{:S(2)}) collective-permute-start(f32[4,256]{1,0:T(4,128)S(1)} %add.24), channel_id=1, source_target_pairs={{0,3},{1,2},{2,1},{3,0},{4,7},{5,6},{6,5},{7,4},{8,11},{9,10},{10,... | collective-permute-start | bytes 12296 | tf_op jit(solution)/shard_map/ppermute | solution.py:568
  24.7 0.3 collective-permute-start.5
  25.0 0.5 collective-permute-done.7
  25.5 0.5 collective-permute-done.8
  26.0 0.3 collective-permute-done.9
  26.4 2.0 %shard_map.68.after = f32[4,256]{1,0:T(4,128)S(1)} custom-call(bf16[768,256]{1,0:T(8,128)(2,1)S(1)} %shard_map.67.after.zs_ref.refs_6_.refs_5_, f32[4,256]{1,0:T(4,128)S(1)} %add_add_fusion.1.x_ref, bf16[8,256,512]{2,1,0:T(8,128)(2,1)S(1)} %get-tuple-element.42.refs_4_.own_ref.refs_1_.refs_2_, bf16[8,768,512]{2,1,0:T(8,128)(2,1)S(1)} %get-tuple-element.46.e_ref.refs_2_.refs_3_), custom_call_target="tpu_custom_call" | custom-call | flops 16777216 | bytes 8388608 | tf_op jit(solution)/shard_map/pallas_call | solution.py:609
  28.4 0.4 collective-permute-start.10
  28.7 0.7 %shard_map.69 = (f32[3,256]{1,0:T(4,128)S(1)}, bf16[2,768,512]{2,1,0:T(8,128)(2,1)S(1)}) custom-call(f32[4,256]{1,0:T(4,128)S(1)} %shard_map.68.after, bf16[768,256]{1,0:T(8,128)(2,1)S(1)} %shard_map.67.after.zs_ref.refs_6_.refs_5_, bf16[8,256,512]{2,1,0:T(8,128)(2,1)S(1)} %get-tuple-element.37.ws_ref), custom_call_target="tpu_custom_call" | custom-call | flops 402653184 | bytes 1572864 | tf_op jit(solution)/shard_map/pallas_call | solution.py:609
  29.4 0.2 collective-permute-done.10
  29.6 2.3 %collective-permute-start.11 = (f32[4,256]{1,0:T(4,128)S(1)}, f32[4,256]{1,0:T(4,128)S(1)}, u32[]{:S(2)}, u32[]{:S(2)}) collective-permute-start(f32[4,256]{1,0:T(4,128)S(1)} %add.28.after), channel_id=1, source_target_pairs={{0,7},{1,6},{2,5},{3,4},{4,3},{5,2},{6,1},{7,0},{8,15},{9,14},{10,... | collective-permute-start | bytes 12296 | tf_op jit(solution)/shard_map/ppermute | solution.py:568
  32.0 0.3 collective-permute-start.12
  32.3 0.4 collective-permute-start.13
  32.7 1.7 %shard_map.70 = (f32[3,256]{1,0:T(4,128)S(1)}, bf16[6,768,512]{2,1,0:T(8,128)(2,1)S(1)}) custom-call(f32[4,256]{1,0:T(4,128)S(1)} %add.28.after, bf16[768,256]{1,0:T(8,128)(2,1)S(1)} %shard_map.67.after.zs_ref.refs_6_.refs_5_, bf16[8,256,512]{2,1,0:T(8,128)(2,1)S(1)} %get-tuple-element.37.ws_ref), custom_call_target="tpu_custom_call" | custom-call | flops 1207959552 | bytes 4718592 | tf_op jit(solution)/shard_map/pallas_call | solution.py:609
  34.5 0.5 collective-permute-done.12
  35.0 0.3 collective-permute-done.13
  35.3 2.4 %shard_map.71 = (f32[8,1,512]{2,1,0:T(1,128)S(1)}, f32[272,256]{1,0:T(8,128)S(1)}, bf16[272,256]{1,0:T(8,128)(2,1)S(1)}) custom-call(f32[4,256]{1,0:T(4,128)S(1)} %add_add_fusion.x_ref, bf16[8,256,512]{2,1,0:T(8,128)(2,1)S(1)} %get-tuple-element.42.refs_4_.own_ref.refs_1_.refs_2_, bf16[8,768,512]{2,1,0:T(8,128)(2,1)S(1)} %get-tuple-element.46.e_ref.refs_2_.refs_3_, ...), custom_call_target="tpu_custom_call" | custom-call | flops 16777216 | bytes 8388608 | tf_op jit(solution)/shard_map/pallas_call | solution.py:609
  37.8 0.4 collective-permute-start.14
  38.1 1.1 %collective-permute-done.14.refs_1_ = bf16[272,256]{1,0:T(8,128)(2,1)S(1)} collective-permute-done((bf16[272,256]{1,0:T(8,128)(2,1)S(1)}, bf16[272,256]{1,0:T(8,128)(2,1)S(1)}, u32[]{:S(2)}, u32[]{:S(2)}) %collective-permute-start.14) | collective-permute-done | bytes 139296 | tf_op jit(solution)/shard_map/ppermute | solution.py:568
  39.2 1.5 %collective-permute-start.15 = (bf16[80,256]{1,0:T(8,128)(2,1)S(1)}, bf16[80,256]{1,0:T(8,128)(2,1)S(1)}, u32[]{:S(2)}, u32[]{:S(2)}) collective-permute-start(bf16[80,256]{1,0:T(8,128)(2,1)S(1)} %get-tuple-element.53), channel_id=1, source_target_pairs={{0,7},{1,6},{2,5},{3,4},{4,3},{5,2},{6,1},{7,0},{8,15},{9,14},{10,... | collective-permute-start | bytes 122888 | tf_op jit(solution)/shard_map/ppermute | solution.py:568
  40.8 0.4 collective-permute-start.16
  41.2 1.3 %collective-permute-start.17 = (bf16[80,256]{1,0:T(8,128)(2,1)S(1)}, bf16[80,256]{1,0:T(8,128)(2,1)S(1)}, u32[]{:S(2)}, u32[]{:S(2)}) collective-permute-start(bf16[80,256]{1,0:T(8,128)(2,1)S(1)} %get-tuple-element.55), channel_id=1, source_target_pairs={{0,3},{1,2},{2,1},{3,0},{4,7},{5,6},{6,5},{7,4},{8,11},{9,10},{10,... | collective-permute-start | bytes 122888 | tf_op jit(solution)/shard_map/ppermute | solution.py:568
  42.4 1.2 %collective-permute-done.15.refs_1_ = bf16[80,256]{1,0:T(8,128)(2,1)S(1)} collective-permute-done((bf16[80,256]{1,0:T(8,128)(2,1)S(1)}, bf16[80,256]{1,0:T(8,128)(2,1)S(1)}, u32[]{:S(2)}, u32[]{:S(2)}) %collective-permute-start.15) | collective-permute-done | bytes 40992 | tf_op jit(solution)/shard_map/ppermute | solution.py:568
  43.6 1.2 %collective-permute-done.16.refs_2_ = bf16[80,256]{1,0:T(8,128)(2,1)S(1)} collective-permute-done((bf16[80,256]{1,0:T(8,128)(2,1)S(1)}, bf16[80,256]{1,0:T(8,128)(2,1)S(1)}, u32[]{:S(2)}, u32[]{:S(2)}) %collective-permute-start.16) | collective-permute-done | bytes 40992 | tf_op jit(solution)/shard_map/ppermute | solution.py:568
  44.9 0.4 shard_map.73
  45.3 0.2 collective-permute-start.18
  45.5 1.2 %shard_map.74 = (bf16[64,4096]{1,0:T(8,128)(2,1)}, f32[8,128]{1,0:T(8,128)S(1)}) custom-call(bf16[32,256]{1,0:T(8,128)(2,1)S(1)} %get-tuple-element.57.refs_0_.share, bf16[8,256,512]{2,1,0:T(8,128)(2,1)S(1)} %get-tuple-element.42.refs_4_.own_ref.refs_1_.refs_2_, bf16[8,768,512]{2,1,0:T(8,128)(2,1)S(1)} %get-tuple-element.46.e_ref.refs_2_.refs_3_, ...), custom_call_target="tpu_custom_call" | custom-call | flops 134217728 | bytes 4194304 | tf_op jit(solution)/shard_map/pallas_call | solution.py:625
  46.7 2.1 %collective-permute-start.19 = (bf16[64,256]{1,0:T(8,128)(2,1)S(1)}, bf16[64,256]{1,0:T(8,128)(2,1)S(1)}, u32[]{:S(2)}, u32[]{:S(2)}) collective-permute-start(bf16[64,256]{1,0:T(8,128)(2,1)S(1)} %shard_map.75.refs_1_.share), channel_id=1, source_target_pairs={{0,7},{1,6},{2,5},{3,4},{4,3},{5,2},{6,1},{7,0},{8,15},{9,14},{10,... | collective-permute-start | bytes 98312 | tf_op jit(solution)/shard_map/ppermute | solution.py:568
  48.8 0.4 collective-permute-start.20
  49.2 0.8 %collective-permute-start.21 = (bf16[64,256]{1,0:T(8,128)(2,1)S(1)}, bf16[64,256]{1,0:T(8,128)(2,1)S(1)}, u32[]{:S(2)}, u32[]{:S(2)}) collective-permute-start(bf16[64,256]{1,0:T(8,128)(2,1)S(1)} %shard_map.75.refs_1_.share), channel_id=1, source_target_pairs={{0,3},{1,2},{2,1},{3,0},{4,7},{5,6},{6,5},{7,4},{8,11},{9,10},{10,... | collective-permute-start | bytes 98312 | tf_op jit(solution)/shard_map/ppermute | solution.py:568
  50.0 2.1 %shard_map.76 = (bf16[64,4096]{1,0:T(8,128)(2,1)}, f32[8,128]{1,0:T(8,128)S(1)}) custom-call(bf16[64,4096]{1,0:T(8,128)(2,1)} %get-tuple-element.64.refs_0_, bf16[64,256]{1,0:T(8,128)(2,1)S(1)} %shard_map.75.refs_1_.share, bf16[8,256,512]{2,1,0:T(8,128)(2,1)S(1)} %get-tuple-element.42.refs_4_.own_ref.refs_1_.refs_2_, ...), custom_call_target="tpu_custom_call", output_to_operand_aliasing={{0}: (0, {})} | custom-call | flops 402653184 | bytes 12582912 | tf_op jit(solution)/shard_map/pallas_call | solution.py:625
  52.1 0.4 collective-permute-done.21.refs_2_
  52.6 0.7 %shard_map.77 = bf16[256,256]{1,0:T(8,128)(2,1)} custom-call(f32[8,128]{1,0:T(8,128)S(1)} %get-tuple-element.67.after, bf16[64,256]{1,0:T(8,128)(2,1)S(1)} %shard_map.75.refs_1_.share, bf16[64,256]{1,0:T(8,128)(2,1)S(1)} %collective-permute-done.19.refs_0_, bf16[64,256]{1,0:T(8,128)(2,1)S(1)} %collective-permute-done.20.refs_1_, ...), custom_call_target="tpu_custom_call" | custom-call | tf_op jit(solution)/shard_map/pallas_call | solution.py:891
  (23 shorter events, 0.3 us)
Async XLA Ops:
  1.5 9.1 %copy-start.1 = (bf16[256,256]{1,0:T(8,128)(2,1)S(1)}, bf16[256,256]{1,0:T(8,128)(2,1)}, u32[]{:S(2)}) copy-start(bf16[256,256]{1,0:T(8,128)(2,1)} %teacher_ref.1) | copy-start | bytes 393220
  1.5 11.5 %collective-permute-start = (bf16[192,256]{1,0:T(8,128)(2,1)S(1)}, bf16[192,256]{1,0:T(8,128)(2,1)S(1)}, u32[]{:S(2)}, u32[]{:S(2)}) collective-permute-start(bf16[192,256]{1,0:T(8,128)(2,1)S(1)} %shard_map.62), channel_id=1, source_target_pairs={{0,24},{8,16},{16,8},{24,0},{1,25},{9,17},{17,9},{25,1},{2,26},{10... | collective-permute-start | bytes 294920 | tf_op jit(solution)/shard_map/ppermute | solution.py:568
  6.6 8.3 %collective-permute-start.1 = (bf16[192,256]{1,0:T(8,128)(2,1)S(1)}, bf16[192,256]{1,0:T(8,128)(2,1)S(1)}, u32[]{:S(2)}, u32[]{:S(2)}) collective-permute-start(bf16[192,256]{1,0:T(8,128)(2,1)S(1)} %shard_map.62), channel_id=1, source_target_pairs={{0,16},{8,24},{16,0},{24,8},{1,17},{9,25},{17,1},{25,9},{2,18},{10... | collective-permute-start | bytes 294920 | tf_op jit(solution)/shard_map/ppermute | solution.py:568
  6.6 8.3 %collective-permute-start.2 = (bf16[192,256]{1,0:T(8,128)(2,1)S(1)}, bf16[192,256]{1,0:T(8,128)(2,1)S(1)}, u32[]{:S(2)}, u32[]{:S(2)}) collective-permute-start(bf16[192,256]{1,0:T(8,128)(2,1)S(1)} %shard_map.62), channel_id=1, source_target_pairs={{0,8},{8,0},{16,24},{24,16},{1,9},{9,1},{17,25},{25,17},{2,10},{10... | collective-permute-start | bytes 294920 | tf_op jit(solution)/shard_map/ppermute | solution.py:568
  10.6 0.9 %copy-start = (bf16[256,256]{1,0:T(8,128)(2,1)S(1)}, bf16[256,256]{1,0:T(8,128)(2,1)}, u32[]{:S(2)}) copy-start(bf16[256,256]{1,0:T(8,128)(2,1)} %refs_4_.1) | copy-start | bytes 393220
  15.1 2.6 %collective-permute-start.3 = (bf16[384,256]{1,0:T(8,128)(2,1)S(1)}, bf16[384,256]{1,0:T(8,128)(2,1)S(1)}, u32[]{:S(2)}, u32[]{:S(2)}) collective-permute-start(bf16[384,256]{1,0:T(8,128)(2,1)S(1)} %get-tuple-element.40.mine.refs_1_), channel_id=1, source_target_pairs={{0,1},{1,0},{2,3},{3,2},{4,5},{5,4},{6,7},{7,6},{8,9},{9,8},{10,11... | collective-permute-start | bytes 589832 | tf_op jit(solution)/shard_map/ppermute | solution.py:568
  15.2 9.5 %collective-permute-start.4 = (bf16[192,256]{1,0:T(8,128)(2,1)S(1)}, bf16[192,256]{1,0:T(8,128)(2,1)S(1)}, u32[]{:S(2)}, u32[]{:S(2)}) collective-permute-start(bf16[192,256]{1,0:T(8,128)(2,1)S(1)} %get-tuple-element.45.mine), channel_id=1, source_target_pairs={{0,2},{1,3},{2,0},{3,1},{4,6},{5,7},{6,4},{7,5},{8,10},{9,11},{10,... | collective-permute-start | bytes 294920 | tf_op jit(solution)/shard_map/ppermute | solution.py:568
  20.3 1.2 %collective-permute-start.6 = (f32[4,256]{1,0:T(4,128)S(1)}, f32[4,256]{1,0:T(4,128)S(1)}, u32[]{:S(2)}, u32[]{:S(2)}) collective-permute-start(f32[4,256]{1,0:T(4,128)S(1)} %get-tuple-element.44.after), channel_id=1, source_target_pairs={{0,1},{1,0},{2,3},{3,2},{4,5},{5,4},{6,7},{7,6},{8,9},{9,8},{10,11... | collective-permute-start | bytes 12296 | tf_op jit(solution)/shard_map/ppermute | solution.py:568
  21.6 3.9 %collective-permute-start.7 = (f32[4,256]{1,0:T(4,128)S(1)}, f32[4,256]{1,0:T(4,128)S(1)}, u32[]{:S(2)}, u32[]{:S(2)}) collective-permute-start(f32[4,256]{1,0:T(4,128)S(1)} %add.24), channel_id=1, source_target_pairs={{0,7},{1,6},{2,5},{3,4},{4,3},{5,2},{6,1},{7,0},{8,15},{9,14},{10,... | collective-permute-start | bytes 12296 | tf_op jit(solution)/shard_map/ppermute | solution.py:568
  23.0 3.1 %collective-permute-start.8 = (f32[4,256]{1,0:T(4,128)S(1)}, f32[4,256]{1,0:T(4,128)S(1)}, u32[]{:S(2)}, u32[]{:S(2)}) collective-permute-start(f32[4,256]{1,0:T(4,128)S(1)} %add.24), channel_id=1, source_target_pairs={{0,5},{1,4},{2,7},{3,6},{4,1},{5,0},{6,3},{7,2},{8,13},{9,12},{10,... | collective-permute-start | bytes 12296 | tf_op jit(solution)/shard_map/ppermute | solution.py:568
  23.3 3.0 %collective-permute-start.9 = (f32[4,256]{1,0:T(4,128)S(1)}, f32[4,256]{1,0:T(4,128)S(1)}, u32[]{:S(2)}, u32[]{:S(2)}) collective-permute-start(f32[4,256]{1,0:T(4,128)S(1)} %add.24), channel_id=1, source_target_pairs={{0,3},{1,2},{2,1},{3,0},{4,7},{5,6},{6,5},{7,4},{8,11},{9,10},{10,... | collective-permute-start | bytes 12296 | tf_op jit(solution)/shard_map/ppermute | solution.py:568
  24.7 1.6 %collective-permute-start.5 = (bf16[384,256]{1,0:T(8,128)(2,1)S(1)}, bf16[384,256]{1,0:T(8,128)(2,1)S(1)}, u32[]{:S(2)}, u32[]{:S(2)}) collective-permute-start(bf16[384,256]{1,0:T(8,128)(2,1)S(1)} %shard_map.66.mine), channel_id=1, source_target_pairs={{0,1},{1,0},{2,3},{3,2},{4,5},{5,4},{6,7},{7,6},{8,9},{9,8},{10,11... | collective-permute-start | bytes 589832 | tf_op jit(solution)/shard_map/ppermute | solution.py:568
  28.4 1.2 %collective-permute-start.10 = (f32[4,256]{1,0:T(4,128)S(1)}, f32[4,256]{1,0:T(4,128)S(1)}, u32[]{:S(2)}, u32[]{:S(2)}) collective-permute-start(f32[4,256]{1,0:T(4,128)S(1)} %shard_map.68.after), channel_id=1, source_target_pairs={{0,1},{1,0},{2,3},{3,2},{4,5},{5,4},{6,7},{7,6},{8,9},{9,8},{10,11... | collective-permute-start | bytes 12296 | tf_op jit(solution)/shard_map/ppermute | solution.py:568
  29.6 4.8 %collective-permute-start.11 = (f32[4,256]{1,0:T(4,128)S(1)}, f32[4,256]{1,0:T(4,128)S(1)}, u32[]{:S(2)}, u32[]{:S(2)}) collective-permute-start(f32[4,256]{1,0:T(4,128)S(1)} %add.28.after), channel_id=1, source_target_pairs={{0,7},{1,6},{2,5},{3,4},{4,3},{5,2},{6,1},{7,0},{8,15},{9,14},{10,... | collective-permute-start | bytes 12296 | tf_op jit(solution)/shard_map/ppermute | solution.py:568
  32.0 3.0 %collective-permute-start.12 = (f32[4,256]{1,0:T(4,128)S(1)}, f32[4,256]{1,0:T(4,128)S(1)}, u32[]{:S(2)}, u32[]{:S(2)}) collective-permute-start(f32[4,256]{1,0:T(4,128)S(1)} %add.28.after), channel_id=1, source_target_pairs={{0,5},{1,4},{2,7},{3,6},{4,1},{5,0},{6,3},{7,2},{8,13},{9,12},{10,... | collective-permute-start | bytes 12296 | tf_op jit(solution)/shard_map/ppermute | solution.py:568
  32.3 3.0 %collective-permute-start.13 = (f32[4,256]{1,0:T(4,128)S(1)}, f32[4,256]{1,0:T(4,128)S(1)}, u32[]{:S(2)}, u32[]{:S(2)}) collective-permute-start(f32[4,256]{1,0:T(4,128)S(1)} %add.28.after), channel_id=1, source_target_pairs={{0,3},{1,2},{2,1},{3,0},{4,7},{5,6},{6,5},{7,4},{8,11},{9,10},{10,... | collective-permute-start | bytes 12296 | tf_op jit(solution)/shard_map/ppermute | solution.py:568
  37.8 1.4 %collective-permute-start.14 = (bf16[272,256]{1,0:T(8,128)(2,1)S(1)}, bf16[272,256]{1,0:T(8,128)(2,1)S(1)}, u32[]{:S(2)}, u32[]{:S(2)}) collective-permute-start(bf16[272,256]{1,0:T(8,128)(2,1)S(1)} %get-tuple-element.51), channel_id=1, source_target_pairs={{0,1},{1,0},{2,3},{3,2},{4,5},{5,4},{6,7},{7,6},{8,9},{9,8},{10,11... | collective-permute-start | bytes 417800 | tf_op jit(solution)/shard_map/ppermute | solution.py:568
  39.2 4.4 %collective-permute-start.15 = (bf16[80,256]{1,0:T(8,128)(2,1)S(1)}, bf16[80,256]{1,0:T(8,128)(2,1)S(1)}, u32[]{:S(2)}, u32[]{:S(2)}) collective-permute-start(bf16[80,256]{1,0:T(8,128)(2,1)S(1)} %get-tuple-element.53), channel_id=1, source_target_pairs={{0,7},{1,6},{2,5},{3,4},{4,3},{5,2},{6,1},{7,0},{8,15},{9,14},{10,... | collective-permute-start | bytes 122888 | tf_op jit(solution)/shard_map/ppermute | solution.py:568
  40.8 4.1 %collective-permute-start.16 = (bf16[80,256]{1,0:T(8,128)(2,1)S(1)}, bf16[80,256]{1,0:T(8,128)(2,1)S(1)}, u32[]{:S(2)}, u32[]{:S(2)}) collective-permute-start(bf16[80,256]{1,0:T(8,128)(2,1)S(1)} %get-tuple-element.54), channel_id=1, source_target_pairs={{0,5},{1,4},{2,7},{3,6},{4,1},{5,0},{6,3},{7,2},{8,13},{9,12},{10,... | collective-permute-start | bytes 122888 | tf_op jit(solution)/shard_map/ppermute | solution.py:568
  41.2 3.7 %collective-permute-start.17 = (bf16[80,256]{1,0:T(8,128)(2,1)S(1)}, bf16[80,256]{1,0:T(8,128)(2,1)S(1)}, u32[]{:S(2)}, u32[]{:S(2)}) collective-permute-start(bf16[80,256]{1,0:T(8,128)(2,1)S(1)} %get-tuple-element.55), channel_id=1, source_target_pairs={{0,3},{1,2},{2,1},{3,0},{4,7},{5,6},{6,5},{7,4},{8,11},{9,10},{10,... | collective-permute-start | bytes 122888 | tf_op jit(solution)/shard_map/ppermute | solution.py:568
  45.3 1.4 %collective-permute-start.18 = (bf16[32,256]{1,0:T(8,128)(2,1)S(1)}, bf16[32,256]{1,0:T(8,128)(2,1)S(1)}, u32[]{:S(2)}, u32[]{:S(2)}) collective-permute-start(bf16[32,256]{1,0:T(8,128)(2,1)S(1)} %get-tuple-element.57.refs_0_.share), channel_id=1, source_target_pairs={{0,1},{1,0},{2,3},{3,2},{4,5},{5,4},{6,7},{7,6},{8,9},{9,8},{10,11... | collective-permute-start | bytes 49160 | tf_op jit(solution)/shard_map/ppermute | solution.py:568
  46.7 5.4 %collective-permute-start.19 = (bf16[64,256]{1,0:T(8,128)(2,1)S(1)}, bf16[64,256]{1,0:T(8,128)(2,1)S(1)}, u32[]{:S(2)}, u32[]{:S(2)}) collective-permute-start(bf16[64,256]{1,0:T(8,128)(2,1)S(1)} %shard_map.75.refs_1_.share), channel_id=1, source_target_pairs={{0,7},{1,6},{2,5},{3,4},{4,3},{5,2},{6,1},{7,0},{8,15},{9,14},{10,... | collective-permute-start | bytes 98312 | tf_op jit(solution)/shard_map/ppermute | solution.py:568
  48.8 3.3 %collective-permute-start.20 = (bf16[64,256]{1,0:T(8,128)(2,1)S(1)}, bf16[64,256]{1,0:T(8,128)(2,1)S(1)}, u32[]{:S(2)}, u32[]{:S(2)}) collective-permute-start(bf16[64,256]{1,0:T(8,128)(2,1)S(1)} %shard_map.75.refs_1_.share), channel_id=1, source_target_pairs={{0,5},{1,4},{2,7},{3,6},{4,1},{5,0},{6,3},{7,2},{8,13},{9,12},{10,... | collective-permute-start | bytes 98312 | tf_op jit(solution)/shard_map/ppermute | solution.py:568
  49.2 3.3 %collective-permute-start.21 = (bf16[64,256]{1,0:T(8,128)(2,1)S(1)}, bf16[64,256]{1,0:T(8,128)(2,1)S(1)}, u32[]{:S(2)}, u32[]{:S(2)}) collective-permute-start(bf16[64,256]{1,0:T(8,128)(2,1)S(1)} %shard_map.75.refs_1_.share), channel_id=1, source_target_pairs={{0,3},{1,2},{2,1},{3,0},{4,7},{5,6},{6,5},{7,4},{8,11},{9,10},{10,... | collective-permute-start | bytes 98312 | tf_op jit(solution)/shard_map/ppermute | solution.py:568

commit v4 on v3

--- a/solution.py
+++ b/solution.py
@@ -168,19 +168,22 @@
         start += size
 
 
-def quarters_kernel(size, after, mine, moved, out):
-    side = lax.axis_index("proto") // 2 % 2
-    for i in range(mine.shape[0] // size):
-        for ref, place in ((mine, side), (moved, 1 - side)):
-            at = pl.multiple_of((2 * i + place) * size, size)
-            out[pl.ds(at, size), :] = ref[i * size : (i + 1) * size, :]
-
-
-def place_kernel(mine, other, out):
+def quarters_kernel(after, mine, moved, out):
+    size = mine.shape[0]
+    out[0:size, :] = mine[...]
+    out[size:, :] = moved[...]
+
+
+def place_kernel(size, mine, other, out):
     far = mine.shape[0]
-    core = lax.axis_index("proto") % 2
-    for ref, place in ((mine, core), (other, 1 - core)):
-        out[pl.ds(pl.multiple_of(place * far, 128), far), :] = ref[...]
+    me = lax.axis_index("proto")
+    core, side = me % 2, me // 2 % 2
+    for ref, own in ((mine, core), (other, 1 - core)):
+        for k, (half, quarter) in enumerate(((own, side), (1 - own, 1 - side))):
+            for i in range(far // (2 * size)):
+                at = pl.multiple_of(half * far + (2 * i + quarter) * size, size)
+                start = k * (far // 2) + i * size
+                out[pl.ds(at, size), :] = ref[start : start + size, :]
 
 
 def weights_kernel(wt_ref, ws_ref, wt_out, ws_out, turned_out, raw, sems):
@@ -640,7 +643,7 @@
     lane_sums = pltpu.VMEM((crops, LANES), F32)
     rounds = stages(n)
     sizes = [steps // 4, steps - steps // 4]
-    weight_sizes = [steps // 4, steps - steps // 4]
+    weight_sizes = [steps // 8, steps - steps // 8]
 
     (mine,) = call(
         halves_kernel,
@@ -700,7 +703,7 @@
         after=(own_cols, own_tot),
     )
     other = permute(mine, "proto", 1)
-    moved = permute(quarters, "proto", 2)
+    moved = permute(quarters, "proto", crossed(2))
 
     begun, cols = (), own_cols
     if keep:
@@ -731,7 +734,7 @@
         aliases={0: 0} if begun else {},
     )
     (student_mine,) = call(
-        functools.partial(quarters_kernel, half // 2),
+        quarters_kernel,
         [shape(rest // 2, width, dtype=BF)],
         [],
         0,
@@ -742,7 +745,7 @@
         after=(x,),
     )
     (zs,) = call(
-        place_kernel,
+        functools.partial(place_kernel, half // 2),
         [shape(rest, width, dtype=BF)],
         [],
         0,

time: 53.6 us -> 53.4 us (level)
  transfers between devices with their start and end apart: 22 -> 22, of which waited for: 12 -> 14; matrix products, arithmetic and copies ran while one was open for 0% -> 0% of each run, Pallas kernels for 28% -> 28%
where the time goes in v4:
time: 53.4 us; the launch traced here: 53.2 us
  Pallas kernels  21.6 us (40%)
  starting transfers between devices  21.1 us (40%)
  waiting for transfers between devices  9.44 us (18%)
  between operations  0.96 us (2%)
    ppermute x22, starting transfers between devices, permute(): return lax.ppermute(value, axis, [(i, i ^ s) for i in range(n)])  21.1 us
    pallas_call x16, Pallas kernels, call(): pl.pallas_call(kernel, out_shape=out_shape, in_specs=[hbm] * len(far) + [...  17.6 us
    ppermute x22, waiting for transfers between devices, permute(): return lax.ppermute(value, axis, [(i, i ^ s) for i in range(n)])  9.44 us
    pallas_call x2, Pallas kernels, weight_call(): pl.pallas_call(kernel, out_shape=[out_shape, shape(8, LANES)], in_specs=[...  3.3 us
  transfers between devices with their start and end apart: 22, of which 14 were waited for; matrix products, arithmetic and copies ran while one was open for 0% of the time, Pallas kernels for 28%

profile of v4, /device:TPU:0, one launch (start us, length us, event | category | flops | bytes accessed | tf_op | source)
XLA Modules:
  0.0 53.2 jit_solution(17125199260592028394)
XLA Ops:
  0.6 0.9 %shard_map.62 = bf16[192,256]{1,0:T(8,128)(2,1)S(1)} custom-call(bf16[256,256]{1,0:T(8,128)(2,1)} %teacher_ref.1, bf16[256,256]{1,0:T(8,128)(2,1)} %refs_4_.1), custom_call_target="tpu_custom_call" | custom-call | bytes 262144 | tf_op jit(solution)/shard_map/pallas_call | solution.py:612
  1.5 5.1 %collective-permute-start = (bf16[192,256]{1,0:T(8,128)(2,1)S(1)}, bf16[192,256]{1,0:T(8,128)(2,1)S(1)}, u32[]{:S(2)}, u32[]{:S(2)}) collective-permute-start(bf16[192,256]{1,0:T(8,128)(2,1)S(1)} %shard_map.62), channel_id=1, source_target_pairs={{0,24},{8,16},{16,8},{24,0},{1,25},{9,17},{17,9},{25,1},{2,26},{10... | collective-permute-start | bytes 294920 | tf_op jit(solution)/shard_map/ppermute | solution.py:571
  6.6 0.6 %collective-permute-start.2 = (bf16[192,256]{1,0:T(8,128)(2,1)S(1)}, bf16[192,256]{1,0:T(8,128)(2,1)S(1)}, u32[]{:S(2)}, u32[]{:S(2)}) collective-permute-start(bf16[192,256]{1,0:T(8,128)(2,1)S(1)} %shard_map.62), channel_id=1, source_target_pairs={{0,8},{8,0},{16,24},{24,16},{1,9},{9,1},{17,25},{25,17},{2,10},{10... | collective-permute-start | bytes 294920 | tf_op jit(solution)/shard_map/ppermute | solution.py:571
  7.3 3.3 %shard_map.59 = (bf16[8,256,512]{2,1,0:T(8,128)(2,1)S(1)}, bf16[8,256,512]{2,1,0:T(8,128)(2,1)S(1)}, bf16[8,512,256]{2,1,0:T(8,128)(2,1)S(1)}) custom-call(bf16[256,4096]{1,0:T(8,128)(2,1)} %wt_ref.1, bf16[256,4096]{1,0:T(8,128)(2,1)} %ws_ref.1), custom_call_target="tpu_custom_call" | custom-call | flops 16777216 | bytes 10485760 | tf_op jit(solution)/shard_map/pallas_call | solution.py:612
  10.7 0.8 %shard_map.60 = (bf16[8,256,512]{2,1,0:T(8,128)(2,1)S(1)}, f32[8,8,512]{2,1,0:T(8,128)S(1)}) custom-call(bf16[256,256]{1,0:T(8,128)(2,1)S(1)} %copy-done.1, bf16[8,256,512]{2,1,0:T(8,128)(2,1)S(1)} %get-tuple-element.35.wt_ref.refs_3_), custom_call_target="tpu_custom_call" | custom-call | flops 536870912 | bytes 2097152 | tf_op jit(solution)/shard_map/pallas_call | solution.py:612
  11.4 0.1 copy-done
  11.5 1.5 %shard_map.61 = (bf16[256,256]{1,0:T(8,128)(2,1)S(1)}, f32[1,256]{1,0:T(1,128)S(1)}, f32[256,256]{1,0:T(8,128)S(1)}, bf16[8,256,512]{2,1,0:T(8,128)(2,1)S(1)}) custom-call(bf16[256,256]{1,0:T(8,128)(2,1)S(1)} %copy-done, bf16[8,256,512]{2,1,0:T(8,128)(2,1)S(1)} %get-tuple-element.37.ws_ref, bf16[8,512,256]{2,1,0:T(8,128)(2,1)S(1)} %get-tuple-element.38.turned_ref.ws_rows), custom_call_target="tpu_custom_call" | custom-call | flops 1073741824 | bytes 2097152 | tf_op jit(solution)/shard_map/pallas_call | solution.py:612
  13.0 1.9 %collective-permute-done.1.refs_1_ = bf16[192,256]{1,0:T(8,128)(2,1)S(1)} collective-permute-done((bf16[192,256]{1,0:T(8,128)(2,1)S(1)}, bf16[192,256]{1,0:T(8,128)(2,1)S(1)}, u32[]{:S(2)}, u32[]{:S(2)}) %collective-permute-start.1) | collective-permute-done | bytes 98336 | tf_op jit(solution)/shard_map/ppermute | solution.py:571
  14.9 0.2 shard_map.63
  15.2 1.6 %collective-permute-start.4 = (bf16[192,256]{1,0:T(8,128)(2,1)S(1)}, bf16[192,256]{1,0:T(8,128)(2,1)S(1)}, u32[]{:S(2)}, u32[]{:S(2)}) collective-permute-start(bf16[192,256]{1,0:T(8,128)(2,1)S(1)} %get-tuple-element.45.mine), channel_id=1, source_target_pairs={{0,3},{1,2},{2,1},{3,0},{4,7},{5,6},{6,5},{7,4},{8,11},{9,10},{10,... | collective-permute-start | bytes 294920 | tf_op jit(solution)/shard_map/ppermute | solution.py:571
  16.8 1.0 %shard_map.64 = (bf16[8,768,512]{2,1,0:T(8,128)(2,1)S(1)}, f32[8,8,512]{2,1,0:T(8,128)S(1)}) custom-call(bf16[384,256]{1,0:T(8,128)(2,1)S(1)} %get-tuple-element.40.mine.refs_1_, bf16[8,256,512]{2,1,0:T(8,128)(2,1)S(1)} %get-tuple-element.35.wt_ref.refs_3_, f32[8,8,512]{2,1,0:T(8,128)S(1)} %get-tuple-element.36.after.own_cols), custom_call_target="tpu_custom_call" | custom-call | flops 805306368 | bytes 3145728 | tf_op jit(solution)/shard_map/pallas_call | solution.py:612
  17.8 2.6 %shard_map.65 = (bf16[8,768,512]{2,1,0:T(8,128)(2,1)S(1)}, f32[4,256]{1,0:T(4,128)S(1)}) custom-call(bf16[8,768,512]{2,1,0:T(8,128)(2,1)S(1)} %get-tuple-element.41.refs_0_, bf16[384,256]{1,0:T(8,128)(2,1)S(1)} %get-tuple-element.40.mine.refs_1_, bf16[384,256]{1,0:T(8,128)(2,1)S(1)} %collective-permute-done.3.refs_2_, ...), custom_call_target="tpu_custom_call", output_to_operand_aliasing={{0}: (0, {})} | custom-call | flops 2147483648 | bytes 8388608 | tf_op jit(solution)/shard_map/pallas_call | solution.py:612
  20.4 0.3 collective-permute-start.6
  20.6 1.0 %collective-permute-done.6 = f32[4,256]{1,0:T(4,128)S(1)} collective-permute-done((f32[4,256]{1,0:T(4,128)S(1)}, f32[4,256]{1,0:T(4,128)S(1)}, u32[]{:S(2)}, u32[]{:S(2)}) %collective-permute-start.6) | collective-permute-done | bytes 4128 | tf_op jit(solution)/shard_map/ppermute | solution.py:571
  21.6 1.3 %collective-permute-start.7 = (f32[4,256]{1,0:T(4,128)S(1)}, f32[4,256]{1,0:T(4,128)S(1)}, u32[]{:S(2)}, u32[]{:S(2)}) collective-permute-start(f32[4,256]{1,0:T(4,128)S(1)} %add.24), channel_id=1, source_target_pairs={{0,7},{1,6},{2,5},{3,4},{4,3},{5,2},{6,1},{7,0},{8,15},{9,14},{10,... | collective-permute-start | bytes 12296 | tf_op jit(solution)/shard_map/ppermute | solution.py:571
  22.9 0.4 collective-permute-start.8
  23.3 1.3 %collective-permute-start.9 = (f32[4,256]{1,0:T(4,128)S(1)}, f32[4,256]{1,0:T(4,128)S(1)}, u32[]{:S(2)}, u32[]{:S(2)}) collective-permute-start(f32[4,256]{1,0:T(4,128)S(1)} %add.24), channel_id=1, source_target_pairs={{0,3},{1,2},{2,1},{3,0},{4,7},{5,6},{6,5},{7,4},{8,11},{9,10},{10,... | collective-permute-start | bytes 12296 | tf_op jit(solution)/shard_map/ppermute | solution.py:571
  24.6 0.4 collective-permute-start.5
  25.0 0.5 collective-permute-done.7
  25.5 0.4 collective-permute-done.8
  26.0 0.4 collective-permute-done.9
  26.4 2.0 %shard_map.68.after = f32[4,256]{1,0:T(4,128)S(1)} custom-call(bf16[768,256]{1,0:T(8,128)(2,1)S(1)} %shard_map.67.after.zs_ref.refs_6_.refs_5_, f32[4,256]{1,0:T(4,128)S(1)} %add_add_fusion.1.x_ref, bf16[8,256,512]{2,1,0:T(8,128)(2,1)S(1)} %get-tuple-element.42.refs_4_.own_ref.refs_1_.refs_2_, bf16[8,768,512]{2,1,0:T(8,128)(2,1)S(1)} %get-tuple-element.46.e_ref.refs_2_.refs_3_), custom_call_target="tpu_custom_call" | custom-call | flops 16777216 | bytes 8388608 | tf_op jit(solution)/shard_map/pallas_call | solution.py:612
  28.4 0.3 collective-permute-start.10
  28.7 0.7 %shard_map.69 = (f32[3,256]{1,0:T(4,128)S(1)}, bf16[2,768,512]{2,1,0:T(8,128)(2,1)S(1)}) custom-call(f32[4,256]{1,0:T(4,128)S(1)} %shard_map.68.after, bf16[768,256]{1,0:T(8,128)(2,1)S(1)} %shard_map.67.after.zs_ref.refs_6_.refs_5_, bf16[8,256,512]{2,1,0:T(8,128)(2,1)S(1)} %get-tuple-element.37.ws_ref), custom_call_target="tpu_custom_call" | custom-call | flops 402653184 | bytes 1572864 | tf_op jit(solution)/shard_map/pallas_call | solution.py:612
  29.4 0.3 collective-permute-done.10
  29.7 2.2 %collective-permute-start.11 = (f32[4,256]{1,0:T(4,128)S(1)}, f32[4,256]{1,0:T(4,128)S(1)}, u32[]{:S(2)}, u32[]{:S(2)}) collective-permute-start(f32[4,256]{1,0:T(4,128)S(1)} %add.28.after), channel_id=1, source_target_pairs={{0,7},{1,6},{2,5},{3,4},{4,3},{5,2},{6,1},{7,0},{8,15},{9,14},{10,... | collective-permute-start | bytes 12296 | tf_op jit(solution)/shard_map/ppermute | solution.py:571
  31.9 0.4 collective-permute-start.12
  32.3 0.3 collective-permute-start.13
  32.7 1.7 %shard_map.70 = (f32[3,256]{1,0:T(4,128)S(1)}, bf16[6,768,512]{2,1,0:T(8,128)(2,1)S(1)}) custom-call(f32[4,256]{1,0:T(4,128)S(1)} %add.28.after, bf16[768,256]{1,0:T(8,128)(2,1)S(1)} %shard_map.67.after.zs_ref.refs_6_.refs_5_, bf16[8,256,512]{2,1,0:T(8,128)(2,1)S(1)} %get-tuple-element.37.ws_ref), custom_call_target="tpu_custom_call" | custom-call | flops 1207959552 | bytes 4718592 | tf_op jit(solution)/shard_map/pallas_call | solution.py:612
  34.4 0.5 %collective-permute-done.12 = f32[4,256]{1,0:T(4,128)S(1)} collective-permute-done((f32[4,256]{1,0:T(4,128)S(1)}, f32[4,256]{1,0:T(4,128)S(1)}, u32[]{:S(2)}, u32[]{:S(2)}) %collective-permute-start.12) | collective-permute-done | bytes 4128 | tf_op jit(solution)/shard_map/ppermute | solution.py:571
  35.0 0.4 collective-permute-done.13
  35.4 2.4 %shard_map.71 = (f32[8,1,512]{2,1,0:T(1,128)S(1)}, f32[272,256]{1,0:T(8,128)S(1)}, bf16[272,256]{1,0:T(8,128)(2,1)S(1)}) custom-call(f32[4,256]{1,0:T(4,128)S(1)} %add_add_fusion.x_ref, bf16[8,256,512]{2,1,0:T(8,128)(2,1)S(1)} %get-tuple-element.42.refs_4_.own_ref.refs_1_.refs_2_, bf16[8,768,512]{2,1,0:T(8,128)(2,1)S(1)} %get-tuple-element.46.e_ref.refs_2_.refs_3_, ...), custom_call_target="tpu_custom_call" | custom-call | flops 16777216 | bytes 8388608 | tf_op jit(solution)/shard_map/pallas_call | solution.py:612
  37.8 0.3 collective-permute-start.14
  38.1 1.2 %collective-permute-done.14.refs_1_ = bf16[272,256]{1,0:T(8,128)(2,1)S(1)} collective-permute-done((bf16[272,256]{1,0:T(8,128)(2,1)S(1)}, bf16[272,256]{1,0:T(8,128)(2,1)S(1)}, u32[]{:S(2)}, u32[]{:S(2)}) %collective-permute-start.14) | collective-permute-done | bytes 139296 | tf_op jit(solution)/shard_map/ppermute | solution.py:571
  39.3 1.5 %collective-permute-start.15 = (bf16[80,256]{1,0:T(8,128)(2,1)S(1)}, bf16[80,256]{1,0:T(8,128)(2,1)S(1)}, u32[]{:S(2)}, u32[]{:S(2)}) collective-permute-start(bf16[80,256]{1,0:T(8,128)(2,1)S(1)} %get-tuple-element.53), channel_id=1, source_target_pairs={{0,7},{1,6},{2,5},{3,4},{4,3},{5,2},{6,1},{7,0},{8,15},{9,14},{10,... | collective-permute-start | bytes 122888 | tf_op jit(solution)/shard_map/ppermute | solution.py:571
  40.8 0.3 collective-permute-start.16
  41.1 1.3 %collective-permute-start.17 = (bf16[80,256]{1,0:T(8,128)(2,1)S(1)}, bf16[80,256]{1,0:T(8,128)(2,1)S(1)}, u32[]{:S(2)}, u32[]{:S(2)}) collective-permute-start(bf16[80,256]{1,0:T(8,128)(2,1)S(1)} %get-tuple-element.55), channel_id=1, source_target_pairs={{0,3},{1,2},{2,1},{3,0},{4,7},{5,6},{6,5},{7,4},{8,11},{9,10},{10,... | collective-permute-start | bytes 122888 | tf_op jit(solution)/shard_map/ppermute | solution.py:571
  42.4 1.5 %collective-permute-done.15.refs_1_ = bf16[80,256]{1,0:T(8,128)(2,1)S(1)} collective-permute-done((bf16[80,256]{1,0:T(8,128)(2,1)S(1)}, bf16[80,256]{1,0:T(8,128)(2,1)S(1)}, u32[]{:S(2)}, u32[]{:S(2)}) %collective-permute-start.15) | collective-permute-done | bytes 40992 | tf_op jit(solution)/shard_map/ppermute | solution.py:571
  43.9 1.1 %collective-permute-done.16.refs_2_ = bf16[80,256]{1,0:T(8,128)(2,1)S(1)} collective-permute-done((bf16[80,256]{1,0:T(8,128)(2,1)S(1)}, bf16[80,256]{1,0:T(8,128)(2,1)S(1)}, u32[]{:S(2)}, u32[]{:S(2)}) %collective-permute-start.16) | collective-permute-done | bytes 40992 | tf_op jit(solution)/shard_map/ppermute | solution.py:571
  45.0 0.4 shard_map.73
  45.4 0.2 collective-permute-start.18
  45.6 1.0 %shard_map.74 = (bf16[64,4096]{1,0:T(8,128)(2,1)}, f32[8,128]{1,0:T(8,128)S(1)}) custom-call(bf16[32,256]{1,0:T(8,128)(2,1)S(1)} %get-tuple-element.57.refs_0_.share, bf16[8,256,512]{2,1,0:T(8,128)(2,1)S(1)} %get-tuple-element.42.refs_4_.own_ref.refs_1_.refs_2_, bf16[8,768,512]{2,1,0:T(8,128)(2,1)S(1)} %get-tuple-element.46.e_ref.refs_2_.refs_3_, ...), custom_call_target="tpu_custom_call" | custom-call | flops 67108864 | bytes 2097152 | tf_op jit(solution)/shard_map/pallas_call | solution.py:628
  46.6 2.2 %collective-permute-start.19 = (bf16[64,256]{1,0:T(8,128)(2,1)S(1)}, bf16[64,256]{1,0:T(8,128)(2,1)S(1)}, u32[]{:S(2)}, u32[]{:S(2)}) collective-permute-start(bf16[64,256]{1,0:T(8,128)(2,1)S(1)} %shard_map.75.refs_1_.share), channel_id=1, source_target_pairs={{0,7},{1,6},{2,5},{3,4},{4,3},{5,2},{6,1},{7,0},{8,15},{9,14},{10,... | collective-permute-start | bytes 98312 | tf_op jit(solution)/shard_map/ppermute | solution.py:571
  48.8 0.2 collective-permute-start.20
  49.0 0.8 %collective-permute-start.21 = (bf16[64,256]{1,0:T(8,128)(2,1)S(1)}, bf16[64,256]{1,0:T(8,128)(2,1)S(1)}, u32[]{:S(2)}, u32[]{:S(2)}) collective-permute-start(bf16[64,256]{1,0:T(8,128)(2,1)S(1)} %shard_map.75.refs_1_.share), channel_id=1, source_target_pairs={{0,3},{1,2},{2,1},{3,0},{4,7},{5,6},{6,5},{7,4},{8,11},{9,10},{10,... | collective-permute-start | bytes 98312 | tf_op jit(solution)/shard_map/ppermute | solution.py:571
  49.9 2.3 %shard_map.76 = (bf16[64,4096]{1,0:T(8,128)(2,1)}, f32[8,128]{1,0:T(8,128)S(1)}) custom-call(bf16[64,4096]{1,0:T(8,128)(2,1)} %get-tuple-element.64.refs_0_, bf16[64,256]{1,0:T(8,128)(2,1)S(1)} %shard_map.75.refs_1_.share, bf16[8,256,512]{2,1,0:T(8,128)(2,1)S(1)} %get-tuple-element.42.refs_4_.own_ref.refs_1_.refs_2_, ...), custom_call_target="tpu_custom_call", output_to_operand_aliasing={{0}: (0, {})} | custom-call | flops 469762048 | bytes 14680064 | tf_op jit(solution)/shard_map/pallas_call | solution.py:628
  52.2 0.1 collective-permute-done.21.refs_2_
  52.4 0.7 %shard_map.77 = bf16[256,256]{1,0:T(8,128)(2,1)} custom-call(f32[8,128]{1,0:T(8,128)S(1)} %get-tuple-element.67.after, bf16[64,256]{1,0:T(8,128)(2,1)S(1)} %shard_map.75.refs_1_.share, bf16[64,256]{1,0:T(8,128)(2,1)S(1)} %collective-permute-done.19.refs_0_, bf16[64,256]{1,0:T(8,128)(2,1)S(1)} %collective-permute-done.20.refs_1_, ...), custom_call_target="tpu_custom_call" | custom-call | tf_op jit(solution)/shard_map/pallas_call | solution.py:894
  (23 shorter events, 0.4 us)
Async XLA Ops:
  1.5 9.1 %copy-start.1 = (bf16[256,256]{1,0:T(8,128)(2,1)S(1)}, bf16[256,256]{1,0:T(8,128)(2,1)}, u32[]{:S(2)}) copy-start(bf16[256,256]{1,0:T(8,128)(2,1)} %teacher_ref.1) | copy-start | bytes 393220
  1.5 11.5 %collective-permute-start = (bf16[192,256]{1,0:T(8,128)(2,1)S(1)}, bf16[192,256]{1,0:T(8,128)(2,1)S(1)}, u32[]{:S(2)}, u32[]{:S(2)}) collective-permute-start(bf16[192,256]{1,0:T(8,128)(2,1)S(1)} %shard_map.62), channel_id=1, source_target_pairs={{0,24},{8,16},{16,8},{24,0},{1,25},{9,17},{17,9},{25,1},{2,26},{10... | collective-permute-start | bytes 294920 | tf_op jit(solution)/shard_map/ppermute | solution.py:571
  6.6 8.3 %collective-permute-start.1 = (bf16[192,256]{1,0:T(8,128)(2,1)S(1)}, bf16[192,256]{1,0:T(8,128)(2,1)S(1)}, u32[]{:S(2)}, u32[]{:S(2)}) collective-permute-start(bf16[192,256]{1,0:T(8,128)(2,1)S(1)} %shard_map.62), channel_id=1, source_target_pairs={{0,16},{8,24},{16,0},{24,8},{1,17},{9,25},{17,1},{25,9},{2,18},{10... | collective-permute-start | bytes 294920 | tf_op jit(solution)/shard_map/ppermute | solution.py:571
  6.6 8.3 %collective-permute-start.2 = (bf16[192,256]{1,0:T(8,128)(2,1)S(1)}, bf16[192,256]{1,0:T(8,128)(2,1)S(1)}, u32[]{:S(2)}, u32[]{:S(2)}) collective-permute-start(bf16[192,256]{1,0:T(8,128)(2,1)S(1)} %shard_map.62), channel_id=1, source_target_pairs={{0,8},{8,0},{16,24},{24,16},{1,9},{9,1},{17,25},{25,17},{2,10},{10... | collective-permute-start | bytes 294920 | tf_op jit(solution)/shard_map/ppermute | solution.py:571
  10.6 0.9 %copy-start = (bf16[256,256]{1,0:T(8,128)(2,1)S(1)}, bf16[256,256]{1,0:T(8,128)(2,1)}, u32[]{:S(2)}) copy-start(bf16[256,256]{1,0:T(8,128)(2,1)} %refs_4_.1) | copy-start | bytes 393220
  15.1 2.7 %collective-permute-start.3 = (bf16[384,256]{1,0:T(8,128)(2,1)S(1)}, bf16[384,256]{1,0:T(8,128)(2,1)S(1)}, u32[]{:S(2)}, u32[]{:S(2)}) collective-permute-start(bf16[384,256]{1,0:T(8,128)(2,1)S(1)} %get-tuple-element.40.mine.refs_1_), channel_id=1, source_target_pairs={{0,1},{1,0},{2,3},{3,2},{4,5},{5,4},{6,7},{7,6},{8,9},{9,8},{10,11... | collective-permute-start | bytes 589832 | tf_op jit(solution)/shard_map/ppermute | solution.py:571
  15.2 9.4 %collective-permute-start.4 = (bf16[192,256]{1,0:T(8,128)(2,1)S(1)}, bf16[192,256]{1,0:T(8,128)(2,1)S(1)}, u32[]{:S(2)}, u32[]{:S(2)}) collective-permute-start(bf16[192,256]{1,0:T(8,128)(2,1)S(1)} %get-tuple-element.45.mine), channel_id=1, source_target_pairs={{0,3},{1,2},{2,1},{3,0},{4,7},{5,6},{6,5},{7,4},{8,11},{9,10},{10,... | collective-permute-start | bytes 294920 | tf_op jit(solution)/shard_map/ppermute | solution.py:571
  20.4 1.2 %collective-permute-start.6 = (f32[4,256]{1,0:T(4,128)S(1)}, f32[4,256]{1,0:T(4,128)S(1)}, u32[]{:S(2)}, u32[]{:S(2)}) collective-permute-start(f32[4,256]{1,0:T(4,128)S(1)} %get-tuple-element.44.after), channel_id=1, source_target_pairs={{0,1},{1,0},{2,3},{3,2},{4,5},{5,4},{6,7},{7,6},{8,9},{9,8},{10,11... | collective-permute-start | bytes 12296 | tf_op jit(solution)/shard_map/ppermute | solution.py:571
  21.6 3.9 %collective-permute-start.7 = (f32[4,256]{1,0:T(4,128)S(1)}, f32[4,256]{1,0:T(4,128)S(1)}, u32[]{:S(2)}, u32[]{:S(2)}) collective-permute-start(f32[4,256]{1,0:T(4,128)S(1)} %add.24), channel_id=1, source_target_pairs={{0,7},{1,6},{2,5},{3,4},{4,3},{5,2},{6,1},{7,0},{8,15},{9,14},{10,... | collective-permute-start | bytes 12296 | tf_op jit(solution)/shard_map/ppermute | solution.py:571
  22.9 3.1 %collective-permute-start.8 = (f32[4,256]{1,0:T(4,128)S(1)}, f32[4,256]{1,0:T(4,128)S(1)}, u32[]{:S(2)}, u32[]{:S(2)}) collective-permute-start(f32[4,256]{1,0:T(4,128)S(1)} %add.24), channel_id=1, source_target_pairs={{0,5},{1,4},{2,7},{3,6},{4,1},{5,0},{6,3},{7,2},{8,13},{9,12},{10,... | collective-permute-start | bytes 12296 | tf_op jit(solution)/shard_map/ppermute | solution.py:571
  23.3 3.0 %collective-permute-start.9 = (f32[4,256]{1,0:T(4,128)S(1)}, f32[4,256]{1,0:T(4,128)S(1)}, u32[]{:S(2)}, u32[]{:S(2)}) collective-permute-start(f32[4,256]{1,0:T(4,128)S(1)} %add.24), channel_id=1, source_target_pairs={{0,3},{1,2},{2,1},{3,0},{4,7},{5,6},{6,5},{7,4},{8,11},{9,10},{10,... | collective-permute-start | bytes 12296 | tf_op jit(solution)/shard_map/ppermute | solution.py:571
  24.6 1.7 %collective-permute-start.5 = (bf16[384,256]{1,0:T(8,128)(2,1)S(1)}, bf16[384,256]{1,0:T(8,128)(2,1)S(1)}, u32[]{:S(2)}, u32[]{:S(2)}) collective-permute-start(bf16[384,256]{1,0:T(8,128)(2,1)S(1)} %shard_map.66.mine), channel_id=1, source_target_pairs={{0,1},{1,0},{2,3},{3,2},{4,5},{5,4},{6,7},{7,6},{8,9},{9,8},{10,11... | collective-permute-start | bytes 589832 | tf_op jit(solution)/shard_map/ppermute | solution.py:571
  28.4 1.2 %collective-permute-start.10 = (f32[4,256]{1,0:T(4,128)S(1)}, f32[4,256]{1,0:T(4,128)S(1)}, u32[]{:S(2)}, u32[]{:S(2)}) collective-permute-start(f32[4,256]{1,0:T(4,128)S(1)} %shard_map.68.after), channel_id=1, source_target_pairs={{0,1},{1,0},{2,3},{3,2},{4,5},{5,4},{6,7},{7,6},{8,9},{9,8},{10,11... | collective-permute-start | bytes 12296 | tf_op jit(solution)/shard_map/ppermute | solution.py:571
  29.7 4.7 %collective-permute-start.11 = (f32[4,256]{1,0:T(4,128)S(1)}, f32[4,256]{1,0:T(4,128)S(1)}, u32[]{:S(2)}, u32[]{:S(2)}) collective-permute-start(f32[4,256]{1,0:T(4,128)S(1)} %add.28.after), channel_id=1, source_target_pairs={{0,7},{1,6},{2,5},{3,4},{4,3},{5,2},{6,1},{7,0},{8,15},{9,14},{10,... | collective-permute-start | bytes 12296 | tf_op jit(solution)/shard_map/ppermute | solution.py:571
  31.9 3.0 %collective-permute-start.12 = (f32[4,256]{1,0:T(4,128)S(1)}, f32[4,256]{1,0:T(4,128)S(1)}, u32[]{:S(2)}, u32[]{:S(2)}) collective-permute-start(f32[4,256]{1,0:T(4,128)S(1)} %add.28.after), channel_id=1, source_target_pairs={{0,5},{1,4},{2,7},{3,6},{4,1},{5,0},{6,3},{7,2},{8,13},{9,12},{10,... | collective-permute-start | bytes 12296 | tf_op jit(solution)/shard_map/ppermute | solution.py:571
  32.3 3.0 %collective-permute-start.13 = (f32[4,256]{1,0:T(4,128)S(1)}, f32[4,256]{1,0:T(4,128)S(1)}, u32[]{:S(2)}, u32[]{:S(2)}) collective-permute-start(f32[4,256]{1,0:T(4,128)S(1)} %add.28.after), channel_id=1, source_target_pairs={{0,3},{1,2},{2,1},{3,0},{4,7},{5,6},{6,5},{7,4},{8,11},{9,10},{10,... | collective-permute-start | bytes 12296 | tf_op jit(solution)/shard_map/ppermute | solution.py:571
  37.8 1.4 %collective-permute-start.14 = (bf16[272,256]{1,0:T(8,128)(2,1)S(1)}, bf16[272,256]{1,0:T(8,128)(2,1)S(1)}, u32[]{:S(2)}, u32[]{:S(2)}) collective-permute-start(bf16[272,256]{1,0:T(8,128)(2,1)S(1)} %get-tuple-element.51), channel_id=1, source_target_pairs={{0,1},{1,0},{2,3},{3,2},{4,5},{5,4},{6,7},{7,6},{8,9},{9,8},{10,11... | collective-permute-start | bytes 417800 | tf_op jit(solution)/shard_map/ppermute | solution.py:571
  39.3 4.6 %collective-permute-start.15 = (bf16[80,256]{1,0:T(8,128)(2,1)S(1)}, bf16[80,256]{1,0:T(8,128)(2,1)S(1)}, u32[]{:S(2)}, u32[]{:S(2)}) collective-permute-start(bf16[80,256]{1,0:T(8,128)(2,1)S(1)} %get-tuple-element.53), channel_id=1, source_target_pairs={{0,7},{1,6},{2,5},{3,4},{4,3},{5,2},{6,1},{7,0},{8,15},{9,14},{10,... | collective-permute-start | bytes 122888 | tf_op jit(solution)/shard_map/ppermute | solution.py:571
  40.8 4.2 %collective-permute-start.16 = (bf16[80,256]{1,0:T(8,128)(2,1)S(1)}, bf16[80,256]{1,0:T(8,128)(2,1)S(1)}, u32[]{:S(2)}, u32[]{:S(2)}) collective-permute-start(bf16[80,256]{1,0:T(8,128)(2,1)S(1)} %get-tuple-element.54), channel_id=1, source_target_pairs={{0,5},{1,4},{2,7},{3,6},{4,1},{5,0},{6,3},{7,2},{8,13},{9,12},{10,... | collective-permute-start | bytes 122888 | tf_op jit(solution)/shard_map/ppermute | solution.py:571
  41.1 3.9 %collective-permute-start.17 = (bf16[80,256]{1,0:T(8,128)(2,1)S(1)}, bf16[80,256]{1,0:T(8,128)(2,1)S(1)}, u32[]{:S(2)}, u32[]{:S(2)}) collective-permute-start(bf16[80,256]{1,0:T(8,128)(2,1)S(1)} %get-tuple-element.55), channel_id=1, source_target_pairs={{0,3},{1,2},{2,1},{3,0},{4,7},{5,6},{6,5},{7,4},{8,11},{9,10},{10,... | collective-permute-start | bytes 122888 | tf_op jit(solution)/shard_map/ppermute | solution.py:571
  45.4 1.2 %collective-permute-start.18 = (bf16[32,256]{1,0:T(8,128)(2,1)S(1)}, bf16[32,256]{1,0:T(8,128)(2,1)S(1)}, u32[]{:S(2)}, u32[]{:S(2)}) collective-permute-start(bf16[32,256]{1,0:T(8,128)(2,1)S(1)} %get-tuple-element.57.refs_0_.share), channel_id=1, source_target_pairs={{0,1},{1,0},{2,3},{3,2},{4,5},{5,4},{6,7},{7,6},{8,9},{9,8},{10,11... | collective-permute-start | bytes 49160 | tf_op jit(solution)/shard_map/ppermute | solution.py:571
  46.6 5.6 %collective-permute-start.19 = (bf16[64,256]{1,0:T(8,128)(2,1)S(1)}, bf16[64,256]{1,0:T(8,128)(2,1)S(1)}, u32[]{:S(2)}, u32[]{:S(2)}) collective-permute-start(bf16[64,256]{1,0:T(8,128)(2,1)S(1)} %shard_map.75.refs_1_.share), channel_id=1, source_target_pairs={{0,7},{1,6},{2,5},{3,4},{4,3},{5,2},{6,1},{7,0},{8,15},{9,14},{10,... | collective-permute-start | bytes 98312 | tf_op jit(solution)/shard_map/ppermute | solution.py:571
  48.8 3.4 %collective-permute-start.20 = (bf16[64,256]{1,0:T(8,128)(2,1)S(1)}, bf16[64,256]{1,0:T(8,128)(2,1)S(1)}, u32[]{:S(2)}, u32[]{:S(2)}) collective-permute-start(bf16[64,256]{1,0:T(8,128)(2,1)S(1)} %shard_map.75.refs_1_.share), channel_id=1, source_target_pairs={{0,5},{1,4},{2,7},{3,6},{4,1},{5,0},{6,3},{7,2},{8,13},{9,12},{10,... | collective-permute-start | bytes 98312 | tf_op jit(solution)/shard_map/ppermute | solution.py:571
  49.0 3.3 %collective-permute-start.21 = (bf16[64,256]{1,0:T(8,128)(2,1)S(1)}, bf16[64,256]{1,0:T(8,128)(2,1)S(1)}, u32[]{:S(2)}, u32[]{:S(2)}) collective-permute-start(bf16[64,256]{1,0:T(8,128)(2,1)S(1)} %shard_map.75.refs_1_.share), channel_id=1, source_target_pairs={{0,3},{1,2},{2,1},{3,0},{4,7},{5,6},{6,5},{7,4},{8,11},{9,10},{10,... | collective-permute-start | bytes 98312 | tf_op jit(solution)/shard_map/ppermute | solution.py:571

commit v5 on v4

--- a/solution.py
+++ b/solution.py
@@ -642,7 +642,7 @@
     turned_crops = pltpu.VMEM((16, crops), BF)
     lane_sums = pltpu.VMEM((crops, LANES), F32)
     rounds = stages(n)
-    sizes = [steps // 4, steps - steps // 4]
+    sizes = [steps * 3 // 8, steps - steps * 3 // 8]
     weight_sizes = [steps // 8, steps - steps // 8]
 
     (mine,) = call(

time: 53.4 us -> 53.4 us (level)
  transfers between devices with their start and end apart: 22 -> 22, of which waited for: 14 -> 13; matrix products, arithmetic and copies ran while one was open for 0% -> 0% of each run, Pallas kernels for 28% -> 28%
where the time goes in v5:
time: 53.4 us; the launch traced here: 53.2 us
  Pallas kernels  21.5 us (40%)
  starting transfers between devices  21.5 us (40%)
  waiting for transfers between devices  9.22 us (17%)
  between operations  0.97 us (2%)
    ppermute x22, starting transfers between devices, permute(): return lax.ppermute(value, axis, [(i, i ^ s) for i in range(n)])  21.5 us
    pallas_call x16, Pallas kernels, call(): pl.pallas_call(kernel, out_shape=out_shape, in_specs=[hbm] * len(far) + [...  17.6 us
    ppermute x22, waiting for transfers between devices, permute(): return lax.ppermute(value, axis, [(i, i ^ s) for i in range(n)])  9.22 us
    pallas_call x2, Pallas kernels, weight_call(): pl.pallas_call(kernel, out_shape=[out_shape, shape(8, LANES)], in_specs=[...  3.17 us
  transfers between devices with their start and end apart: 22, of which 13 were waited for; matrix products, arithmetic and copies ran while one was open for 0% of the time, Pallas kernels for 28%

profile of v5, /device:TPU:0, one launch (start us, length us, event | category | flops | bytes accessed | tf_op | source)
XLA Modules:
  0.0 53.2 jit_solution(11619340526897831709)
XLA Ops:
  0.6 0.9 %shard_map.62 = bf16[192,256]{1,0:T(8,128)(2,1)S(1)} custom-call(bf16[256,256]{1,0:T(8,128)(2,1)} %teacher_ref.1, bf16[256,256]{1,0:T(8,128)(2,1)} %refs_4_.1), custom_call_target="tpu_custom_call" | custom-call | bytes 262144 | tf_op jit(solution)/shard_map/pallas_call | solution.py:612
  1.5 5.1 %collective-permute-start = (bf16[192,256]{1,0:T(8,128)(2,1)S(1)}, bf16[192,256]{1,0:T(8,128)(2,1)S(1)}, u32[]{:S(2)}, u32[]{:S(2)}) collective-permute-start(bf16[192,256]{1,0:T(8,128)(2,1)S(1)} %shard_map.62), channel_id=1, source_target_pairs={{0,24},{8,16},{16,8},{24,0},{1,25},{9,17},{17,9},{25,1},{2,26},{10... | collective-permute-start | bytes 294920 | tf_op jit(solution)/shard_map/ppermute | solution.py:571
  6.6 0.6 %collective-permute-start.2 = (bf16[192,256]{1,0:T(8,128)(2,1)S(1)}, bf16[192,256]{1,0:T(8,128)(2,1)S(1)}, u32[]{:S(2)}, u32[]{:S(2)}) collective-permute-start(bf16[192,256]{1,0:T(8,128)(2,1)S(1)} %shard_map.62), channel_id=1, source_target_pairs={{0,8},{8,0},{16,24},{24,16},{1,9},{9,1},{17,25},{25,17},{2,10},{10... | collective-permute-start | bytes 294920 | tf_op jit(solution)/shard_map/ppermute | solution.py:571
  7.3 3.3 %shard_map.59 = (bf16[8,256,512]{2,1,0:T(8,128)(2,1)S(1)}, bf16[8,256,512]{2,1,0:T(8,128)(2,1)S(1)}, bf16[8,512,256]{2,1,0:T(8,128)(2,1)S(1)}) custom-call(bf16[256,4096]{1,0:T(8,128)(2,1)} %wt_ref.1, bf16[256,4096]{1,0:T(8,128)(2,1)} %ws_ref.1), custom_call_target="tpu_custom_call" | custom-call | flops 16777216 | bytes 10485760 | tf_op jit(solution)/shard_map/pallas_call | solution.py:612
  10.7 0.8 %shard_map.60 = (bf16[8,256,512]{2,1,0:T(8,128)(2,1)S(1)}, f32[8,8,512]{2,1,0:T(8,128)S(1)}) custom-call(bf16[256,256]{1,0:T(8,128)(2,1)S(1)} %copy-done.1, bf16[8,256,512]{2,1,0:T(8,128)(2,1)S(1)} %get-tuple-element.35.wt_ref.refs_3_), custom_call_target="tpu_custom_call" | custom-call | flops 536870912 | bytes 2097152 | tf_op jit(solution)/shard_map/pallas_call | solution.py:612
  11.4 0.1 copy-done
  11.5 1.5 %shard_map.61 = (bf16[256,256]{1,0:T(8,128)(2,1)S(1)}, f32[1,256]{1,0:T(1,128)S(1)}, f32[256,256]{1,0:T(8,128)S(1)}, bf16[8,256,512]{2,1,0:T(8,128)(2,1)S(1)}) custom-call(bf16[256,256]{1,0:T(8,128)(2,1)S(1)} %copy-done, bf16[8,256,512]{2,1,0:T(8,128)(2,1)S(1)} %get-tuple-element.37.ws_ref, bf16[8,512,256]{2,1,0:T(8,128)(2,1)S(1)} %get-tuple-element.38.turned_ref.ws_rows), custom_call_target="tpu_custom_call" | custom-call | flops 1073741824 | bytes 2097152 | tf_op jit(solution)/shard_map/pallas_call | solution.py:612
  13.0 1.9 %collective-permute-done.1.refs_1_ = bf16[192,256]{1,0:T(8,128)(2,1)S(1)} collective-permute-done((bf16[192,256]{1,0:T(8,128)(2,1)S(1)}, bf16[192,256]{1,0:T(8,128)(2,1)S(1)}, u32[]{:S(2)}, u32[]{:S(2)}) %collective-permute-start.1) | collective-permute-done | bytes 98336 | tf_op jit(solution)/shard_map/ppermute | solution.py:571
  14.9 0.2 shard_map.63
  15.2 1.6 %collective-permute-start.4 = (bf16[192,256]{1,0:T(8,128)(2,1)S(1)}, bf16[192,256]{1,0:T(8,128)(2,1)S(1)}, u32[]{:S(2)}, u32[]{:S(2)}) collective-permute-start(bf16[192,256]{1,0:T(8,128)(2,1)S(1)} %get-tuple-element.45.mine), channel_id=1, source_target_pairs={{0,3},{1,2},{2,1},{3,0},{4,7},{5,6},{6,5},{7,4},{8,11},{9,10},{10,... | collective-permute-start | bytes 294920 | tf_op jit(solution)/shard_map/ppermute | solution.py:571
  16.8 1.0 %shard_map.64 = (bf16[8,768,512]{2,1,0:T(8,128)(2,1)S(1)}, f32[8,8,512]{2,1,0:T(8,128)S(1)}) custom-call(bf16[384,256]{1,0:T(8,128)(2,1)S(1)} %get-tuple-element.40.mine.refs_1_, bf16[8,256,512]{2,1,0:T(8,128)(2,1)S(1)} %get-tuple-element.35.wt_ref.refs_3_, f32[8,8,512]{2,1,0:T(8,128)S(1)} %get-tuple-element.36.after.own_cols), custom_call_target="tpu_custom_call" | custom-call | flops 805306368 | bytes 3145728 | tf_op jit(solution)/shard_map/pallas_call | solution.py:612
  17.8 2.6 %shard_map.65 = (bf16[8,768,512]{2,1,0:T(8,128)(2,1)S(1)}, f32[4,256]{1,0:T(4,128)S(1)}) custom-call(bf16[8,768,512]{2,1,0:T(8,128)(2,1)S(1)} %get-tuple-element.41.refs_0_, bf16[384,256]{1,0:T(8,128)(2,1)S(1)} %get-tuple-element.40.mine.refs_1_, bf16[384,256]{1,0:T(8,128)(2,1)S(1)} %collective-permute-done.3.refs_2_, ...), custom_call_target="tpu_custom_call", output_to_operand_aliasing={{0}: (0, {})} | custom-call | flops 2147483648 | bytes 8388608 | tf_op jit(solution)/shard_map/pallas_call | solution.py:612
  20.4 0.3 collective-permute-start.6
  20.6 1.0 %collective-permute-done.6 = f32[4,256]{1,0:T(4,128)S(1)} collective-permute-done((f32[4,256]{1,0:T(4,128)S(1)}, f32[4,256]{1,0:T(4,128)S(1)}, u32[]{:S(2)}, u32[]{:S(2)}) %collective-permute-start.6) | collective-permute-done | bytes 4128 | tf_op jit(solution)/shard_map/ppermute | solution.py:571
  21.6 1.3 %collective-permute-start.7 = (f32[4,256]{1,0:T(4,128)S(1)}, f32[4,256]{1,0:T(4,128)S(1)}, u32[]{:S(2)}, u32[]{:S(2)}) collective-permute-start(f32[4,256]{1,0:T(4,128)S(1)} %add.24), channel_id=1, source_target_pairs={{0,7},{1,6},{2,5},{3,4},{4,3},{5,2},{6,1},{7,0},{8,15},{9,14},{10,... | collective-permute-start | bytes 12296 | tf_op jit(solution)/shard_map/ppermute | solution.py:571
  22.9 0.4 collective-permute-start.8
  23.3 1.3 %collective-permute-start.9 = (f32[4,256]{1,0:T(4,128)S(1)}, f32[4,256]{1,0:T(4,128)S(1)}, u32[]{:S(2)}, u32[]{:S(2)}) collective-permute-start(f32[4,256]{1,0:T(4,128)S(1)} %add.24), channel_id=1, source_target_pairs={{0,3},{1,2},{2,1},{3,0},{4,7},{5,6},{6,5},{7,4},{8,11},{9,10},{10,... | collective-permute-start | bytes 12296 | tf_op jit(solution)/shard_map/ppermute | solution.py:571
  24.6 0.4 collective-permute-start.5
  25.0 0.5 collective-permute-done.7
  25.5 0.4 collective-permute-done.8
  26.0 0.4 collective-permute-done.9
  26.4 2.0 %shard_map.68.after = f32[4,256]{1,0:T(4,128)S(1)} custom-call(bf16[768,256]{1,0:T(8,128)(2,1)S(1)} %shard_map.67.after.zs_ref.refs_6_.refs_5_, f32[4,256]{1,0:T(4,128)S(1)} %add_add_fusion.1.x_ref, bf16[8,256,512]{2,1,0:T(8,128)(2,1)S(1)} %get-tuple-element.42.refs_4_.own_ref.refs_1_.refs_2_, bf16[8,768,512]{2,1,0:T(8,128)(2,1)S(1)} %get-tuple-element.46.e_ref.refs_2_.refs_3_), custom_call_target="tpu_custom_call" | custom-call | flops 16777216 | bytes 8388608 | tf_op jit(solution)/shard_map/pallas_call | solution.py:612
  28.4 0.3 collective-permute-start.10
  28.7 0.9 %shard_map.69 = (f32[3,256]{1,0:T(4,128)S(1)}, bf16[3,768,512]{2,1,0:T(8,128)(2,1)S(1)}) custom-call(f32[4,256]{1,0:T(4,128)S(1)} %shard_map.68.after, bf16[768,256]{1,0:T(8,128)(2,1)S(1)} %shard_map.67.after.zs_ref.refs_6_.refs_5_, bf16[8,256,512]{2,1,0:T(8,128)(2,1)S(1)} %get-tuple-element.37.ws_ref), custom_call_target="tpu_custom_call" | custom-call | flops 603979776 | bytes 2359296 | tf_op jit(solution)/shard_map/pallas_call | solution.py:612
  29.7 2.4 %collective-permute-start.11 = (f32[4,256]{1,0:T(4,128)S(1)}, f32[4,256]{1,0:T(4,128)S(1)}, u32[]{:S(2)}, u32[]{:S(2)}) collective-permute-start(f32[4,256]{1,0:T(4,128)S(1)} %add.28.after), channel_id=1, source_target_pairs={{0,7},{1,6},{2,5},{3,4},{4,3},{5,2},{6,1},{7,0},{8,15},{9,14},{10,... | collective-permute-start | bytes 12296 | tf_op jit(solution)/shard_map/ppermute | solution.py:571
  32.0 0.3 collective-permute-start.12
  32.3 0.5 collective-permute-start.13
  32.8 1.5 %shard_map.70 = (f32[3,256]{1,0:T(4,128)S(1)}, bf16[5,768,512]{2,1,0:T(8,128)(2,1)S(1)}) custom-call(f32[4,256]{1,0:T(4,128)S(1)} %add.28.after, bf16[768,256]{1,0:T(8,128)(2,1)S(1)} %shard_map.67.after.zs_ref.refs_6_.refs_5_, bf16[8,256,512]{2,1,0:T(8,128)(2,1)S(1)} %get-tuple-element.37.ws_ref), custom_call_target="tpu_custom_call" | custom-call | flops 1006632960 | bytes 3932160 | tf_op jit(solution)/shard_map/pallas_call | solution.py:612
  34.3 0.7 %collective-permute-done.12 = f32[4,256]{1,0:T(4,128)S(1)} collective-permute-done((f32[4,256]{1,0:T(4,128)S(1)}, f32[4,256]{1,0:T(4,128)S(1)}, u32[]{:S(2)}, u32[]{:S(2)}) %collective-permute-start.12) | collective-permute-done | bytes 4128 | tf_op jit(solution)/shard_map/ppermute | solution.py:571
  35.1 0.3 collective-permute-done.13
  35.4 2.4 %shard_map.71 = (f32[8,1,512]{2,1,0:T(1,128)S(1)}, f32[272,256]{1,0:T(8,128)S(1)}, bf16[272,256]{1,0:T(8,128)(2,1)S(1)}) custom-call(f32[4,256]{1,0:T(4,128)S(1)} %add_add_fusion.x_ref, bf16[8,256,512]{2,1,0:T(8,128)(2,1)S(1)} %get-tuple-element.42.refs_4_.own_ref.refs_1_.refs_2_, bf16[8,768,512]{2,1,0:T(8,128)(2,1)S(1)} %get-tuple-element.46.e_ref.refs_2_.refs_3_, ...), custom_call_target="tpu_custom_call" | custom-call | flops 16777216 | bytes 8388608 | tf_op jit(solution)/shard_map/pallas_call | solution.py:612
  37.8 0.4 collective-permute-start.14
  38.2 1.0 %collective-permute-done.14.refs_1_ = bf16[272,256]{1,0:T(8,128)(2,1)S(1)} collective-permute-done((bf16[272,256]{1,0:T(8,128)(2,1)S(1)}, bf16[272,256]{1,0:T(8,128)(2,1)S(1)}, u32[]{:S(2)}, u32[]{:S(2)}) %collective-permute-start.14) | collective-permute-done | bytes 139296 | tf_op jit(solution)/shard_map/ppermute | solution.py:571
  39.3 1.5 %collective-permute-start.15 = (bf16[80,256]{1,0:T(8,128)(2,1)S(1)}, bf16[80,256]{1,0:T(8,128)(2,1)S(1)}, u32[]{:S(2)}, u32[]{:S(2)}) collective-permute-start(bf16[80,256]{1,0:T(8,128)(2,1)S(1)} %get-tuple-element.53), channel_id=1, source_target_pairs={{0,7},{1,6},{2,5},{3,4},{4,3},{5,2},{6,1},{7,0},{8,15},{9,14},{10,... | collective-permute-start | bytes 122888 | tf_op jit(solution)/shard_map/ppermute | solution.py:571
  40.8 0.3 collective-permute-start.16
  41.1 1.4 %collective-permute-start.17 = (bf16[80,256]{1,0:T(8,128)(2,1)S(1)}, bf16[80,256]{1,0:T(8,128)(2,1)S(1)}, u32[]{:S(2)}, u32[]{:S(2)}) collective-permute-start(bf16[80,256]{1,0:T(8,128)(2,1)S(1)} %get-tuple-element.55), channel_id=1, source_target_pairs={{0,3},{1,2},{2,1},{3,0},{4,7},{5,6},{6,5},{7,4},{8,11},{9,10},{10,... | collective-permute-start | bytes 122888 | tf_op jit(solution)/shard_map/ppermute | solution.py:571
  42.5 1.2 %collective-permute-done.15.refs_1_ = bf16[80,256]{1,0:T(8,128)(2,1)S(1)} collective-permute-done((bf16[80,256]{1,0:T(8,128)(2,1)S(1)}, bf16[80,256]{1,0:T(8,128)(2,1)S(1)}, u32[]{:S(2)}, u32[]{:S(2)}) %collective-permute-start.15) | collective-permute-done | bytes 40992 | tf_op jit(solution)/shard_map/ppermute | solution.py:571
  43.7 1.3 %collective-permute-done.16.refs_2_ = bf16[80,256]{1,0:T(8,128)(2,1)S(1)} collective-permute-done((bf16[80,256]{1,0:T(8,128)(2,1)S(1)}, bf16[80,256]{1,0:T(8,128)(2,1)S(1)}, u32[]{:S(2)}, u32[]{:S(2)}) %collective-permute-start.16) | collective-permute-done | bytes 40992 | tf_op jit(solution)/shard_map/ppermute | solution.py:571
  45.0 0.4 shard_map.73
  45.4 0.2 collective-permute-start.18
  45.6 1.0 %shard_map.74 = (bf16[64,4096]{1,0:T(8,128)(2,1)}, f32[8,128]{1,0:T(8,128)S(1)}) custom-call(bf16[32,256]{1,0:T(8,128)(2,1)S(1)} %get-tuple-element.57.refs_0_.share, bf16[8,256,512]{2,1,0:T(8,128)(2,1)S(1)} %get-tuple-element.42.refs_4_.own_ref.refs_1_.refs_2_, bf16[8,768,512]{2,1,0:T(8,128)(2,1)S(1)} %get-tuple-element.46.e_ref.refs_2_.refs_3_, ...), custom_call_target="tpu_custom_call" | custom-call | flops 67108864 | bytes 2097152 | tf_op jit(solution)/shard_map/pallas_call | solution.py:628
  46.6 0.1 collective-permute-done.18.refs_0_
  46.7 1.9 %collective-permute-start.19 = (bf16[64,256]{1,0:T(8,128)(2,1)S(1)}, bf16[64,256]{1,0:T(8,128)(2,1)S(1)}, u32[]{:S(2)}, u32[]{:S(2)}) collective-permute-start(bf16[64,256]{1,0:T(8,128)(2,1)S(1)} %shard_map.75.refs_1_.share), channel_id=1, source_target_pairs={{0,7},{1,6},{2,5},{3,4},{4,3},{5,2},{6,1},{7,0},{8,15},{9,14},{10,... | collective-permute-start | bytes 98312 | tf_op jit(solution)/shard_map/ppermute | solution.py:571
  48.6 0.4 collective-permute-start.20
  49.1 0.9 %collective-permute-start.21 = (bf16[64,256]{1,0:T(8,128)(2,1)S(1)}, bf16[64,256]{1,0:T(8,128)(2,1)S(1)}, u32[]{:S(2)}, u32[]{:S(2)}) collective-permute-start(bf16[64,256]{1,0:T(8,128)(2,1)S(1)} %shard_map.75.refs_1_.share), channel_id=1, source_target_pairs={{0,3},{1,2},{2,1},{3,0},{4,7},{5,6},{6,5},{7,4},{8,11},{9,10},{10,... | collective-permute-start | bytes 98312 | tf_op jit(solution)/shard_map/ppermute | solution.py:571
  49.9 2.2 %shard_map.76 = (bf16[64,4096]{1,0:T(8,128)(2,1)}, f32[8,128]{1,0:T(8,128)S(1)}) custom-call(bf16[64,4096]{1,0:T(8,128)(2,1)} %get-tuple-element.64.refs_0_, bf16[64,256]{1,0:T(8,128)(2,1)S(1)} %shard_map.75.refs_1_.share, bf16[8,256,512]{2,1,0:T(8,128)(2,1)S(1)} %get-tuple-element.42.refs_4_.own_ref.refs_1_.refs_2_, ...), custom_call_target="tpu_custom_call", output_to_operand_aliasing={{0}: (0, {})} | custom-call | flops 469762048 | bytes 14680064 | tf_op jit(solution)/shard_map/pallas_call | solution.py:628
  52.1 0.3 collective-permute-done.21.refs_2_
  52.4 0.7 %shard_map.77 = bf16[256,256]{1,0:T(8,128)(2,1)} custom-call(f32[8,128]{1,0:T(8,128)S(1)} %get-tuple-element.67.after, bf16[64,256]{1,0:T(8,128)(2,1)S(1)} %shard_map.75.refs_1_.share, bf16[64,256]{1,0:T(8,128)(2,1)S(1)} %collective-permute-done.19.refs_0_, bf16[64,256]{1,0:T(8,128)(2,1)S(1)} %collective-permute-done.20.refs_1_, ...), custom_call_target="tpu_custom_call" | custom-call | tf_op jit(solution)/shard_map/pallas_call | solution.py:894
  (23 shorter events, 0.3 us)
Async XLA Ops:
  1.5 9.1 %copy-start.1 = (bf16[256,256]{1,0:T(8,128)(2,1)S(1)}, bf16[256,256]{1,0:T(8,128)(2,1)}, u32[]{:S(2)}) copy-start(bf16[256,256]{1,0:T(8,128)(2,1)} %teacher_ref.1) | copy-start | bytes 393220
  1.5 11.5 %collective-permute-start = (bf16[192,256]{1,0:T(8,128)(2,1)S(1)}, bf16[192,256]{1,0:T(8,128)(2,1)S(1)}, u32[]{:S(2)}, u32[]{:S(2)}) collective-permute-start(bf16[192,256]{1,0:T(8,128)(2,1)S(1)} %shard_map.62), channel_id=1, source_target_pairs={{0,24},{8,16},{16,8},{24,0},{1,25},{9,17},{17,9},{25,1},{2,26},{10... | collective-permute-start | bytes 294920 | tf_op jit(solution)/shard_map/ppermute | solution.py:571
  6.6 8.3 %collective-permute-start.1 = (bf16[192,256]{1,0:T(8,128)(2,1)S(1)}, bf16[192,256]{1,0:T(8,128)(2,1)S(1)}, u32[]{:S(2)}, u32[]{:S(2)}) collective-permute-start(bf16[192,256]{1,0:T(8,128)(2,1)S(1)} %shard_map.62), channel_id=1, source_target_pairs={{0,16},{8,24},{16,0},{24,8},{1,17},{9,25},{17,1},{25,9},{2,18},{10... | collective-permute-start | bytes 294920 | tf_op jit(solution)/shard_map/ppermute | solution.py:571
  6.6 8.3 %collective-permute-start.2 = (bf16[192,256]{1,0:T(8,128)(2,1)S(1)}, bf16[192,256]{1,0:T(8,128)(2,1)S(1)}, u32[]{:S(2)}, u32[]{:S(2)}) collective-permute-start(bf16[192,256]{1,0:T(8,128)(2,1)S(1)} %shard_map.62), channel_id=1, source_target_pairs={{0,8},{8,0},{16,24},{24,16},{1,9},{9,1},{17,25},{25,17},{2,10},{10... | collective-permute-start | bytes 294920 | tf_op jit(solution)/shard_map/ppermute | solution.py:571
  10.6 0.9 %copy-start = (bf16[256,256]{1,0:T(8,128)(2,1)S(1)}, bf16[256,256]{1,0:T(8,128)(2,1)}, u32[]{:S(2)}) copy-start(bf16[256,256]{1,0:T(8,128)(2,1)} %refs_4_.1) | copy-start | bytes 393220
  15.1 2.7 %collective-permute-start.3 = (bf16[384,256]{1,0:T(8,128)(2,1)S(1)}, bf16[384,256]{1,0:T(8,128)(2,1)S(1)}, u32[]{:S(2)}, u32[]{:S(2)}) collective-permute-start(bf16[384,256]{1,0:T(8,128)(2,1)S(1)} %get-tuple-element.40.mine.refs_1_), channel_id=1, source_target_pairs={{0,1},{1,0},{2,3},{3,2},{4,5},{5,4},{6,7},{7,6},{8,9},{9,8},{10,11... | collective-permute-start | bytes 589832 | tf_op jit(solution)/shard_map/ppermute | solution.py:571
  15.2 9.4 %collective-permute-start.4 = (bf16[192,256]{1,0:T(8,128)(2,1)S(1)}, bf16[192,256]{1,0:T(8,128)(2,1)S(1)}, u32[]{:S(2)}, u32[]{:S(2)}) collective-permute-start(bf16[192,256]{1,0:T(8,128)(2,1)S(1)} %get-tuple-element.45.mine), channel_id=1, source_target_pairs={{0,3},{1,2},{2,1},{3,0},{4,7},{5,6},{6,5},{7,4},{8,11},{9,10},{10,... | collective-permute-start | bytes 294920 | tf_op jit(solution)/shard_map/ppermute | solution.py:571
  20.4 1.2 %collective-permute-start.6 = (f32[4,256]{1,0:T(4,128)S(1)}, f32[4,256]{1,0:T(4,128)S(1)}, u32[]{:S(2)}, u32[]{:S(2)}) collective-permute-start(f32[4,256]{1,0:T(4,128)S(1)} %get-tuple-element.44.after), channel_id=1, source_target_pairs={{0,1},{1,0},{2,3},{3,2},{4,5},{5,4},{6,7},{7,6},{8,9},{9,8},{10,11... | collective-permute-start | bytes 12296 | tf_op jit(solution)/shard_map/ppermute | solution.py:571
  21.6 3.9 %collective-permute-start.7 = (f32[4,256]{1,0:T(4,128)S(1)}, f32[4,256]{1,0:T(4,128)S(1)}, u32[]{:S(2)}, u32[]{:S(2)}) collective-permute-start(f32[4,256]{1,0:T(4,128)S(1)} %add.24), channel_id=1, source_target_pairs={{0,7},{1,6},{2,5},{3,4},{4,3},{5,2},{6,1},{7,0},{8,15},{9,14},{10,... | collective-permute-start | bytes 12296 | tf_op jit(solution)/shard_map/ppermute | solution.py:571
  22.9 3.1 %collective-permute-start.8 = (f32[4,256]{1,0:T(4,128)S(1)}, f32[4,256]{1,0:T(4,128)S(1)}, u32[]{:S(2)}, u32[]{:S(2)}) collective-permute-start(f32[4,256]{1,0:T(4,128)S(1)} %add.24), channel_id=1, source_target_pairs={{0,5},{1,4},{2,7},{3,6},{4,1},{5,0},{6,3},{7,2},{8,13},{9,12},{10,... | collective-permute-start | bytes 12296 | tf_op jit(solution)/shard_map/ppermute | solution.py:571
  23.3 3.0 %collective-permute-start.9 = (f32[4,256]{1,0:T(4,128)S(1)}, f32[4,256]{1,0:T(4,128)S(1)}, u32[]{:S(2)}, u32[]{:S(2)}) collective-permute-start(f32[4,256]{1,0:T(4,128)S(1)} %add.24), channel_id=1, source_target_pairs={{0,3},{1,2},{2,1},{3,0},{4,7},{5,6},{6,5},{7,4},{8,11},{9,10},{10,... | collective-permute-start | bytes 12296 | tf_op jit(solution)/shard_map/ppermute | solution.py:571
  24.6 1.7 %collective-permute-start.5 = (bf16[384,256]{1,0:T(8,128)(2,1)S(1)}, bf16[384,256]{1,0:T(8,128)(2,1)S(1)}, u32[]{:S(2)}, u32[]{:S(2)}) collective-permute-start(bf16[384,256]{1,0:T(8,128)(2,1)S(1)} %shard_map.66.mine), channel_id=1, source_target_pairs={{0,1},{1,0},{2,3},{3,2},{4,5},{5,4},{6,7},{7,6},{8,9},{9,8},{10,11... | collective-permute-start | bytes 589832 | tf_op jit(solution)/shard_map/ppermute | solution.py:571
  28.4 1.2 %collective-permute-start.10 = (f32[4,256]{1,0:T(4,128)S(1)}, f32[4,256]{1,0:T(4,128)S(1)}, u32[]{:S(2)}, u32[]{:S(2)}) collective-permute-start(f32[4,256]{1,0:T(4,128)S(1)} %shard_map.68.after), channel_id=1, source_target_pairs={{0,1},{1,0},{2,3},{3,2},{4,5},{5,4},{6,7},{7,6},{8,9},{9,8},{10,11... | collective-permute-start | bytes 12296 | tf_op jit(solution)/shard_map/ppermute | solution.py:571
  29.7 4.7 %collective-permute-start.11 = (f32[4,256]{1,0:T(4,128)S(1)}, f32[4,256]{1,0:T(4,128)S(1)}, u32[]{:S(2)}, u32[]{:S(2)}) collective-permute-start(f32[4,256]{1,0:T(4,128)S(1)} %add.28.after), channel_id=1, source_target_pairs={{0,7},{1,6},{2,5},{3,4},{4,3},{5,2},{6,1},{7,0},{8,15},{9,14},{10,... | collective-permute-start | bytes 12296 | tf_op jit(solution)/shard_map/ppermute | solution.py:571
  32.0 3.0 %collective-permute-start.12 = (f32[4,256]{1,0:T(4,128)S(1)}, f32[4,256]{1,0:T(4,128)S(1)}, u32[]{:S(2)}, u32[]{:S(2)}) collective-permute-start(f32[4,256]{1,0:T(4,128)S(1)} %add.28.after), channel_id=1, source_target_pairs={{0,5},{1,4},{2,7},{3,6},{4,1},{5,0},{6,3},{7,2},{8,13},{9,12},{10,... | collective-permute-start | bytes 12296 | tf_op jit(solution)/shard_map/ppermute | solution.py:571
  32.3 3.0 %collective-permute-start.13 = (f32[4,256]{1,0:T(4,128)S(1)}, f32[4,256]{1,0:T(4,128)S(1)}, u32[]{:S(2)}, u32[]{:S(2)}) collective-permute-start(f32[4,256]{1,0:T(4,128)S(1)} %add.28.after), channel_id=1, source_target_pairs={{0,3},{1,2},{2,1},{3,0},{4,7},{5,6},{6,5},{7,4},{8,11},{9,10},{10,... | collective-permute-start | bytes 12296 | tf_op jit(solution)/shard_map/ppermute | solution.py:571
  37.8 1.4 %collective-permute-start.14 = (bf16[272,256]{1,0:T(8,128)(2,1)S(1)}, bf16[272,256]{1,0:T(8,128)(2,1)S(1)}, u32[]{:S(2)}, u32[]{:S(2)}) collective-permute-start(bf16[272,256]{1,0:T(8,128)(2,1)S(1)} %get-tuple-element.51), channel_id=1, source_target_pairs={{0,1},{1,0},{2,3},{3,2},{4,5},{5,4},{6,7},{7,6},{8,9},{9,8},{10,11... | collective-permute-start | bytes 417800 | tf_op jit(solution)/shard_map/ppermute | solution.py:571
  39.3 4.4 %collective-permute-start.15 = (bf16[80,256]{1,0:T(8,128)(2,1)S(1)}, bf16[80,256]{1,0:T(8,128)(2,1)S(1)}, u32[]{:S(2)}, u32[]{:S(2)}) collective-permute-start(bf16[80,256]{1,0:T(8,128)(2,1)S(1)} %get-tuple-element.53), channel_id=1, source_target_pairs={{0,7},{1,6},{2,5},{3,4},{4,3},{5,2},{6,1},{7,0},{8,15},{9,14},{10,... | collective-permute-start | bytes 122888 | tf_op jit(solution)/shard_map/ppermute | solution.py:571
  40.8 4.3 %collective-permute-start.16 = (bf16[80,256]{1,0:T(8,128)(2,1)S(1)}, bf16[80,256]{1,0:T(8,128)(2,1)S(1)}, u32[]{:S(2)}, u32[]{:S(2)}) collective-permute-start(bf16[80,256]{1,0:T(8,128)(2,1)S(1)} %get-tuple-element.54), channel_id=1, source_target_pairs={{0,5},{1,4},{2,7},{3,6},{4,1},{5,0},{6,3},{7,2},{8,13},{9,12},{10,... | collective-permute-start | bytes 122888 | tf_op jit(solution)/shard_map/ppermute | solution.py:571
  41.1 4.0 %collective-permute-start.17 = (bf16[80,256]{1,0:T(8,128)(2,1)S(1)}, bf16[80,256]{1,0:T(8,128)(2,1)S(1)}, u32[]{:S(2)}, u32[]{:S(2)}) collective-permute-start(bf16[80,256]{1,0:T(8,128)(2,1)S(1)} %get-tuple-element.55), channel_id=1, source_target_pairs={{0,3},{1,2},{2,1},{3,0},{4,7},{5,6},{6,5},{7,4},{8,11},{9,10},{10,... | collective-permute-start | bytes 122888 | tf_op jit(solution)/shard_map/ppermute | solution.py:571
  45.4 1.2 %collective-permute-start.18 = (bf16[32,256]{1,0:T(8,128)(2,1)S(1)}, bf16[32,256]{1,0:T(8,128)(2,1)S(1)}, u32[]{:S(2)}, u32[]{:S(2)}) collective-permute-start(bf16[32,256]{1,0:T(8,128)(2,1)S(1)} %get-tuple-element.57.refs_0_.share), channel_id=1, source_target_pairs={{0,1},{1,0},{2,3},{3,2},{4,5},{5,4},{6,7},{7,6},{8,9},{9,8},{10,11... | collective-permute-start | bytes 49160 | tf_op jit(solution)/shard_map/ppermute | solution.py:571
  46.7 5.4 %collective-permute-start.19 = (bf16[64,256]{1,0:T(8,128)(2,1)S(1)}, bf16[64,256]{1,0:T(8,128)(2,1)S(1)}, u32[]{:S(2)}, u32[]{:S(2)}) collective-permute-start(bf16[64,256]{1,0:T(8,128)(2,1)S(1)} %shard_map.75.refs_1_.share), channel_id=1, source_target_pairs={{0,7},{1,6},{2,5},{3,4},{4,3},{5,2},{6,1},{7,0},{8,15},{9,14},{10,... | collective-permute-start | bytes 98312 | tf_op jit(solution)/shard_map/ppermute | solution.py:571
  48.6 3.5 %collective-permute-start.20 = (bf16[64,256]{1,0:T(8,128)(2,1)S(1)}, bf16[64,256]{1,0:T(8,128)(2,1)S(1)}, u32[]{:S(2)}, u32[]{:S(2)}) collective-permute-start(bf16[64,256]{1,0:T(8,128)(2,1)S(1)} %shard_map.75.refs_1_.share), channel_id=1, source_target_pairs={{0,5},{1,4},{2,7},{3,6},{4,1},{5,0},{6,3},{7,2},{8,13},{9,12},{10,... | collective-permute-start | bytes 98312 | tf_op jit(solution)/shard_map/ppermute | solution.py:571
  49.1 3.3 %collective-permute-start.21 = (bf16[64,256]{1,0:T(8,128)(2,1)S(1)}, bf16[64,256]{1,0:T(8,128)(2,1)S(1)}, u32[]{:S(2)}, u32[]{:S(2)}) collective-permute-start(bf16[64,256]{1,0:T(8,128)(2,1)S(1)} %shard_map.75.refs_1_.share), channel_id=1, source_target_pairs={{0,3},{1,2},{2,1},{3,0},{4,7},{5,6},{6,5},{7,4},{8,11},{9,10},{10,... | collective-permute-start | bytes 98312 | tf_op jit(solution)/shard_map/ppermute | solution.py:571
